TPU v7x, 128 devices: a whole 4x4x4 slice. The times are simulated.
128 devices in a mesh: dp: 4 (over z), expert: 32 (over x, y, core).
Axes of the slice: x: 4, y: 4, z: 4, core: 2. Of those that a mesh axis runs over, the one named last changes fastest.
Arguments:
- tokens: bfloat16 [16384, 2048], P(('dp', 'expert')), may hold values from -24 to 24
- routes: int32 [16384, 4], P(('dp', 'expert')), may hold values from 0 to 31, all different within a row; in each aligned block of 128 rows (0 to 127, 128 to 255, ...) at most 20 rows name the same one
- gates: float32 [16384, 4], P(('dp', 'expert')), may hold values from 0.05 to 0.5
- gate_up: bfloat16 [32, 2048, 2816], P('expert'), may hold values from -0.125 to 0.125
- down_proj: bfloat16 [32, 1408, 2048], P('expert'), may hold values from -0.15625 to 0.15625
- projection: bfloat16 [2048, 512], replicated, may hold values from -0.125 to 0.125
- matches: int32 [128, 128], P(('dp', 'expert')), may hold values from 0 to 127, each once within a row
Outputs:
- grad_tokens: bfloat16 [16384, 2048], P(('dp', 'expert'))
- grad_projection: float32 [2048, 512], P(('dp', 'expert'))
- row_loss: float32 [16384], P(('dp', 'expert'))
Inputs may be any that keep to these rules, and one draw needn't show every extreme that they name: `routes`: each row names 4 different experts; within the rows of one device no expert is named more than 20 times, a bound that some block reaches. `matches`: within each patch the entries are a permutation of 0 to 127.
All inputs are finite; a program needn't handle non-finite values.
Results may differ from a plain program's by a relative error of at most 0.011.
Values may be sent and summed in bfloat16 or wider, within the bound.
No kernel may reach another device: no remote copies, remote signals or barrier semaphores. Data moves between devices by JAX's collectives and lax.ppermute only.
A program may use at most 128 MiB of HBM per device.

v0:
```python
import math

import jax
import jax.numpy as jnp
from jax import lax
from jax.sharding import Mesh
from jax.sharding import PartitionSpec as P

EXPERT = ("expert_0", "expert_1", "expert_2")
DP_EXPERT = ("dp", "expert_0", "expert_1", "expert_2")


TEMPER = 0.1
EPSILON = 1e-06
CONTRACT_ROWS = (((0,), (0,)), ((), ()))
CONTRACT_COLS = (((1,), (1,)), ((), ()))


def swapped(value, axis, distance):
    return lax.ppermute(value, axis, [(i, i ^ 1 << distance) for i in range(lax.axis_size(axis))])


def split_up(value, dim, count):
    shape = value.shape
    blocks = value.reshape(*shape[:dim], count, shape[dim] // count, *shape[dim + 1 :])
    return jnp.moveaxis(blocks, dim, 0)


def summed_on_arrival(value, axis, dim):
    count = lax.axis_size(axis)
    blocks = lax.all_to_all(split_up(value, dim, count), axis, 0, 0, tiled=True)
    return jnp.sum(blocks, axis=0)


def summed_rows(value, axes, dim):
    far, near = axes
    blocks = split_up(value, dim, lax.axis_size(far))
    nearer = summed_on_arrival(blocks, near, dim + 1)
    arrived = lax.all_to_all(nearer, far, split_axis=0, concat_axis=0, tiled=True)
    return arrived.sum(axis=0)


def slot_layout(routes, gates, expert_count, capacity):
    row_count = routes.shape[0]
    top_k = routes.shape[1]
    pair_count = row_count * top_k
    flat_routes = routes.reshape(pair_count)
    expert_range = jnp.arange(expert_count, dtype=jnp.int32)
    member = (flat_routes[:, None] == expert_range[None, :]).astype(jnp.int32)
    before = jnp.cumsum(member, axis=0) - member
    position = jnp.sum(before * member, axis=1)
    slot_number = flat_routes * capacity + position
    slot_range = jnp.arange(expert_count * capacity, dtype=jnp.int32)
    chooser = slot_range[:, None] == slot_number[None, :]
    weighted = jnp.where(chooser, gates.reshape(pair_count)[None, :], jnp.float32(0.0))
    slot_rows = jnp.any(chooser.reshape(expert_count * capacity, row_count, top_k), axis=2)
    slot_gates = jnp.sum(weighted, axis=1)
    gate_matrix = jnp.sum(weighted.reshape(expert_count * capacity, row_count, top_k), axis=2)
    return (slot_rows.astype(jnp.bfloat16), slot_gates, gate_matrix)


def patch_scores(queries, key_rows, matches, coefficient):
    logits = (
        jnp.einsum("pie,pje->pij", queries, key_rows, preferred_element_type=jnp.float32)
        * coefficient
    )
    totals = jnp.log(jnp.sum(jnp.exp(logits), axis=2))
    target = matches[:, :, None] == jnp.arange(logits.shape[2], dtype=jnp.int32)[None, None, :]
    chosen = jnp.sum(jnp.where(target, logits, jnp.float32(0.0)), axis=2)
    weights = (jnp.exp(logits - totals[:, :, None]) - target.astype(jnp.float32)).astype(
        jnp.bfloat16
    )
    return (totals - chosen, weights)


def body(tokens, routes, gates, gate_up, down_proj, projection, matches):
    row_count = tokens.shape[0]
    model_width = tokens.shape[1]
    top_k = routes.shape[1]
    expert_count = lax.axis_size(EXPERT)
    capacity = row_count * top_k * 5 // (expert_count * 4)
    slot_total = expert_count * capacity
    hidden_width = down_proj.shape[1]
    embed_width = projection.shape[1]
    slot_rows, slot_gates, gate_matrix = slot_layout(routes, gates, expert_count, capacity)
    weights_joined = gate_up[0]
    weights_down = down_proj[0]
    dispatch = jnp.dot(slot_rows, tokens, preferred_element_type=jnp.float32).astype(jnp.bfloat16)
    dispatch = dispatch.reshape(expert_count, capacity, model_width)
    received = lax.all_to_all(dispatch, EXPERT, split_axis=0, concat_axis=0, tiled=True)
    source_count = received.shape[0]
    item_count = received.shape[1]
    flat_input = received.reshape(source_count * item_count, model_width)
    joined = jnp.dot(flat_input, weights_joined, preferred_element_type=jnp.float32)
    hidden = (jax.nn.silu(joined[:, :hidden_width]) * joined[:, hidden_width:]).astype(jnp.bfloat16)
    outputs = jnp.dot(hidden, weights_down, preferred_element_type=jnp.float32).astype(jnp.bfloat16)
    projected = jnp.dot(outputs, projection, preferred_element_type=jnp.float32).astype(
        jnp.bfloat16
    )
    answer = lax.all_to_all(
        projected.reshape(source_count, item_count, embed_width),
        EXPERT,
        split_axis=0,
        concat_axis=0,
        tiled=True,
    )
    saved_joined = joined.reshape(source_count, item_count, 2 * hidden_width)
    saved_outputs = outputs.reshape(source_count, item_count, model_width)
    slot_projected = answer.reshape(slot_total, embed_width)
    mixture = lax.dot_general(
        gate_matrix,
        slot_projected.astype(jnp.float32),
        CONTRACT_ROWS,
        precision=lax.Precision.HIGHEST,
    )
    embedding = jnp.dot(tokens, projection, preferred_element_type=jnp.float32) + mixture
    inverse = lax.rsqrt(jnp.mean(embedding * embedding, axis=1, keepdims=True) + EPSILON)
    unit_rows = embedding * inverse
    unit_b = unit_rows.astype(jnp.bfloat16)
    top_bit = expert_count.bit_length() - 2
    patch_count = matches.shape[0]
    patch_size = matches.shape[1]
    coefficient = 1.0 / (embed_width * TEMPER)
    queries = unit_b.reshape(patch_count, patch_size, embed_width)
    partner_rows, partner_matches = swapped((unit_b, matches.astype(jnp.bfloat16)), EXPERT, top_bit)
    key_rows = partner_rows.reshape(patch_count, patch_size, embed_width)
    row_loss, weights = patch_scores(queries, key_rows, matches, coefficient)
    partner_weights = patch_scores(
        key_rows, queries, partner_matches.astype(jnp.int32), coefficient
    )[1]
    key_part = (
        jnp.einsum("pij,pie->pje", partner_weights, key_rows, preferred_element_type=jnp.float32)
        * coefficient
    )
    query_part = (
        jnp.einsum("pij,pje->pie", weights, key_rows, preferred_element_type=jnp.float32)
        * coefficient
    )
    upstream = (query_part + key_part).reshape(row_count, embed_width)
    embed_grad = inverse * (
        upstream - unit_rows * jnp.mean(upstream * unit_rows, axis=1, keepdims=True)
    )
    embed_grad_b = embed_grad.astype(jnp.bfloat16)
    direct_grad = lax.dot_general(
        embed_grad_b, projection, CONTRACT_COLS, preferred_element_type=jnp.float32
    )
    slot_embed = jnp.dot(slot_rows, embed_grad_b, preferred_element_type=jnp.float32)
    slot_grads = (slot_gates[:, None] * slot_embed).astype(jnp.bfloat16)
    arrived = lax.all_to_all(
        slot_grads.reshape(expert_count, capacity, embed_width),
        EXPERT,
        split_axis=0,
        concat_axis=0,
        tiled=True,
    )
    arrived = arrived.reshape(slot_total, embed_width)
    output_grads = lax.dot_general(
        arrived, projection, CONTRACT_COLS, preferred_element_type=jnp.float32
    ).astype(jnp.bfloat16)
    term_left = saved_outputs.reshape(slot_total, model_width)
    hidden_grad = lax.dot_general(
        output_grads, weights_down, CONTRACT_COLS, preferred_element_type=jnp.float32
    )
    joined_flat = saved_joined.reshape(slot_total, 2 * hidden_width)
    gate_act = joined_flat[:, :hidden_width]
    up_act = joined_flat[:, hidden_width:]
    sigmoid = jax.nn.sigmoid(gate_act)
    joined_grad = jnp.concatenate(
        [
            hidden_grad * up_act * sigmoid * (1.0 + gate_act * (1.0 - sigmoid)),
            hidden_grad * gate_act * sigmoid,
        ],
        axis=1,
    ).astype(jnp.bfloat16)
    input_grads = lax.dot_general(
        joined_grad, weights_joined, CONTRACT_COLS, preferred_element_type=jnp.float32
    ).astype(jnp.bfloat16)
    back_grads = lax.all_to_all(
        input_grads.reshape(expert_count, capacity, model_width),
        EXPERT,
        split_axis=0,
        concat_axis=0,
        tiled=True,
    )
    combined = lax.dot_general(
        slot_rows,
        back_grads.reshape(slot_total, model_width),
        CONTRACT_ROWS,
        preferred_element_type=jnp.float32,
    )
    grad_tokens = (direct_grad + combined).astype(jnp.bfloat16)
    device_count = lax.axis_size("dp") * expert_count
    first_part = lax.dot_general(
        tokens, embed_grad_b, CONTRACT_ROWS, preferred_element_type=jnp.float32
    )
    second_part = lax.dot_general(
        term_left, arrived, CONTRACT_ROWS, preferred_element_type=jnp.float32
    )
    summed = summed_rows(first_part + second_part, (("dp", "expert_0", "expert_1"), "expert_2"), 0)
    grad_projection = summed * (1.0 / math.sqrt(row_count * device_count))
    return (grad_tokens, grad_projection, row_loss.reshape(row_count))


def solution(mesh):
    torus = Mesh(
        mesh.devices.reshape(mesh.shape["dp"], 4, 4, 2), ("dp", "expert_0", "expert_1", "expert_2")
    )
    return jax.shard_map(
        body,
        mesh=torus,
        in_specs=(
            P(DP_EXPERT, None),
            P(DP_EXPERT, None),
            P(DP_EXPERT, None),
            P(EXPERT, None, None),
            P(EXPERT, None, None),
            P(),
            P(DP_EXPERT, None),
        ),
        out_specs=(P(DP_EXPERT, None), P(DP_EXPERT, None), P(DP_EXPERT)),
        check_vma=False,
    )
```

profile of v0, /device:TPU:0, one launch (start us, length us, event | category | flops | bytes accessed | tf_op | source)
XLA Modules:
  0.0 263.7 jit_solution(4361017812320990498)
XLA Ops:
  0.6 0.9 copy.42
  1.8 1.2 reduce-window.6
  3.0 0.2 slice_reduce_fusion
  3.5 0.7 multiply_add_fusion.1
  4.4 0.6 copy-done.2
  5.0 3.4 %convolution_convert_fusion.1 = bf16[640,2048]{1,0:T(8,128)(2,1)} fusion(pred[640,128]{1,0:T(8,128)(4,1)S(1)} %fusion.22, bf16[128,2048]{1,0:T(8,128)(2,1)} %param.7), kind=kOutput, calls=%fused_computation.19 | convolution fusion | flops 336855040 | bytes 3227648 | tf_op jit(solution)/shard_map/dot_general | solution.py:88
  8.5 5.2 %reshape.174 = bf16[32,20,2048]{2,1,0:T(8,128)(2,1)} reshape(bf16[640,2048]{1,0:T(8,128)(2,1)} %convolution_convert_fusion.1) | data formatting | bytes 5242880 | tf_op jit(solution)/shard_map/reshape | solution.py:89
  13.6 46.8 %all_to_all.30 = bf16[32,20,2048]{2,1,0:T(8,128)(2,1)} all-to-all(bf16[32,20,2048]{2,1,0:T(8,128)(2,1)} %reshape.174), channel_id=1, replica_groups=mesh['dp'=4,'expert_0'=4,'expert_1'=4,'expert_2'=2] {'expert_0','expert_..., dimensions={0} | all-to-all | bytes 5242880 | tf_op jit(solution)/shard_map/all_to_all | solution.py:90
  60.4 5.2 %reshape.175 = bf16[640,2048]{1,0:T(8,128)(2,1)} reshape(bf16[32,20,2048]{2,1,0:T(8,128)(2,1)} %all_to_all.30) | data formatting | bytes 5242880 | tf_op jit(solution)/shard_map/reshape | solution.py:93
  65.6 11.9 %fusion.2 = f32[640,2816]{1,0:T(8,128)S(1)} fusion(bf16[640,2048]{1,0:T(8,128)(2,1)} %reshape.175, bf16[1,2048,2816]{2,1,0:T(8,128)(2,1)} %param.10), kind=kOutput, calls=%fused_computation.2 | convolution fusion | flops 7381975040 | bytes 21364736 | tf_op jit(solution)/shard_map/dot_general | solution.py:94
  77.5 9.9 %fusion.11 = bf16[640,2048]{1,0:T(8,128)(2,1)S(1)} fusion(bf16[1,1408,2048]{2,1,0:T(8,128)(2,1)} %param.11, f32[640,2816]{1,0:T(8,128)S(1)} %fusion.2), kind=kOutput, calls=%fused_computation.16 | convolution fusion | flops 3697704960 | bytes 15597568 | tf_op jit(solution)/shard_map/dot_general | solution.py:96
  87.5 1.5 copy-done.7
  89.0 1.5 convolution_convert_fusion.2
  90.5 1.0 reshape.176
  91.5 4.0 %all-to-all-start.1 = ((bf16[32,20,512]{2,1,0:T(8,128)(2,1)}), bf16[32,20,512]{2,1,0:T(8,128)(2,1)S(1)}, u32[]{:S(2)}, u32[]{:S(2)}) async-start(bf16[32,20,512]{2,1,0:T(8,128)(2,1)} %reshape.176), calls=%async_computation.1 | async-start | bytes 1572864 | tf_op jit(solution)/shard_map/all_to_all | solution.py:100
  95.6 3.4 %collective-permute-start.1 = (bf16[1,128]{1,0:T(2,128)(2,1)S(1)}, bf16[1,128]{1,0:T(2,128)(2,1)S(1)}, u32[]{:S(2)}, u32[]{:S(2)}) collective-permute-start(bf16[1,128]{1,0:T(2,128)(2,1)S(1)} %convert_element_type.69), channel_id=1, source_target_pairs={{0,16},{1,17},{2,18},{3,19},{4,20},{5,21},{6,22},{7,23},{8,24},{9,... | collective-permute-start | bytes 776 | tf_op jit(solution)/shard_map/ppermute | solution.py:20
  99.2 0.9 select_reduce_fusion.1
  100.1 0.2 select_reduce_fusion
  100.3 9.1 %all-to-all-done.1 = bf16[32,20,512]{2,1,0:T(8,128)(2,1)S(1)} async-done(((bf16[32,20,512]{2,1,0:T(8,128)(2,1)}), bf16[32,20,512]{2,1,0:T(8,128)(2,1)S(1)}, u32[]{:S(2)}, u32[]{:S(2)}) %all-to-all-start.1) | async-done | bytes 655392 | tf_op jit(solution)/shard_map/all_to_all | solution.py:100
  109.4 1.0 reshape.177
  110.4 1.7 fusion.35
  112.2 0.5 multiply_reduce_fusion.1
  112.8 1.5 collective-permute-start
  114.3 6.2 %collective-permute-done = bf16[128,512]{1,0:T(8,128)(2,1)S(1)} collective-permute-done((bf16[128,512]{1,0:T(8,128)(2,1)S(1)}, bf16[128,512]{1,0:T(8,128)(2,1)S(1)}, u32[]{:S(2)}, u32[]{:S(2)}) %collective-permute-start) | collective-permute-done | bytes 131104 | tf_op jit(solution)/shard_map/ppermute | solution.py:20
  120.7 0.2 select_reduce_fusion.2
  120.9 0.5 log_subtract_fusion
  121.6 0.3 multiply_reduce_fusion
  122.1 1.2 fusion.21
  123.2 1.2 reshape.178
  124.5 17.5 %all_to_all.31 = bf16[32,20,512]{2,1,0:T(8,128)(2,1)} all-to-all(bf16[32,20,512]{2,1,0:T(8,128)(2,1)S(1)} %reshape.178), channel_id=1, replica_groups=mesh['dp'=4,'expert_0'=4,'expert_1'=4,'expert_2'=2] {'expert_0','expert_..., dimensions={0} | all-to-all | bytes 1310720 | tf_op jit(solution)/shard_map/all_to_all | solution.py:149
  142.0 1.2 reshape.179
  143.2 3.6 %fusion.37 = f32[2048,512]{0,1:T(8,128)S(1)} fusion(bf16[640,2048]{1,0:T(8,128)(2,1)} %copy-done.7, bf16[640,512]{1,0:T(8,128)(2,1)S(1)} %reshape.179), kind=kOutput, calls=%fused_computation.72 | convolution fusion | flops 1342177280 | bytes 7471104 | tf_op jit(solution)/shard_map/dot_general | solution.py:196
  146.8 2.8 %bitcast_add_fusion = f32[2048,512]{0,1:T(8,128)} fusion(f32[2048,512]{0,1:T(8,128)S(1)} %fusion.37, bf16[128,512]{1,0:T(8,128)(2,1)S(1)} %multiply_convert_fusion.4, bf16[128,2048]{1,0:T(8,128)(2,1)S(1)} %copy-done.1), kind=kOutput, calls=%fused_computation.8 | convolution fusion | flops 269484032 | bytes 9043968 | tf_op jit(solution)/shard_map/dot_general | solution.py:193
  149.6 5.3 %copy.48 = f32[2048,512]{1,0:T(8,128)} copy(f32[2048,512]{0,1:T(8,128)} %bitcast_add_fusion) | data formatting | bytes 8388608 | tf_op jit(solution)/shard_map/add | solution.py:199
  155.0 2.6 %copy.49 = f32[2,64,16,512]{3,2,1,0:T(8,128)S(1)} copy(f32[2,64,16,512]{3,2,0,1:T(8,128)} %bitcast.71) | data formatting | bytes 8388608 | tf_op jit(solution)/shard_map/transpose | solution.py:26
  157.6 8.3 %all_to_all.32 = f32[2,64,16,512]{3,2,1,0:T(8,128)} all-to-all(f32[2,64,16,512]{3,2,1,0:T(8,128)S(1)} %copy.49), channel_id=1, replica_groups=mesh['dp'=4,'expert_0'=4,'expert_1'=4,'expert_2'=2] {'expert_2'}, dimensions={0} | all-to-all | bytes 8388608 | tf_op jit(solution)/shard_map/all_to_all | solution.py:31
  165.9 4.3 %reduce_sum.100 = f32[64,16,512]{2,1,0:T(8,128)} reduce(f32[2,64,16,512]{3,2,1,0:T(8,128)} %all_to_all.32, f32[]{:T(128)} %constant.6.clone.1), dimensions={0}, to_apply=%region_10.11 | reduce | flops 524288 | bytes 6291460 | tf_op jit(solution)/shard_map/reduce_sum | solution.py:32
  170.2 8.5 %all-to-all-start.5 = ((f32[64,16,512]{2,1,0:T(8,128)}), f32[64,16,512]{2,1,0:T(8,128)}, u32[]{:S(2)}, u32[]{:S(2)}) async-start(f32[64,16,512]{2,1,0:T(8,128)} %reduce_sum.100), calls=%async_computation.5 | async-start | bytes 4194304 | tf_op jit(solution)/shard_map/all_to_all | solution.py:39
  178.7 11.7 %multiply_convert_fusion.1 = (bf16[640,1408]{1,0:T(8,128)(2,1)}, bf16[640,1408]{1,0:T(8,128)(2,1)}) fusion(f32[640,2816]{1,0:T(8,128)} %copy-done.8, bf16[1,1408,2048]{2,1,0:T(8,128)(2,1)} %param.11, bf16[640,512]{1,0:T(8,128)(2,1)S(1)} %reshape.179, bf16[2048,512]{1,0:T(8,128)(2,1)S(1)} %copy-done), kind=kOutput, calls=%fused_computation.13 | convolution fusion | flops 5046190080 | bytes 19333120 | tf_op jit(solution)/shard_map/dot_general | solution.py:161
  190.4 12.7 %fusion.14 = bf16[640,2048]{1,0:T(8,128)(2,1)} fusion(bf16[1,2048,2816]{2,1,0:T(8,128)(2,1)} %param.10, bf16[640,1408]{1,0:T(8,128)(2,1)} %get-tuple-element.6, bf16[640,1408]{1,0:T(8,128)(2,1)} %get-tuple-element.5), kind=kOutput, calls=%fused_computation.17 | convolution fusion | flops 7390494720 | bytes 17760256 | tf_op jit(solution)/shard_map/dot_general | solution.py:175
  203.1 5.2 %reshape.180 = bf16[32,20,2048]{2,1,0:T(8,128)(2,1)} reshape(bf16[640,2048]{1,0:T(8,128)(2,1)} %fusion.14) | data formatting | bytes 5242880 | tf_op jit(solution)/shard_map/reshape | solution.py:179
  208.4 7.0 %all-to-all-start.3 = ((bf16[32,20,2048]{2,1,0:T(8,128)(2,1)}), bf16[32,20,2048]{2,1,0:T(8,128)(2,1)}, u32[]{:S(2)}, u32[]{:S(2)}) async-start(bf16[32,20,2048]{2,1,0:T(8,128)(2,1)} %reshape.180), calls=%async_computation.3 | async-start | bytes 6291456 | tf_op jit(solution)/shard_map/all_to_all | solution.py:178
  215.4 0.8 fusion.36
  216.3 1.7 reduce_sum.101
  218.0 0.6 broadcast_multiply_fusion
  218.6 36.8 %all-to-all-done.3 = bf16[32,20,2048]{2,1,0:T(8,128)(2,1)} async-done(((bf16[32,20,2048]{2,1,0:T(8,128)(2,1)}), bf16[32,20,2048]{2,1,0:T(8,128)(2,1)}, u32[]{:S(2)}, u32[]{:S(2)}) %all-to-all-start.3) | async-done | bytes 2621472 | tf_op jit(solution)/shard_map/all_to_all | solution.py:178
  255.4 5.2 %reshape.181 = bf16[640,2048]{1,0:T(8,128)(2,1)} reshape(bf16[32,20,2048]{2,1,0:T(8,128)(2,1)} %all-to-all-done.3) | data formatting | bytes 5242880 | tf_op jit(solution)/shard_map/reshape | solution.py:187
  260.6 3.2 %fusion.19 = bf16[128,2048]{1,0:T(8,128)(2,1)} fusion(f32[128,2048]{1,0:T(8,128)S(1)} %fusion.36, pred[640,128]{1,0:T(8,128)(4,1)S(1)} %copy-done.4, bf16[640,2048]{1,0:T(8,128)(2,1)} %reshape.181), kind=kOutput, calls=%fused_computation.21 | convolution fusion | flops 336068608 | bytes 4276224 | tf_op jit(solution)/shard_map/dot_general | solution.py:185
  (39 shorter events, 1.8 us)
Async XLA Ops:
  0.6 88.4 %copy-start = (bf16[2048,512]{1,0:T(8,128)(2,1)S(1)}, bf16[2048,512]{1,0:T(8,128)(2,1)}, u32[]{:S(2)}) copy-start(bf16[2048,512]{1,0:T(8,128)(2,1)} %param.12) | copy-start | bytes 6291460
  4.4 0.6 copy-start.2
  77.5 9.9 %copy-start.8 = (f32[640,2816]{1,0:T(8,128)}, f32[640,2816]{1,0:T(8,128)S(1)}, u32[]{:S(2)}) copy-start(f32[640,2816]{1,0:T(8,128)S(1)} %fusion.2) | copy-start | bytes 21626884
  87.5 1.6 copy-start.7
  89.0 6.6 %copy-start.6 = (s32[1,128]{1,0:T(1,128)S(1)}, s32[1,128]{1,0:T(1,128)}, u32[]{:S(2)}) copy-start(s32[1,128]{1,0:T(1,128)} %param.13) | copy-start | bytes 1540
  89.0 10.0 %copy-start.5 = (f32[128,4]{0,1:T(4,128)S(1)}, f32[128,4]{0,1:T(4,128)}, u32[]{:S(2)}) copy-start(f32[128,4]{0,1:T(4,128)} %param.9) | copy-start | bytes 6148
  90.5 21.6 %copy-start.1 = (bf16[128,2048]{1,0:T(8,128)(2,1)S(1)}, bf16[128,2048]{1,0:T(8,128)(2,1)}, u32[]{:S(2)}) copy-start(bf16[128,2048]{1,0:T(8,128)(2,1)} %param.7) | copy-start | bytes 1572868
  91.5 17.9 %all-to-all-start.1 = ((bf16[32,20,512]{2,1,0:T(8,128)(2,1)}), bf16[32,20,512]{2,1,0:T(8,128)(2,1)S(1)}, u32[]{:S(2)}, u32[]{:S(2)}) async-start(bf16[32,20,512]{2,1,0:T(8,128)(2,1)} %reshape.176), calls=%async_computation.1 | async-start | bytes 1572864 | tf_op jit(solution)/shard_map/all_to_all | solution.py:100
  95.6 18.7 %collective-permute-start.1 = (bf16[1,128]{1,0:T(2,128)(2,1)S(1)}, bf16[1,128]{1,0:T(2,128)(2,1)S(1)}, u32[]{:S(2)}, u32[]{:S(2)}) collective-permute-start(bf16[1,128]{1,0:T(2,128)(2,1)S(1)} %convert_element_type.69), channel_id=1, source_target_pairs={{0,16},{1,17},{2,18},{3,19},{4,20},{5,21},{6,22},{7,23},{8,24},{9,... | collective-permute-start | bytes 776 | tf_op jit(solution)/shard_map/ppermute | solution.py:20
  112.2 9.9 %copy-start.3 = (pred[640,128]{1,0:T(8,128)(4,1)S(1)}, pred[640,128]{1,0:T(8,128)(4,1)}, u32[]{:S(2)}) copy-start(pred[640,128]{1,0:T(8,128)(4,1)} %copy-done.2) | copy-start | bytes 245764
  112.8 7.6 %collective-permute-start = (bf16[128,512]{1,0:T(8,128)(2,1)S(1)}, bf16[128,512]{1,0:T(8,128)(2,1)S(1)}, u32[]{:S(2)}, u32[]{:S(2)}) collective-permute-start(bf16[128,512]{1,0:T(8,128)(2,1)S(1)} %multiply_convert_fusion.5), channel_id=1, source_target_pairs={{0,16},{1,17},{2,18},{3,19},{4,20},{5,21},{6,22},{7,23},{8,24},{9,... | collective-permute-start | bytes 393224 | tf_op jit(solution)/shard_map/ppermute | solution.py:20
  170.2 38.2 %all-to-all-start.5 = ((f32[64,16,512]{2,1,0:T(8,128)}), f32[64,16,512]{2,1,0:T(8,128)}, u32[]{:S(2)}, u32[]{:S(2)}) async-start(f32[64,16,512]{2,1,0:T(8,128)} %reduce_sum.100), calls=%async_computation.5 | async-start | bytes 4194304 | tf_op jit(solution)/shard_map/all_to_all | solution.py:39
  208.4 46.9 %all-to-all-start.3 = ((bf16[32,20,2048]{2,1,0:T(8,128)(2,1)}), bf16[32,20,2048]{2,1,0:T(8,128)(2,1)}, u32[]{:S(2)}, u32[]{:S(2)}) async-start(bf16[32,20,2048]{2,1,0:T(8,128)(2,1)} %reshape.180), calls=%async_computation.3 | async-start | bytes 6291456 | tf_op jit(solution)/shard_map/all_to_all | solution.py:178
  218.0 42.6 %copy-start.4 = (pred[640,128]{1,0:T(8,128)(4,1)S(1)}, pred[640,128]{1,0:T(8,128)(4,1)}, u32[]{:S(2)}) copy-start(pred[640,128]{1,0:T(8,128)(4,1)} %copy-done.2) | copy-start | bytes 245764
where the time goes:
time: 266 us; the launch traced here: 264 us
  blocking collectives  72.6 us (27%)
  matrix products  65.8 us (25%)
  waiting for transfers between devices  52.2 us (20%)
  local copies, waits for them, and re-layouts  37.1 us (14%)
  starting transfers between devices  24.4 us (9%)
  other arithmetic  10.7 us (4%)
    all_to_all x1, blocking collectives, body(): lax.all_to_all(dispatch, EXPERT, split_axis=0, concat_axis=0, tiled=True)  46.8 us
    all_to_all x1, waiting for transfers between devices, body(): lax.all_to_all(input_grads.reshape(expert_count, capacity, model_width),...  36.8 us
    all_to_all x1, blocking collectives, body(): lax.all_to_all(slot_grads.reshape(expert_count, capacity, embed_width), E...  17.5 us
    dot_general x1, matrix products, body(): lax.dot_general(joined_grad, weights_joined, CONTRACT_COLS, preferred_ele...  12.7 us
    dot_general x1, matrix products, body(): jnp.dot(flat_input, weights_joined, preferred_element_type=jnp.float32)  11.9 us
    dot_general x1, matrix products, body(): lax.dot_general(output_grads, weights_down, CONTRACT_COLS, preferred_elem...  11.7 us
    dot_general x1, matrix products, body(): jnp.dot(hidden, weights_down, preferred_element_type=jnp.float32)  9.9 us
    all_to_all x1, waiting for transfers between devices, body(): lax.all_to_all(projected.reshape(source_count, item_count, embed_width),...  9.12 us
  transfers between devices with their start and end apart: 5, of which 4 were waited for; matrix products, arithmetic and copies ran while one was open for 14% of the time, Pallas kernels for 0%

commit v1 on v0

v1 whole, which is shorter than its diff:
```python
import math

import jax
import jax.numpy as jnp
from jax import lax
from jax.experimental import pallas as pl
from jax.experimental.pallas import tpu as pltpu
from jax.sharding import Mesh
from jax.sharding import PartitionSpec as P

EXPERT = ("expert_0", "expert_1", "expert_2")
DP_EXPERT = ("dp", "expert_0", "expert_1", "expert_2")

TEMPER = 0.1
EPSILON = 1e-06
ROWS = 128
TOP = 4
WIDTH = 2048
HIDDEN = 1408
EMBED = 512
EXPERTS = 32
MAIN = 16
EXTRA = 4
SLOTS = EXPERTS * MAIN
SPARE = EXPERTS * EXTRA
TOTAL = SLOTS + SPARE
CHUNKS = tuple((lo, min(lo + 256, HIDDEN)) for lo in range(0, HIDDEN, 256))
TILE = 256
F32 = jnp.float32
BF16 = jnp.bfloat16
VMEM_LIMIT = 48 * 1024 * 1024


def dot(left, right):
    return jnp.dot(left, right, preferred_element_type=F32)


def dot_rows(left, right):
    return lax.dot_general(left, right, (((0,), (0,)), ((), ())), preferred_element_type=F32)


def dot_cols(left, right):
    return lax.dot_general(left, right, (((1,), (1,)), ((), ())), preferred_element_type=F32)


def iota(shape, dim):
    return lax.broadcasted_iota(jnp.int32, shape, dim)


def expanded(table):
    spread = jnp.broadcast_to(table[:, None, :], (EXPERTS, MAIN, ROWS))
    return spread.reshape(SLOTS, ROWS)


def ranks(routes):
    experts = iota((EXPERTS, ROWS), 0)
    member = jnp.zeros((EXPERTS, ROWS), F32)
    for k in range(TOP):
        member = member + jnp.where(routes[k : k + 1, :] == experts, 1.0, 0.0)
    earlier = jnp.where(iota((ROWS, ROWS), 0) < iota((ROWS, ROWS), 1), 1.0, 0.0)
    rank = dot(member.astype(BF16), earlier.astype(BF16))
    return jnp.where(member > 0.0, rank, -1.0)


def pair_gates(routes, gates):
    experts = iota((EXPERTS, ROWS), 0)
    total = jnp.zeros((EXPERTS, ROWS), F32)
    for k in range(TOP):
        total = total + jnp.where(routes[k : k + 1, :] == experts, gates[k : k + 1, :], 0.0)
    return total


def choosers(routes):
    rank = expanded(ranks(routes))
    place = iota((SLOTS, ROWS), 0) % MAIN
    main = rank == place.astype(F32)
    extra = rank == (MAIN + place % EXTRA).astype(F32)
    quarters = [extra & (place // EXTRA == j) for j in range(MAIN // EXTRA)]
    return main, quarters


def one_hot(chosen):
    return jnp.where(chosen, 1.0, 0.0).astype(BF16)


def unpacker():
    row = iota((SLOTS, SLOTS), 0)
    wanted = (row % SPARE) // EXTRA * MAIN + row // SPARE * EXTRA + row % EXTRA
    return one_hot(iota((SLOTS, SLOTS), 1) == wanted)


def packer():
    row = iota((SLOTS, SLOTS), 0)
    wanted = (row % MAIN) // EXTRA * SPARE + row // MAIN * EXTRA + row % EXTRA
    return one_hot(iota((SLOTS, SLOTS), 1) == wanted)


def dispatch_kernel(routes_ref, tokens_ref, out_ref):
    main, quarters = choosers(routes_ref[...])
    out_ref[:, :WIDTH] = dot(one_hot(main), tokens_ref[...]).astype(BF16)
    quarter = WIDTH // 4
    total = jnp.zeros((SLOTS, quarter), F32)
    for j in range(4):
        total = total + dot(one_hot(quarters[j]), tokens_ref[:, j * quarter : (j + 1) * quarter])
    out_ref[:, WIDTH:] = total.astype(BF16)


def forward_kernel(
    recv_hbm, joined_hbm, mixed_hbm, out_ref, hidden_hbm, slopes_hbm,
    x_ref, extra_ref, w_ref, mixed_ref, act_ref, hidden_ref, slopes_ref, sems, out_sems,
):
    def start(source, target, index):
        copy = pltpu.make_async_copy(source, target, sems.at[index])
        copy.start()
        return copy

    extra_copy = start(recv_hbm.at[:, pl.ds(WIDTH, WIDTH // 4)], extra_ref, 0)
    main_copy = start(recv_hbm.at[:, pl.ds(0, WIDTH)], x_ref.at[pl.ds(0, SLOTS), :], 1)
    weight_copies = []
    for c, (lo, hi) in enumerate(CHUNKS):
        pair = []
        for h in range(2):
            cols = pl.ds(h * HIDDEN + lo, hi - lo)
            pair.append(start(joined_hbm.at[:, cols], w_ref.at[:, cols], 3 + 2 * c + h))
        weight_copies.append(pair)
    mixed_copy = start(mixed_hbm, mixed_ref, 2)
    turned = unpacker()
    extra_copy.wait()
    quarter = WIDTH // 4
    spread = dot(turned, extra_ref[...]).astype(BF16)
    for j in range(4):
        x_ref[SLOTS:, j * quarter : (j + 1) * quarter] = spread[j * SPARE : (j + 1) * SPARE]
    main_copy.wait()
    outgoing = []
    for c, (lo, hi) in enumerate(CHUNKS):
        slot = c % 2
        wide = hi - lo
        for copy in weight_copies[c]:
            copy.wait()
        act_ref[slot, 0, :, :wide] = dot(x_ref[...], w_ref[:, lo:hi])
        act_ref[slot, 1, :, :wide] = dot(x_ref[...], w_ref[:, HIDDEN + lo : HIDDEN + hi])
        for m in range(0, TOTAL, 64):
            gate = act_ref[slot, 0, m : m + 64, :wide]
            up = act_ref[slot, 1, m : m + 64, :wide]
            sigmoid = jax.nn.sigmoid(gate)
            silu = gate * sigmoid
            hidden_ref[m : m + 64, lo:hi] = (silu * up).astype(BF16)
            slopes_ref[m : m + 64, HIDDEN + lo : HIDDEN + hi] = silu.astype(BF16)
            slopes_ref[m : m + 64, lo:hi] = (up * sigmoid * (1.0 + gate * (1.0 - sigmoid))).astype(BF16)
        for n, (source, target, offset) in enumerate(
            ((hidden_ref, hidden_hbm, 0), (slopes_ref, slopes_hbm, 0), (slopes_ref, slopes_hbm, HIDDEN))
        ):
            cols = pl.ds(offset + lo, wide)
            copy = pltpu.make_async_copy(source.at[:, cols], target.at[:, cols], out_sems.at[3 * c + n])
            copy.start()
            outgoing.append(copy)
    mixed_copy.wait()
    projected = dot(hidden_ref[...], mixed_ref[...]).astype(BF16)
    out_ref[:, :EMBED] = projected[:SLOTS]
    quarter = EMBED // 4
    stacked = jnp.concatenate(
        [projected[SLOTS:, j * quarter : (j + 1) * quarter] for j in range(4)], axis=0
    )
    out_ref[:, EMBED:] = dot(packer(), stacked).astype(BF16)
    for copy in outgoing:
        copy.wait()


def weighted(chosen, gates):
    return jnp.where(chosen, gates, 0.0)


def split_product(chosen, gates, values):
    whole = weighted(chosen, gates)
    high = whole.astype(BF16)
    low = (whole - high.astype(F32)).astype(BF16)
    return dot_rows(high, values) + dot_rows(low, values)


def embed_kernel(routes_ref, gates_ref, answer_ref, base_ref, embedding_ref, unit_ref):
    main, quarters = choosers(routes_ref[...])
    gates = expanded(pair_gates(routes_ref[...], gates_ref[...]))
    mixture = split_product(main, gates, answer_ref[:, :EMBED])
    extra = jnp.concatenate(
        [split_product(quarters[j], gates, answer_ref[:, EMBED:]) for j in range(4)], axis=1
    )
    embedding = base_ref[...] + mixture + extra
    inverse = lax.rsqrt(jnp.mean(embedding * embedding, axis=1, keepdims=True) + EPSILON)
    embedding_ref[...] = embedding
    unit_ref[...] = (embedding * inverse).astype(BF16)


def loss_kernel(
    routes_ref, gates_ref, matches_ref, partner_ref, embedding_ref, unit_ref, key_ref,
    loss_ref, grad_ref, out_ref,
):
    embedding = embedding_ref[...]
    unit = unit_ref[...]
    keys = key_ref[...]
    coefficient = 1.0 / (EMBED * TEMPER)
    inverse = lax.rsqrt(jnp.mean(embedding * embedding, axis=1, keepdims=True) + EPSILON)
    unit_rows = embedding * inverse
    entry = iota((ROWS, ROWS), 0)

    def scores(rows, columns, matches):
        logits = dot_cols(rows, columns) * coefficient
        totals = jnp.log(jnp.sum(jnp.exp(logits), axis=0, keepdims=True))
        target = matches == entry
        chosen = jnp.sum(jnp.where(target, logits, 0.0), axis=0, keepdims=True)
        weights = jnp.exp(logits - totals) - jnp.where(target, 1.0, 0.0)
        return totals - chosen, weights.astype(BF16)

    loss, own = scores(keys, unit, matches_ref[...])
    loss_ref[...] = loss
    partner = scores(unit, keys, partner_ref[...].astype(jnp.int32))[1]
    upstream = (dot_rows(own, keys) + dot(partner, keys)) * coefficient
    grad = inverse * (upstream - unit_rows * jnp.mean(upstream * unit_rows, axis=1, keepdims=True))
    grad = grad.astype(BF16)
    grad_ref[...] = grad
    main, quarters = choosers(routes_ref[...])
    gates = expanded(pair_gates(routes_ref[...], gates_ref[...]))
    slot_gates = jnp.sum(weighted(main, gates), axis=1, keepdims=True)
    out_ref[:, :EMBED] = (slot_gates * dot(one_hot(main), grad)).astype(BF16)
    quarter = EMBED // 4
    total = jnp.zeros((SLOTS, quarter), F32)
    extra_gates = jnp.zeros((SLOTS, 1), F32)
    for j in range(4):
        total = total + dot(one_hot(quarters[j]), grad[:, j * quarter : (j + 1) * quarter])
        extra_gates = extra_gates + jnp.sum(weighted(quarters[j], gates), axis=1, keepdims=True)
    out_ref[:, EMBED:] = (extra_gates * total).astype(BF16)


def backward_kernel(
    arrived_ref, mixed_hbm, slopes_hbm, joined_hbm, out_hbm, grads_ref,
    mixed_ref, slopes_ref, w_ref, act_ref, joined_ref, extra_ref, out_ref, sems, out_sems,
):
    def start(source, target, index):
        copy = pltpu.make_async_copy(source, target, sems.at[index])
        copy.start()
        return copy

    mixed_copy = start(mixed_hbm, mixed_ref, 0)
    slopes_copy = start(slopes_hbm, slopes_ref, 1)
    weight_copies = [
        start(joined_hbm.at[pl.ds(n, TILE), :], w_ref.at[pl.ds(n, TILE), :], 2 + n // TILE)
        for n in range(0, WIDTH, TILE)
    ]
    quarter = EMBED // 4
    grads_ref[:SLOTS, :] = arrived_ref[:, :EMBED]
    spread = dot(unpacker(), arrived_ref[:, EMBED:]).astype(BF16)
    for j in range(4):
        grads_ref[SLOTS:, j * quarter : (j + 1) * quarter] = spread[j * SPARE : (j + 1) * SPARE]
    mixed_copy.wait()
    slopes_copy.wait()
    for c, (lo, hi) in enumerate(CHUNKS):
        slot = c % 2
        wide = hi - lo
        act_ref[slot, :, :wide] = dot_cols(grads_ref[...], mixed_ref[lo:hi, :])
        for m in range(0, TOTAL, 64):
            hidden_grad = act_ref[slot, m : m + 64, :wide]
            for offset in (0, HIDDEN):
                slope = slopes_ref[m : m + 64, offset + lo : offset + hi].astype(F32)
                joined_ref[m : m + 64, offset + lo : offset + hi] = (hidden_grad * slope).astype(BF16)
    outgoing = []
    quarter = WIDTH // 4
    for n in range(0, WIDTH, TILE):
        weight_copies[n // TILE].wait()
        result = dot_cols(joined_ref[...], w_ref[n : n + TILE, :]).astype(BF16)
        out_ref[:, n : n + TILE] = result[:SLOTS]
        j, within = n // quarter, n % quarter
        extra_ref[j * SPARE : (j + 1) * SPARE, within : within + TILE] = result[SLOTS:]
        cols = pl.ds(n, TILE)
        copy = pltpu.make_async_copy(out_ref.at[:, cols], out_hbm.at[:, cols], out_sems.at[n // TILE])
        copy.start()
        outgoing.append(copy)
    out_ref[:, WIDTH:] = dot(packer(), extra_ref[...]).astype(BF16)
    cols = pl.ds(WIDTH, quarter)
    copy = pltpu.make_async_copy(out_ref.at[:, cols], out_hbm.at[:, cols], out_sems.at[WIDTH // TILE])
    copy.start()
    outgoing.append(copy)
    for copy in outgoing:
        copy.wait()


def head_kernel(hidden_ref, grads_ref, tokens_ref, embed_grad_ref, down_ref, out_ref):
    inner = dot_rows(hidden_ref[...], grads_ref[...]).astype(BF16)
    for n in range(0, WIDTH, TILE):
        part = dot_rows(down_ref[:, n : n + TILE], inner)
        part = part + dot_rows(tokens_ref[:, n : n + TILE], embed_grad_ref[...])
        part = part.astype(BF16)
        for b in range(TILE // 32):
            row = n // 2 + 16 * b
            for core in range(2):
                out_ref[core, row : row + 16, :] = part[32 * b + 16 * core : 32 * b + 16 * core + 16]


def combine_kernel(routes_ref, back_ref, direct_ref, out_ref):
    main, quarters = choosers(routes_ref[...])
    main = one_hot(main)
    quarter = WIDTH // 4
    for j in range(4):
        cols = slice(j * quarter, (j + 1) * quarter)
        total = dot_rows(main, back_ref[:, cols]) + dot_rows(one_hot(quarters[j]), back_ref[:, WIDTH:])
        out_ref[:, cols] = (direct_ref[:, cols] + total).astype(BF16)


def call(kernel, outs, ins, scratch=(), flops=0, moved=0):
    def spec(space):
        return pl.BlockSpec(memory_space=space)

    return pl.pallas_call(
        kernel,
        out_shape=tuple(jax.ShapeDtypeStruct(shape, dtype) for shape, dtype, _ in outs),
        in_specs=[spec(space) for _, space in ins],
        out_specs=tuple(spec(space) for _, _, space in outs),
        scratch_shapes=scratch,
        compiler_params=pltpu.CompilerParams(vmem_limit_bytes=VMEM_LIMIT),
        cost_estimate=pl.CostEstimate(flops=flops, bytes_accessed=moved, transcendentals=0),
    )(*[value for value, _ in ins])


def exchanged(value, axes, parts):
    rows, width = value.shape
    blocks = value.reshape(parts, rows // parts, width)
    return lax.all_to_all(blocks, axes, 0, 0, tiled=True).reshape(rows, width)


def body(tokens, routes, gates, gate_up, down_proj, projection, matches):
    vmem, hbm = pltpu.VMEM, pl.ANY
    routes, gates = routes.T, gates.T
    weights_joined, weights_down = gate_up[0], down_proj[0]
    partner = [(i, i ^ EXPERTS // 2) for i in range(EXPERTS)]
    dma = pltpu.SemaphoreType.DMA

    (dispatch,) = call(
        dispatch_kernel, [((SLOTS, WIDTH * 5 // 4), BF16, vmem)], [(routes, vmem), (tokens, vmem)],
        flops=2 * SLOTS * ROWS * WIDTH * 2, moved=3 << 20,
    )
    received = exchanged(dispatch, EXPERT, EXPERTS)
    partner_matches = lax.ppermute(matches.astype(BF16), EXPERT, partner)
    mixed = dot(weights_down, projection).astype(BF16)
    base = dot(tokens, projection)

    packed_embed = ((SLOTS, EMBED * 5 // 4), BF16, vmem)
    packed, hidden, slopes = call(
        forward_kernel,
        [packed_embed, ((TOTAL, HIDDEN), BF16, hbm), ((TOTAL, 2 * HIDDEN), BF16, hbm)],
        [(received, hbm), (weights_joined, hbm), (mixed, hbm)],
        scratch=[
            pltpu.VMEM((TOTAL, WIDTH), BF16),
            pltpu.VMEM((SLOTS, WIDTH // 4), BF16),
            pltpu.VMEM((WIDTH, 2 * HIDDEN), BF16),
            pltpu.VMEM((HIDDEN, EMBED), BF16),
            pltpu.VMEM((2, 2, TOTAL, 256), F32),
            pltpu.VMEM((TOTAL, HIDDEN), BF16),
            pltpu.VMEM((TOTAL, 2 * HIDDEN), BF16),
            dma((3 + 2 * len(CHUNKS),)),
            dma((3 * len(CHUNKS),)),
        ],
        flops=2 * TOTAL * HIDDEN * (2 * WIDTH + EMBED), moved=22 << 20,
    )
    answer = exchanged(packed, EXPERT, EXPERTS)
    embedding, unit = call(
        embed_kernel,
        [((ROWS, EMBED), F32, vmem), ((ROWS, EMBED), BF16, vmem)],
        [(routes, vmem), (gates, vmem), (answer, vmem), (base, vmem)],
        flops=4 * SLOTS * ROWS * EMBED * 2, moved=2 << 20,
    )
    keys = lax.ppermute(unit, EXPERT, partner)
    row_loss, embed_grad, slot_grads = call(
        loss_kernel,
        [((1, ROWS), F32, vmem), ((ROWS, EMBED), BF16, vmem), packed_embed],
        [(routes, vmem), (gates, vmem), (matches, vmem), (partner_matches, vmem),
         (embedding, vmem), (unit, vmem), (keys, vmem)],
        flops=2 * SLOTS * ROWS * EMBED * 2, moved=2 << 20,
    )
    arrived = exchanged(slot_grads, EXPERT, EXPERTS)
    direct = dot_cols(embed_grad, projection)
    input_grads, grads = call(
        backward_kernel,
        [((SLOTS, WIDTH * 5 // 4), BF16, hbm), ((TOTAL, EMBED), BF16, vmem)],
        [(arrived, vmem), (mixed, hbm), (slopes, hbm), (weights_joined, hbm)],
        scratch=[
            pltpu.VMEM((HIDDEN, EMBED), BF16),
            pltpu.VMEM((TOTAL, 2 * HIDDEN), BF16),
            pltpu.VMEM((WIDTH, 2 * HIDDEN), BF16),
            pltpu.VMEM((2, TOTAL, 256), F32),
            pltpu.VMEM((TOTAL, 2 * HIDDEN), BF16),
            pltpu.VMEM((SLOTS, WIDTH // 4), BF16),
            pltpu.VMEM((SLOTS, WIDTH * 5 // 4), BF16),
            dma((2 + WIDTH // TILE,)),
            dma((1 + WIDTH // TILE,)),
        ],
        flops=2 * TOTAL * HIDDEN * (2 * WIDTH + EMBED), moved=22 << 20,
    )
    back = exchanged(input_grads, EXPERT, EXPERTS)
    (head,) = call(
        head_kernel,
        [((2, WIDTH // 2, EMBED), BF16, vmem)],
        [(hidden, vmem), (grads, vmem), (tokens, vmem), (embed_grad, vmem), (weights_down, vmem)],
        flops=2 * HIDDEN * EMBED * (TOTAL + WIDTH), moved=12 << 20,
    )
    halves = lax.all_to_all(head, "expert_2", 0, 0, tiled=True)
    half = (halves[0].astype(F32) + halves[1].astype(F32)).astype(BF16)
    parts = lax.all_to_all(
        half.reshape(64, 16, EMBED), ("dp", "expert_0", "expert_1"), 0, 0, tiled=True
    )
    summed = jnp.sum(parts.astype(F32), axis=0)
    device_count = lax.axis_size("dp") * EXPERTS
    grad_projection = summed * (1.0 / math.sqrt(ROWS * device_count))
    (grad_tokens,) = call(
        combine_kernel, [((ROWS, WIDTH), BF16, vmem)], [(routes, vmem), (back, vmem), (direct, vmem)],
        flops=2 * SLOTS * ROWS * WIDTH * 2, moved=4 << 20,
    )
    return grad_tokens, grad_projection, row_loss.reshape(ROWS)


def solution(mesh):
    torus = Mesh(
        mesh.devices.reshape(mesh.shape["dp"], 4, 4, 2), ("dp", "expert_0", "expert_1", "expert_2")
    )
    return jax.shard_map(
        body,
        mesh=torus,
        in_specs=(
            P(DP_EXPERT, None),
            P(DP_EXPERT, None),
            P(DP_EXPERT, None),
            P(EXPERT, None, None),
            P(EXPERT, None, None),
            P(),
            P(DP_EXPERT, None),
        ),
        out_specs=(P(DP_EXPERT, None), P(DP_EXPERT, None), P(DP_EXPERT)),
        check_vma=False,
    )
```

time: 266 us -> 215 us (0.81)
  matrix products: 65.8 us -> 8.19 us
  Pallas kernels: 0 us -> 49.9 us
  local copies, waits for them, and re-layouts: 37.1 us -> 8.78 us
  waiting for transfers between devices: 52.2 us -> 76.4 us
  blocking collectives: 72.6 us -> 48.8 us
  other arithmetic: 10.7 us -> 1.08 us
  starting transfers between devices: 24.4 us -> 20.2 us
    dot_general x17 -> x3, matrix products: 65.8 us -> 8.19 us  [the longest x2 7.39 us: dot(): return jnp.dot(left, right, preferred_element_type=F32)]
    pallas_call x0 -> x7, Pallas kernels: none -> 49.9 us  [call(): pl.pallas_call(kernel, out_shape=tuple((jax.ShapeDtypeStruct(shape, dtype...]
    all_to_all x3, waiting for transfers between devices: 46.1 us -> 72.3 us  [exchanged(): return lax.all_to_all(blocks, axes, 0, 0, tiled=True).reshape(rows, width)]
    reshape x8 -> x0, local copies, waits for them, and re-layouts: 25.2 us -> none  [the longest x1 5.19 us: body(): flat_input = received.reshape(source_count * item_count, model_width)]
    all_to_all x3, blocking collectives: 72.6 us -> 48.8 us  [the longest x1 27 us: body(): lax.all_to_all(half.reshape(64, 16, EMBED), ('dp', 'expert_0', 'expert_1'...]
    reduce_sum x5 -> x1, other arithmetic: 7.24 us -> 0.18 us  [body(): summed = jnp.sum(parts.astype(F32), axis=0)]
    unnamed x20 -> x30, local copies, waits for them, and re-layouts: 3.26 us -> 8.78 us
    add x1 -> x0, local copies, waits for them, and re-layouts: 5.33 us -> none  [body(): first_part + second_part]
  transfers between devices with their start and end apart: 5 -> 5, of which waited for: 4 -> 4; matrix products, arithmetic and copies ran while one was open for 14% -> 4% of each run, Pallas kernels for 0% -> 0%
where the time goes in v1:
time: 215 us; the launch traced here: 214 us
  waiting for transfers between devices  76.4 us (36%)
  Pallas kernels  49.9 us (23%)
  blocking collectives  48.8 us (23%)
  starting transfers between devices  20.2 us (9%)
  local copies, waits for them, and re-layouts  8.78 us (4%)
  matrix products  8.19 us (4%)
    all_to_all x3, waiting for transfers between devices, exchanged(): return lax.all_to_all(blocks, axes, 0, 0, tiled=True).reshape(rows, width)  72.3 us
    pallas_call x7, Pallas kernels, call(): pl.pallas_call(kernel, out_shape=tuple((jax.ShapeDtypeStruct(shape, dtype...  49.9 us
    all_to_all x1, blocking collectives, body(): lax.all_to_all(half.reshape(64, 16, EMBED), ('dp', 'expert_0', 'expert_1'...  27 us
    all_to_all x3, starting transfers between devices, exchanged(): return lax.all_to_all(blocks, axes, 0, 0, tiled=True).reshape(rows, width)  16.4 us
    all_to_all x1, blocking collectives, exchanged(): return lax.all_to_all(blocks, axes, 0, 0, tiled=True).reshape(rows, width)  16.2 us
    unnamed x30, local copies, waits for them, and re-layouts  8.78 us
    dot_general x2, matrix products, dot(): return jnp.dot(left, right, preferred_element_type=F32)  7.39 us
    all_to_all x1, blocking collectives, body(): halves = lax.all_to_all(head, 'expert_2', 0, 0, tiled=True)  5.6 us
  transfers between devices with their start and end apart: 5, of which 4 were waited for; matrix products, arithmetic and copies ran while one was open for 4% of the time, Pallas kernels for 0%

profile of v1, /device:TPU:0, one launch (start us, length us, event | category | flops | bytes accessed | tf_op | source)
XLA Modules:
  0.0 214.1 jit_solution(4194651884496591610)
XLA Ops:
  0.6 0.0 copy-start
  0.6 0.0 copy-start.3
  0.7 1.2 copy-done.3
  1.8 0.7 copy-done.6
  2.5 1.4 shard_map.94
  3.9 0.0 copy-start.1
  3.9 1.5 copy-done.1
  5.4 7.5 %all-to-all-start = ((bf16[32,16,2560]{2,1,0:T(8,128)(2,1)}), bf16[32,16,2560]{2,1,0:T(8,128)(2,1)}, u32[]{:S(2)}, u32[]{:S(2)}) async-start(bf16[32,16,2560]{2,1,0:T(8,128)(2,1)} %bitcast.21), calls=%async_computation | async-start | bytes 5242880 | tf_op jit(solution)/shard_map/all_to_all | solution.py:325
  13.0 0.0 copy-done
  13.0 6.9 %convolution_convert_fusion.mixed_hbm = bf16[1408,512]{1,0:T(8,128)(2,1)} fusion(bf16[2048,512]{1,0:T(8,128)(2,1)S(1)} %copy-done, bf16[1,1408,2048]{2,1,0:T(8,128)(2,1)} %param.11), kind=kOutput, calls=%fused_computation | convolution fusion | flops 2953510912 | bytes 9306112 | tf_op jit(solution)/shard_map/dot_general | solution.py:35
  19.9 27.7 %all-to-all-done = bf16[32,16,2560]{2,1,0:T(8,128)(2,1)} async-done(((bf16[32,16,2560]{2,1,0:T(8,128)(2,1)}), bf16[32,16,2560]{2,1,0:T(8,128)(2,1)}, u32[]{:S(2)}, u32[]{:S(2)}) %all-to-all-start) | async-done | bytes 2621472 | tf_op jit(solution)/shard_map/all_to_all | solution.py:325
  47.6 1.4 copy-done.12
  49.0 14.1 %shard_map.95 = (bf16[512,640]{1,0:T(8,128)(2,1)S(1)}, bf16[640,1408]{1,0:T(8,128)(2,1)S(1)}, bf16[640,2816]{1,0:T(8,128)(2,1)}) custom-call(bf16[512,2560]{1,0:T(8,128)(2,1)} %bitcast.3.recv_hbm, bf16[2048,2816]{1,0:T(8,128)(2,1)} %bitcast.34, bf16[1408,512]{1,0:T(8,128)(2,1)S(1)} %copy-done.12), custom_call_target="tpu_custom_call" | custom-call | flops 8304721920 | bytes 23068672 | tf_op jit(solution)/shard_map/pallas_call | solution.py:311
  63.1 0.0 copy-start.5
  63.1 0.8 copy-done.5
  63.9 1.3 copy-done.10
  65.2 4.0 %all-to-all-start.1 = ((bf16[32,16,640]{2,1,0:T(8,128)(2,1)}), bf16[32,16,640]{2,1,0:T(8,128)(2,1)S(1)}, u32[]{:S(2)}, u32[]{:S(2)}) async-start(bf16[32,16,640]{2,1,0:T(8,128)(2,1)} %bitcast.24), calls=%async_computation.1 | async-start | bytes 1310720 | tf_op jit(solution)/shard_map/all_to_all | solution.py:325
  69.2 0.0 copy-done.4
  69.2 0.0 copy-start.9
  69.3 0.5 fusion.1.base_ref
  69.7 12.0 %all-to-all-done.1 = bf16[32,16,640]{2,1,0:T(8,128)(2,1)S(1)} async-done(((bf16[32,16,640]{2,1,0:T(8,128)(2,1)}), bf16[32,16,640]{2,1,0:T(8,128)(2,1)S(1)}, u32[]{:S(2)}, u32[]{:S(2)}) %all-to-all-start.1) | async-done | bytes 655392 | tf_op jit(solution)/shard_map/all_to_all | solution.py:325
  81.7 0.0 copy-done.7
  81.7 0.0 copy-done.8
  81.7 0.9 shard_map.96
  82.6 1.9 collective-permute-start.1
  84.6 0.0 copy-done.9
  84.6 1.9 collective-permute-start
  86.4 4.2 %collective-permute-done.partner_ref = bf16[1,128]{1,0:T(2,128)(2,1)S(1)} collective-permute-done((bf16[1,128]{1,0:T(2,128)(2,1)S(1)}, bf16[1,128]{1,0:T(2,128)(2,1)S(1)}, u32[]{:S(2)}, u32[]{:S(2)}) %collective-permute-start) | collective-permute-done | bytes 288 | tf_op jit(solution)/shard_map/ppermute | solution.py:340
  90.6 0.0 collective-permute-done.1.key_ref
  90.6 1.1 shard_map.97
  91.7 16.2 %all_to_all.30 = bf16[32,16,640]{2,1,0:T(8,128)(2,1)S(1)} all-to-all(bf16[32,16,640]{2,1,0:T(8,128)(2,1)S(1)} %bitcast.25), channel_id=1, replica_groups=mesh['dp'=4,'expert_0'=4,'expert_1'=4,'expert_2'=2] {'expert_0','expert_..., dimensions={0} | all-to-all | bytes 1310720 | tf_op jit(solution)/shard_map/all_to_all | solution.py:325
  107.9 0.0 copy-done.13
  107.9 21.1 %shard_map.98 = (bf16[512,2560]{1,0:T(8,128)(2,1)S(1)}, bf16[640,512]{1,0:T(8,128)(2,1)S(1)}) custom-call(bf16[512,640]{1,0:T(8,128)(2,1)S(1)} %bitcast.26, bf16[1408,512]{1,0:T(8,128)(2,1)S(1)} %copy-done.13, bf16[640,2816]{1,0:T(8,128)(2,1)} %get-tuple-element.17.slopes_hbm, bf16[2048,2816]{1,0:T(8,128)(2,1)} %bitcast.35), custom_call_target="tpu_custom_call" | custom-call | flops 8304721920 | bytes 23068672 | tf_op jit(solution)/shard_map/pallas_call | solution.py:311
  129.1 0.0 copy-start.2
  129.1 1.5 copy-done.2
  130.6 0.0 copy-done.11
  130.6 7.7 %shard_map.100 = bf16[2,1024,512]{2,1,0:T(8,128)(2,1)S(1)} custom-call(bf16[640,1408]{1,0:T(8,128)(2,1)S(1)} %copy-done.11, bf16[640,512]{1,0:T(8,128)(2,1)S(1)} %get-tuple-element.21.grads_ref, bf16[128,2048]{1,0:T(8,128)(2,1)S(1)} %copy-done.4, bf16[128,512]{1,0:T(8,128)(2,1)S(1)} %get-tuple-element.19.embed_grad_ref, bf16[1408,2048]{1,0:T(8,128)(2,1)} %bitcast.36), custom_call_target="tpu_custom_call" | custom-call | flops 3875536896 | bytes 12582912 | tf_op jit(solution)/shard_map/pallas_call | solution.py:311
  138.3 5.6 %all_to_all.31 = bf16[2,1024,512]{2,1,0:T(8,128)(2,1)S(1)} all-to-all(bf16[2,1024,512]{2,1,0:T(8,128)(2,1)S(1)} %shard_map.100), channel_id=1, replica_groups=mesh['dp'=4,'expert_0'=4,'expert_1'=4,'expert_2'=2] {'expert_2'}, dimensions={0} | all-to-all | bytes 4194304 | tf_op jit(solution)/shard_map/all_to_all | solution.py:403
  143.9 0.3 add_convert_fusion
  144.2 27.0 %all_to_all.32 = bf16[64,16,512]{2,1,0:T(8,128)(2,1)} all-to-all(bf16[64,16,512]{2,1,0:T(8,128)(2,1)S(1)} %bitcast.33), channel_id=1, replica_groups=mesh['dp'=4,'expert_0'=4,'expert_1'=4,'expert_2'=2] {'dp','expert_0','ex..., dimensions={0} | all-to-all | bytes 2097152 | tf_op jit(solution)/shard_map/all_to_all | solution.py:405
  171.2 4.8 %all-to-all-start.3 = ((bf16[32,16,2560]{2,1,0:T(8,128)(2,1)}), bf16[32,16,2560]{2,1,0:T(8,128)(2,1)}, u32[]{:S(2)}, u32[]{:S(2)}) async-start(bf16[32,16,2560]{2,1,0:T(8,128)(2,1)} %bitcast.22), calls=%async_computation.3 | async-start | bytes 5242880 | tf_op jit(solution)/shard_map/all_to_all | solution.py:325
  176.0 0.0 copy-start.14
  176.0 0.8 fusion.2.direct_ref
  176.8 0.4 copy-done.14
  177.2 0.2 convert_reduce_fusion
  177.4 0.6 broadcast_multiply_fusion
  178.0 32.6 %all-to-all-done.3 = bf16[32,16,2560]{2,1,0:T(8,128)(2,1)} async-done(((bf16[32,16,2560]{2,1,0:T(8,128)(2,1)}), bf16[32,16,2560]{2,1,0:T(8,128)(2,1)}, u32[]{:S(2)}, u32[]{:S(2)}) %all-to-all-start.3) | async-done | bytes 2621472 | tf_op jit(solution)/shard_map/all_to_all | solution.py:325
  210.6 3.5 %shard_map.99 = bf16[128,2048]{1,0:T(8,128)(2,1)} custom-call(s32[4,128]{1,0:T(4,128)S(1)} %bitcast.30, bf16[512,2560]{1,0:T(8,128)(2,1)} %bitcast.11.back_ref, f32[128,2048]{1,0:T(8,128)S(1)} %fusion.2.direct_ref), custom_call_target="tpu_custom_call" | custom-call | flops 536870912 | bytes 4194304 | tf_op jit(solution)/shard_map/pallas_call | solution.py:311
  (9 shorter events, 0.0 us)
Async XLA Ops:
  0.6 12.3 %copy-start = (bf16[2048,512]{1,0:T(8,128)(2,1)S(1)}, bf16[2048,512]{1,0:T(8,128)(2,1)}, u32[]{:S(2)}) copy-start(bf16[2048,512]{1,0:T(8,128)(2,1)} %param.12) | copy-start | bytes 6291460
  0.6 1.2 copy-start.3
  1.8 0.7 copy-start.6
  3.9 1.5 copy-start.1
  5.4 42.2 %all-to-all-start = ((bf16[32,16,2560]{2,1,0:T(8,128)(2,1)}), bf16[32,16,2560]{2,1,0:T(8,128)(2,1)}, u32[]{:S(2)}, u32[]{:S(2)}) async-start(bf16[32,16,2560]{2,1,0:T(8,128)(2,1)} %bitcast.21), calls=%async_computation | async-start | bytes 5242880 | tf_op jit(solution)/shard_map/all_to_all | solution.py:325
  47.6 1.4 copy-start.12
  49.0 20.3 %copy-start.4 = (bf16[128,2048]{1,0:T(8,128)(2,1)S(1)}, bf16[128,2048]{1,0:T(8,128)(2,1)}, u32[]{:S(2)}) copy-start(bf16[128,2048]{1,0:T(8,128)(2,1)} %tokens_ref.3) | copy-start | bytes 1572868
  63.1 0.8 copy-start.5
  63.9 1.3 copy-start.10
  65.2 16.5 %copy-start.7 = (s32[128,4]{0,1:T(4,128)S(1)}, s32[128,4]{0,1:T(4,128)}, u32[]{:S(2)}) copy-start(s32[128,4]{0,1:T(4,128)} %param.8) | copy-start | bytes 6148
  65.2 16.5 %copy-start.8 = (f32[128,4]{0,1:T(4,128)S(1)}, f32[128,4]{0,1:T(4,128)}, u32[]{:S(2)}) copy-start(f32[128,4]{0,1:T(4,128)} %param.9) | copy-start | bytes 6148
  65.2 16.5 %all-to-all-start.1 = ((bf16[32,16,640]{2,1,0:T(8,128)(2,1)}), bf16[32,16,640]{2,1,0:T(8,128)(2,1)S(1)}, u32[]{:S(2)}, u32[]{:S(2)}) async-start(bf16[32,16,640]{2,1,0:T(8,128)(2,1)} %bitcast.24), calls=%async_computation.1 | async-start | bytes 1310720 | tf_op jit(solution)/shard_map/all_to_all | solution.py:325
  69.2 15.3 %copy-start.9 = (s32[1,128]{1,0:T(1,128)S(1)}, s32[1,128]{1,0:T(1,128)}, u32[]{:S(2)}) copy-start(s32[1,128]{1,0:T(1,128)} %matches_ref.1) | copy-start | bytes 1540
  81.7 26.2 %copy-start.13 = (bf16[1408,512]{1,0:T(8,128)(2,1)S(1)}, bf16[1408,512]{1,0:T(8,128)(2,1)}, u32[]{:S(2)}) copy-start(bf16[1408,512]{1,0:T(8,128)(2,1)} %convolution_convert_fusion.mixed_hbm) | copy-start | bytes 4325380
  82.6 8.0 %collective-permute-start.1 = (bf16[128,512]{1,0:T(8,128)(2,1)S(1)}, bf16[128,512]{1,0:T(8,128)(2,1)S(1)}, u32[]{:S(2)}, u32[]{:S(2)}) collective-permute-start(bf16[128,512]{1,0:T(8,128)(2,1)S(1)} %get-tuple-element.15.unit_ref), channel_id=1, source_target_pairs={{0,16},{1,17},{2,18},{3,19},{4,20},{5,21},{6,22},{7,23},{8,24},{9,... | collective-permute-start | bytes 393224 | tf_op jit(solution)/shard_map/ppermute | solution.py:369
  84.6 6.0 %collective-permute-start = (bf16[1,128]{1,0:T(2,128)(2,1)S(1)}, bf16[1,128]{1,0:T(2,128)(2,1)S(1)}, u32[]{:S(2)}, u32[]{:S(2)}) collective-permute-start(bf16[1,128]{1,0:T(2,128)(2,1)S(1)} %convert_element_type.26), channel_id=1, source_target_pairs={{0,16},{1,17},{2,18},{3,19},{4,20},{5,21},{6,22},{7,23},{8,24},{9,... | collective-permute-start | bytes 776 | tf_op jit(solution)/shard_map/ppermute | solution.py:340
  107.9 22.7 %copy-start.11 = (bf16[640,1408]{1,0:T(8,128)(2,1)S(1)}, bf16[640,1408]{1,0:T(8,128)(2,1)}, u32[]{:S(2)}) copy-start(bf16[640,1408]{1,0:T(8,128)(2,1)} %copy-done.10) | copy-start | bytes 5406724
  129.1 1.5 copy-start.2
  171.2 39.4 %all-to-all-start.3 = ((bf16[32,16,2560]{2,1,0:T(8,128)(2,1)}), bf16[32,16,2560]{2,1,0:T(8,128)(2,1)}, u32[]{:S(2)}, u32[]{:S(2)}) async-start(bf16[32,16,2560]{2,1,0:T(8,128)(2,1)} %bitcast.22), calls=%async_computation.3 | async-start | bytes 5242880 | tf_op jit(solution)/shard_map/all_to_all | solution.py:325
  176.0 1.2 copy-start.14

commit v2 on v1

--- a/solution.py
+++ b/solution.py
@@ -28,7 +28,7 @@
 TILE = 256
 F32 = jnp.float32
 BF16 = jnp.bfloat16
-VMEM_LIMIT = 48 * 1024 * 1024
+VMEM_LIMIT = 24 * 1024 * 1024
 
 
 def dot(left, right):
@@ -95,75 +95,78 @@
     return one_hot(iota((SLOTS, SLOTS), 1) == wanted)
 
 
-def dispatch_kernel(routes_ref, tokens_ref, out_ref):
+def dispatch_kernel(routes_hbm, tokens_hbm, out_hbm, routes_ref, tokens_ref, out_ref, sems, out_sems):
+    routes_copy = pltpu.make_async_copy(routes_hbm, routes_ref, sems.at[0])
+    tokens_copy = pltpu.make_async_copy(tokens_hbm, tokens_ref, sems.at[1])
+    routes_copy.start()
+    tokens_copy.start()
+    routes_copy.wait()
     main, quarters = choosers(routes_ref[...])
-    out_ref[:, :WIDTH] = dot(one_hot(main), tokens_ref[...]).astype(BF16)
+    main = one_hot(main)
     quarter = WIDTH // 4
     total = jnp.zeros((SLOTS, quarter), F32)
-    for j in range(4):
-        total = total + dot(one_hot(quarters[j]), tokens_ref[:, j * quarter : (j + 1) * quarter])
-    out_ref[:, WIDTH:] = total.astype(BF16)
+    tokens_copy.wait()
+    outgoing = []
+    for j in range(5):
+        cols = slice(j * quarter, (j + 1) * quarter)
+        if j < 4:
+            out_ref[:, cols] = dot(main, tokens_ref[:, cols]).astype(BF16)
+            total = total + dot(one_hot(quarters[j]), tokens_ref[:, cols])
+        else:
+            out_ref[:, cols] = total.astype(BF16)
+        part = pl.ds(j * quarter, quarter)
+        copy = pltpu.make_async_copy(out_ref.at[:, part], out_hbm.at[:, part], out_sems.at[j])
+        copy.start()
+        outgoing.append(copy)
+    for copy in outgoing:
+        copy.wait()
 
 
 def forward_kernel(
-    recv_hbm, joined_hbm, mixed_hbm, out_ref, hidden_hbm, slopes_hbm,
-    x_ref, extra_ref, w_ref, mixed_ref, act_ref, hidden_ref, slopes_ref, sems, out_sems,
+    recv_hbm, w_ref, mixed_ref, out_hbm, hidden_ref, slopes_ref,
+    x_ref, extra_ref, act_ref, out_ref, sems, out_sems,
 ):
-    def start(source, target, index):
-        copy = pltpu.make_async_copy(source, target, sems.at[index])
-        copy.start()
-        return copy
-
-    extra_copy = start(recv_hbm.at[:, pl.ds(WIDTH, WIDTH // 4)], extra_ref, 0)
-    main_copy = start(recv_hbm.at[:, pl.ds(0, WIDTH)], x_ref.at[pl.ds(0, SLOTS), :], 1)
-    weight_copies = []
-    for c, (lo, hi) in enumerate(CHUNKS):
-        pair = []
-        for h in range(2):
-            cols = pl.ds(h * HIDDEN + lo, hi - lo)
-            pair.append(start(joined_hbm.at[:, cols], w_ref.at[:, cols], 3 + 2 * c + h))
-        weight_copies.append(pair)
-    mixed_copy = start(mixed_hbm, mixed_ref, 2)
+    quarter = WIDTH // 4
+    extra_copy = pltpu.make_async_copy(recv_hbm.at[:, pl.ds(WIDTH, quarter)], extra_ref, sems.at[0])
+    extra_copy.start()
+    main_copy = pltpu.make_async_copy(
+        recv_hbm.at[:, pl.ds(0, WIDTH)], x_ref.at[pl.ds(0, SLOTS), :], sems.at[1]
+    )
+    main_copy.start()
     turned = unpacker()
     extra_copy.wait()
-    quarter = WIDTH // 4
     spread = dot(turned, extra_ref[...]).astype(BF16)
     for j in range(4):
         x_ref[SLOTS:, j * quarter : (j + 1) * quarter] = spread[j * SPARE : (j + 1) * SPARE]
     main_copy.wait()
-    outgoing = []
     for c, (lo, hi) in enumerate(CHUNKS):
         slot = c % 2
         wide = hi - lo
-        for copy in weight_copies[c]:
-            copy.wait()
         act_ref[slot, 0, :, :wide] = dot(x_ref[...], w_ref[:, lo:hi])
         act_ref[slot, 1, :, :wide] = dot(x_ref[...], w_ref[:, HIDDEN + lo : HIDDEN + hi])
         for m in range(0, TOTAL, 64):
             gate = act_ref[slot, 0, m : m + 64, :wide]
             up = act_ref[slot, 1, m : m + 64, :wide]
-            sigmoid = jax.nn.sigmoid(gate)
+            sigmoid = 0.5 + 0.5 * jnp.tanh(0.5 * gate)
             silu = gate * sigmoid
             hidden_ref[m : m + 64, lo:hi] = (silu * up).astype(BF16)
             slopes_ref[m : m + 64, HIDDEN + lo : HIDDEN + hi] = silu.astype(BF16)
             slopes_ref[m : m + 64, lo:hi] = (up * sigmoid * (1.0 + gate * (1.0 - sigmoid))).astype(BF16)
-        for n, (source, target, offset) in enumerate(
-            ((hidden_ref, hidden_hbm, 0), (slopes_ref, slopes_hbm, 0), (slopes_ref, slopes_hbm, HIDDEN))
-        ):
-            cols = pl.ds(offset + lo, wide)
-            copy = pltpu.make_async_copy(source.at[:, cols], target.at[:, cols], out_sems.at[3 * c + n])
-            copy.start()
-            outgoing.append(copy)
-    mixed_copy.wait()
     projected = dot(hidden_ref[...], mixed_ref[...]).astype(BF16)
     out_ref[:, :EMBED] = projected[:SLOTS]
+    cols = pl.ds(0, EMBED)
+    first = pltpu.make_async_copy(out_ref.at[:, cols], out_hbm.at[:, cols], out_sems.at[0])
+    first.start()
     quarter = EMBED // 4
     stacked = jnp.concatenate(
         [projected[SLOTS:, j * quarter : (j + 1) * quarter] for j in range(4)], axis=0
     )
     out_ref[:, EMBED:] = dot(packer(), stacked).astype(BF16)
-    for copy in outgoing:
-        copy.wait()
+    cols = pl.ds(EMBED, quarter)
+    second = pltpu.make_async_copy(out_ref.at[:, cols], out_hbm.at[:, cols], out_sems.at[1])
+    second.start()
+    first.wait()
+    second.wait()
 
 
 def weighted(chosen, gates):
@@ -231,27 +234,14 @@
 
 
 def backward_kernel(
-    arrived_ref, mixed_hbm, slopes_hbm, joined_hbm, out_hbm, grads_ref,
-    mixed_ref, slopes_ref, w_ref, act_ref, joined_ref, extra_ref, out_ref, sems, out_sems,
+    arrived_ref, mixed_ref, slopes_ref, w_ref, out_hbm, grads_ref,
+    act_ref, joined_ref, extra_ref, out_ref, out_sems,
 ):
-    def start(source, target, index):
-        copy = pltpu.make_async_copy(source, target, sems.at[index])
-        copy.start()
-        return copy
-
-    mixed_copy = start(mixed_hbm, mixed_ref, 0)
-    slopes_copy = start(slopes_hbm, slopes_ref, 1)
-    weight_copies = [
-        start(joined_hbm.at[pl.ds(n, TILE), :], w_ref.at[pl.ds(n, TILE), :], 2 + n // TILE)
-        for n in range(0, WIDTH, TILE)
-    ]
     quarter = EMBED // 4
     grads_ref[:SLOTS, :] = arrived_ref[:, :EMBED]
     spread = dot(unpacker(), arrived_ref[:, EMBED:]).astype(BF16)
     for j in range(4):
         grads_ref[SLOTS:, j * quarter : (j + 1) * quarter] = spread[j * SPARE : (j + 1) * SPARE]
-    mixed_copy.wait()
-    slopes_copy.wait()
     for c, (lo, hi) in enumerate(CHUNKS):
         slot = c % 2
         wide = hi - lo
@@ -263,35 +253,53 @@
                 joined_ref[m : m + 64, offset + lo : offset + hi] = (hidden_grad * slope).astype(BF16)
     outgoing = []
     quarter = WIDTH // 4
+
+    def send(start, wide, index):
+        cols = pl.ds(start, wide)
+        copy = pltpu.make_async_copy(out_ref.at[:, cols], out_hbm.at[:, cols], out_sems.at[index])
+        copy.start()
+        outgoing.append(copy)
+
     for n in range(0, WIDTH, TILE):
-        weight_copies[n // TILE].wait()
         result = dot_cols(joined_ref[...], w_ref[n : n + TILE, :]).astype(BF16)
         out_ref[:, n : n + TILE] = result[:SLOTS]
         j, within = n // quarter, n % quarter
         extra_ref[j * SPARE : (j + 1) * SPARE, within : within + TILE] = result[SLOTS:]
-        cols = pl.ds(n, TILE)
-        copy = pltpu.make_async_copy(out_ref.at[:, cols], out_hbm.at[:, cols], out_sems.at[n // TILE])
-        copy.start()
-        outgoing.append(copy)
+        if n % quarter:
+            send(j * quarter, quarter, j)
     out_ref[:, WIDTH:] = dot(packer(), extra_ref[...]).astype(BF16)
-    cols = pl.ds(WIDTH, quarter)
-    copy = pltpu.make_async_copy(out_ref.at[:, cols], out_hbm.at[:, cols], out_sems.at[WIDTH // TILE])
-    copy.start()
-    outgoing.append(copy)
+    send(WIDTH, quarter, 4)
     for copy in outgoing:
         copy.wait()
 
 
-def head_kernel(hidden_ref, grads_ref, tokens_ref, embed_grad_ref, down_ref, out_ref):
+def head_kernel(
+    core_ref, hidden_ref, grads_ref, tokens_ref, embed_grad_ref, down_ref, own_ref, other_ref
+):
+    first = core_ref[0] == 0
     inner = dot_rows(hidden_ref[...], grads_ref[...]).astype(BF16)
     for n in range(0, WIDTH, TILE):
         part = dot_rows(down_ref[:, n : n + TILE], inner)
         part = part + dot_rows(tokens_ref[:, n : n + TILE], embed_grad_ref[...])
-        part = part.astype(BF16)
         for b in range(TILE // 32):
             row = n // 2 + 16 * b
-            for core in range(2):
-                out_ref[core, row : row + 16, :] = part[32 * b + 16 * core : 32 * b + 16 * core + 16]
+            even, odd = part[32 * b : 32 * b + 16], part[32 * b + 16 : 32 * b + 32]
+            own_ref[row : row + 16, :] = jnp.where(first, even, odd)
+            other_ref[row : row + 16, :] = jnp.where(first, odd, even).astype(BF16)
+
+
+def share_kernel(place_ref, own_ref, *refs):
+    received, (kept_ref, *sent_refs) = refs[: len(refs) - 4], refs[len(refs) - 4 :]
+    place = place_ref[0]
+    for k in range(4):
+        quarter = jnp.bitwise_xor(place, k)
+        total = own_ref[quarter]
+        for ref in received:
+            total = total + ref[quarter].astype(F32)
+        if k == 0:
+            kept_ref[...] = total
+        else:
+            sent_refs[k - 1][...] = total.astype(BF16)
 
 
 def combine_kernel(routes_ref, back_ref, direct_ref, out_ref):
@@ -326,36 +334,41 @@
 
 
 def body(tokens, routes, gates, gate_up, down_proj, projection, matches):
-    vmem, hbm = pltpu.VMEM, pl.ANY
+    vmem, hbm, smem = pltpu.VMEM, pltpu.HBM, pltpu.SMEM
     routes, gates = routes.T, gates.T
     weights_joined, weights_down = gate_up[0], down_proj[0]
     partner = [(i, i ^ EXPERTS // 2) for i in range(EXPERTS)]
     dma = pltpu.SemaphoreType.DMA
 
     (dispatch,) = call(
-        dispatch_kernel, [((SLOTS, WIDTH * 5 // 4), BF16, vmem)], [(routes, vmem), (tokens, vmem)],
+        dispatch_kernel, [((SLOTS, WIDTH * 5 // 4), BF16, hbm)], [(routes, hbm), (tokens, hbm)],
+        scratch=[
+            pltpu.VMEM((TOP, ROWS), jnp.int32),
+            pltpu.VMEM((ROWS, WIDTH), BF16),
+            pltpu.VMEM((SLOTS, WIDTH * 5 // 4), BF16),
+            dma((2,)),
+            dma((5,)),
+        ],
         flops=2 * SLOTS * ROWS * WIDTH * 2, moved=3 << 20,
     )
+    partner_matches = lax.ppermute(matches.astype(BF16), EXPERT, partner)
     received = exchanged(dispatch, EXPERT, EXPERTS)
-    partner_matches = lax.ppermute(matches.astype(BF16), EXPERT, partner)
     mixed = dot(weights_down, projection).astype(BF16)
     base = dot(tokens, projection)
-
-    packed_embed = ((SLOTS, EMBED * 5 // 4), BF16, vmem)
+    received, partner_matches = lax.optimization_barrier((received, partner_matches))
+
+    packed_shape = (SLOTS, EMBED * 5 // 4)
     packed, hidden, slopes = call(
         forward_kernel,
-        [packed_embed, ((TOTAL, HIDDEN), BF16, hbm), ((TOTAL, 2 * HIDDEN), BF16, hbm)],
-        [(received, hbm), (weights_joined, hbm), (mixed, hbm)],
+        [(packed_shape, BF16, hbm), ((TOTAL, HIDDEN), BF16, vmem), ((TOTAL, 2 * HIDDEN), BF16, vmem)],
+        [(received, hbm), (weights_joined, vmem), (mixed, vmem)],
         scratch=[
             pltpu.VMEM((TOTAL, WIDTH), BF16),
             pltpu.VMEM((SLOTS, WIDTH // 4), BF16),
-            pltpu.VMEM((WIDTH, 2 * HIDDEN), BF16),
-            pltpu.VMEM((HIDDEN, EMBED), BF16),
             pltpu.VMEM((2, 2, TOTAL, 256), F32),
-            pltpu.VMEM((TOTAL, HIDDEN), BF16),
-            pltpu.VMEM((TOTAL, 2 * HIDDEN), BF16),
-            dma((3 + 2 * len(CHUNKS),)),
-            dma((3 * len(CHUNKS),)),
+            pltpu.VMEM(packed_shape, BF16),
+            dma((2,)),
+            dma((2,)),
         ],
         flops=2 * TOTAL * HIDDEN * (2 * WIDTH + EMBED), moved=22 << 20,
     )
@@ -369,7 +382,7 @@
     keys = lax.ppermute(unit, EXPERT, partner)
     row_loss, embed_grad, slot_grads = call(
         loss_kernel,
-        [((1, ROWS), F32, vmem), ((ROWS, EMBED), BF16, vmem), packed_embed],
+        [((1, ROWS), F32, vmem), ((ROWS, EMBED), BF16, vmem), (packed_shape, BF16, vmem)],
         [(routes, vmem), (gates, vmem), (matches, vmem), (partner_matches, vmem),
          (embedding, vmem), (unit, vmem), (keys, vmem)],
         flops=2 * SLOTS * ROWS * EMBED * 2, moved=2 << 20,
@@ -379,33 +392,43 @@
     input_grads, grads = call(
         backward_kernel,
         [((SLOTS, WIDTH * 5 // 4), BF16, hbm), ((TOTAL, EMBED), BF16, vmem)],
-        [(arrived, vmem), (mixed, hbm), (slopes, hbm), (weights_joined, hbm)],
+        [(arrived, vmem), (mixed, vmem), (slopes, vmem), (weights_joined, vmem)],
         scratch=[
-            pltpu.VMEM((HIDDEN, EMBED), BF16),
-            pltpu.VMEM((TOTAL, 2 * HIDDEN), BF16),
-            pltpu.VMEM((WIDTH, 2 * HIDDEN), BF16),
             pltpu.VMEM((2, TOTAL, 256), F32),
             pltpu.VMEM((TOTAL, 2 * HIDDEN), BF16),
             pltpu.VMEM((SLOTS, WIDTH // 4), BF16),
             pltpu.VMEM((SLOTS, WIDTH * 5 // 4), BF16),
-            dma((2 + WIDTH // TILE,)),
-            dma((1 + WIDTH // TILE,)),
+            dma((5,)),
         ],
         flops=2 * TOTAL * HIDDEN * (2 * WIDTH + EMBED), moved=22 << 20,
     )
     back = exchanged(input_grads, EXPERT, EXPERTS)
-    (head,) = call(
+
+    def place(axis):
+        return lax.axis_index(axis).astype(jnp.int32).reshape(1), smem
+
+    own, other = call(
         head_kernel,
-        [((2, WIDTH // 2, EMBED), BF16, vmem)],
-        [(hidden, vmem), (grads, vmem), (tokens, vmem), (embed_grad, vmem), (weights_down, vmem)],
-        flops=2 * HIDDEN * EMBED * (TOTAL + WIDTH), moved=12 << 20,
-    )
-    halves = lax.all_to_all(head, "expert_2", 0, 0, tiled=True)
-    half = (halves[0].astype(F32) + halves[1].astype(F32)).astype(BF16)
-    parts = lax.all_to_all(
-        half.reshape(64, 16, EMBED), ("dp", "expert_0", "expert_1"), 0, 0, tiled=True
-    )
-    summed = jnp.sum(parts.astype(F32), axis=0)
+        [((WIDTH // 2, EMBED), F32, vmem), ((WIDTH // 2, EMBED), BF16, vmem)],
+        [place("expert_2"), (hidden, vmem), (grads, vmem), (tokens, vmem), (embed_grad, vmem),
+         (weights_down, vmem)],
+    )
+    arrivals = [lax.ppermute(other, "expert_2", [(0, 1), (1, 0)])]
+    for axis in ("dp", "expert_0", "expert_1"):
+        rows = own.shape[0] // 4
+        own, *sent = call(
+            share_kernel,
+            [((rows, EMBED), F32, vmem)] + [((rows, EMBED), BF16, vmem)] * 3,
+            [place(axis), (own.reshape(4, rows, EMBED), vmem)]
+            + [(value.reshape(4, rows, EMBED), vmem) for value in arrivals],
+        )
+        arrivals = [
+            lax.ppermute(value, axis, [(i, i ^ (k + 1)) for i in range(4)])
+            for k, value in enumerate(sent)
+        ]
+    summed = own
+    for value in arrivals:
+        summed = summed + value.astype(F32)
     device_count = lax.axis_size("dp") * EXPERTS
     grad_projection = summed * (1.0 / math.sqrt(ROWS * device_count))
     (grad_tokens,) = call(

time: 215 us -> 198 us (0.921)
  blocking collectives: 48.8 us -> 15.9 us
  local copies, waits for them, and re-layouts: 8.78 us -> 29.7 us
  starting transfers between devices: 20.2 us -> 37 us
  Pallas kernels: 49.9 us -> 37.7 us
  waiting for transfers between devices: 76.4 us -> 67.4 us
    all_to_all x3, waiting for transfers between devices: 72.3 us -> 13.3 us  [exchanged(): return lax.all_to_all(blocks, axes, 0, 0, tiled=True).reshape(rows, width)]
    all_to_all x2 -> x0, blocking collectives: 32.6 us -> none  [the longest x1 27 us: body(): lax.all_to_all(half.reshape(64, 16, EMBED), ('dp', 'expert_0', 'expert_1'...]
    ppermute x0 -> x10, waiting for transfers between devices: none -> 25.2 us  [the longest x9 22.7 us: body(): lax.ppermute(value, axis, [(i, i ^ k + 1) for i in range(4)])]
    unnamed x30 -> x46, local copies, waits for them, and re-layouts: 8.78 us -> 29.7 us
    ppermute x1, waiting for transfers between devices: 4.15 us -> 23 us  [body(): partner_matches = lax.ppermute(matches.astype(BF16), EXPERT, partner)]
    ppermute x0 -> x10, starting transfers between devices: none -> 15 us  [the longest x9 14.5 us: body(): lax.ppermute(value, axis, [(i, i ^ k + 1) for i in range(4)])]
    pallas_call x7 -> x10, Pallas kernels: 49.9 us -> 37.7 us  [call(): pl.pallas_call(kernel, out_shape=tuple((jax.ShapeDtypeStruct(shape, dtype...]
    ppermute x1, waiting for transfers between devices: 0.01 us -> 5.94 us  [body(): keys = lax.ppermute(unit, EXPERT, partner)]
  transfers between devices with their start and end apart: 5 -> 15, of which waited for: 4 -> 12; matrix products, arithmetic and copies ran while one was open for 4% -> 4% of each run, Pallas kernels for 0% -> 4%
where the time goes in v2:
time: 198 us; the launch traced here: 197 us
  waiting for transfers between devices  67.4 us (34%)
  Pallas kernels  37.7 us (19%)
  starting transfers between devices  37 us (19%)
  local copies, waits for them, and re-layouts  29.7 us (15%)
  blocking collectives  15.9 us (8%)
  matrix products  8.14 us (4%)
    pallas_call x10, Pallas kernels, call(): pl.pallas_call(kernel, out_shape=tuple((jax.ShapeDtypeStruct(shape, dtype...  37.7 us
    unnamed x46, local copies, waits for them, and re-layouts  29.7 us
    ppermute x1, waiting for transfers between devices, body(): partner_matches = lax.ppermute(matches.astype(BF16), EXPERT, partner)  23 us
    ppermute x9, waiting for transfers between devices, body(): lax.ppermute(value, axis, [(i, i ^ k + 1) for i in range(4)])  22.7 us
    all_to_all x3, starting transfers between devices, exchanged(): return lax.all_to_all(blocks, axes, 0, 0, tiled=True).reshape(rows, width)  16.9 us
    all_to_all x1, blocking collectives, exchanged(): return lax.all_to_all(blocks, axes, 0, 0, tiled=True).reshape(rows, width)  15.9 us
    ppermute x9, starting transfers between devices, body(): lax.ppermute(value, axis, [(i, i ^ k + 1) for i in range(4)])  14.5 us
    all_to_all x3, waiting for transfers between devices, exchanged(): return lax.all_to_all(blocks, axes, 0, 0, tiled=True).reshape(rows, width)  13.3 us
  transfers between devices with their start and end apart: 15, of which 12 were waited for; matrix products, arithmetic and copies ran while one was open for 4% of the time, Pallas kernels for 4%

profile of v2, /device:TPU:0, one launch (start us, length us, event | category | flops | bytes accessed | tf_op | source)
XLA Modules:
  0.0 197.2 jit_solution(10085694782294292529)
XLA Ops:
  0.7 1.2 copy-done.3
  2.5 2.1 %shard_map.94 = bf16[512,2560]{1,0:T(8,128)(2,1)S(1)} custom-call(s32[4,128]{1,0:T(4,128)S(1)} %bitcast.51, bf16[128,2048]{1,0:T(8,128)(2,1)S(1)} %copy-done.3), custom_call_target="tpu_custom_call" | custom-call | flops 536870912 | bytes 3145728 | tf_op jit(solution)/shard_map/pallas_call | solution.py:319
  4.7 1.5 copy-done.1
  6.2 7.6 %all-to-all-start = ((bf16[32,16,2560]{2,1,0:T(8,128)(2,1)}), bf16[32,16,2560]{2,1,0:T(8,128)(2,1)}, u32[]{:S(2)}, u32[]{:S(2)}) async-start(bf16[32,16,2560]{2,1,0:T(8,128)(2,1)} %bitcast.34), calls=%async_computation | async-start | bytes 5242880 | tf_op jit(solution)/shard_map/all_to_all | solution.py:333
  13.9 3.3 %collective-permute-start = (bf16[1,128]{1,0:T(2,128)(2,1)S(1)}, bf16[1,128]{1,0:T(2,128)(2,1)S(1)}, u32[]{:S(2)}, u32[]{:S(2)}) collective-permute-start(bf16[1,128]{1,0:T(2,128)(2,1)S(1)} %convert_element_type.15), channel_id=1, source_target_pairs={{0,16},{1,17},{2,18},{3,19},{4,20},{5,21},{6,22},{7,23},{8,24},{9,... | collective-permute-start | bytes 776 | tf_op jit(solution)/shard_map/ppermute | solution.py:354
  17.2 6.9 %convolution_convert_fusion.mixed_ref = bf16[1408,512]{1,0:T(8,128)(2,1)} fusion(bf16[2048,512]{1,0:T(8,128)(2,1)S(1)} %copy-done, bf16[1,1408,2048]{2,1,0:T(8,128)(2,1)} %param.11), kind=kOutput, calls=%fused_computation | convolution fusion | flops 2953510912 | bytes 9306112 | tf_op jit(solution)/shard_map/dot_general | solution.py:35
  24.1 23.0 %collective-permute-done.partner_ref = bf16[1,128]{1,0:T(2,128)(2,1)S(1)} collective-permute-done((bf16[1,128]{1,0:T(2,128)(2,1)S(1)}, bf16[1,128]{1,0:T(2,128)(2,1)S(1)}, u32[]{:S(2)}, u32[]{:S(2)}) %collective-permute-start) | collective-permute-done | bytes 288 | tf_op jit(solution)/shard_map/ppermute | solution.py:354
  47.0 1.4 all-to-all-done
  48.5 4.3 %copy-done.17 = bf16[1,2048,2816]{2,1,0:T(8,128)(2,1)S(1)} copy-done((bf16[1,2048,2816]{2,1,0:T(8,128)(2,1)S(1)}, bf16[1,2048,2816]{2,1,0:T(8,128)(2,1)}, u32[]{:S(2)}) %copy-start.17) | copy-done | bytes 11534360
  52.7 1.4 copy-done.21
  54.1 12.6 %shard_map.95 = (bf16[512,640]{1,0:T(8,128)(2,1)S(1)}, bf16[640,1408]{1,0:T(8,128)(2,1)S(1)}, bf16[640,2816]{1,0:T(8,128)(2,1)S(1)}) custom-call(bf16[512,2560]{1,0:T(8,128)(2,1)} %bitcast.3.recv_hbm, bf16[2048,2816]{1,0:T(8,128)(2,1)S(1)} %bitcast.57, bf16[1408,512]{1,0:T(8,128)(2,1)S(1)} %copy-done.21), custom_call_target="tpu_custom_call" | custom-call | flops 8304721920 | bytes 23068672 | tf_op jit(solution)/shard_map/pallas_call | solution.py:319
  66.7 1.2 copy-done.8
  67.9 0.9 copy-done.10
  68.8 1.8 copy-done.19
  70.7 4.2 %all-to-all-start.1 = ((bf16[32,16,640]{2,1,0:T(8,128)(2,1)}), bf16[32,16,640]{2,1,0:T(8,128)(2,1)S(1)}, u32[]{:S(2)}, u32[]{:S(2)}) async-start(bf16[32,16,640]{2,1,0:T(8,128)(2,1)} %bitcast.40), calls=%async_computation.1 | async-start | bytes 1310720 | tf_op jit(solution)/shard_map/all_to_all | solution.py:333
  75.4 11.9 %all-to-all-done.1 = bf16[32,16,640]{2,1,0:T(8,128)(2,1)S(1)} async-done(((bf16[32,16,640]{2,1,0:T(8,128)(2,1)}), bf16[32,16,640]{2,1,0:T(8,128)(2,1)S(1)}, u32[]{:S(2)}, u32[]{:S(2)}) %all-to-all-start.1) | async-done | bytes 655392 | tf_op jit(solution)/shard_map/all_to_all | solution.py:333
  87.2 0.9 shard_map.96
  88.1 1.8 collective-permute-start.1
  89.9 5.9 %collective-permute-done.1.key_ref = bf16[128,512]{1,0:T(8,128)(2,1)S(1)} collective-permute-done((bf16[128,512]{1,0:T(8,128)(2,1)S(1)}, bf16[128,512]{1,0:T(8,128)(2,1)S(1)}, u32[]{:S(2)}, u32[]{:S(2)}) %collective-permute-start.1) | collective-permute-done | bytes 131104 | tf_op jit(solution)/shard_map/ppermute | solution.py:382
  95.8 1.1 shard_map.97
  96.9 15.9 %all_to_all.20 = bf16[32,16,640]{2,1,0:T(8,128)(2,1)S(1)} all-to-all(bf16[32,16,640]{2,1,0:T(8,128)(2,1)S(1)} %bitcast.41), channel_id=1, replica_groups=mesh['dp'=4,'expert_0'=4,'expert_1'=4,'expert_2'=2] {'expert_0','expert_..., dimensions={0} | all-to-all | bytes 1310720 | tf_op jit(solution)/shard_map/all_to_all | solution.py:333
  112.9 4.3 %copy-done.18 = bf16[1,2048,2816]{2,1,0:T(8,128)(2,1)S(1)} copy-done((bf16[1,2048,2816]{2,1,0:T(8,128)(2,1)S(1)}, bf16[1,2048,2816]{2,1,0:T(8,128)(2,1)}, u32[]{:S(2)}) %copy-start.18) | copy-done | bytes 11534360
  117.1 2.0 %copy-done.20 = bf16[640,2816]{1,0:T(8,128)(2,1)S(1)} copy-done((bf16[640,2816]{1,0:T(8,128)(2,1)S(1)}, bf16[640,2816]{1,0:T(8,128)(2,1)}, u32[]{:S(2)}) %copy-start.20) | copy-done | bytes 3604504
  119.2 10.2 %shard_map.98 = (bf16[512,2560]{1,0:T(8,128)(2,1)S(1)}, bf16[640,512]{1,0:T(8,128)(2,1)S(1)}) custom-call(bf16[512,640]{1,0:T(8,128)(2,1)S(1)} %bitcast.42, bf16[1408,512]{1,0:T(8,128)(2,1)S(1)} %copy-done.22, bf16[640,2816]{1,0:T(8,128)(2,1)S(1)} %copy-done.20, bf16[2048,2816]{1,0:T(8,128)(2,1)S(1)} %bitcast.58), custom_call_target="tpu_custom_call" | custom-call | flops 8304721920 | bytes 23068672 | tf_op jit(solution)/shard_map/pallas_call | solution.py:319
  129.3 1.5 copy-done.5
  130.8 5.0 %all-to-all-start.3 = ((bf16[32,16,2560]{2,1,0:T(8,128)(2,1)}), bf16[32,16,2560]{2,1,0:T(8,128)(2,1)}, u32[]{:S(2)}, u32[]{:S(2)}) async-start(bf16[32,16,2560]{2,1,0:T(8,128)(2,1)} %bitcast.36), calls=%async_computation.3 | async-start | bytes 5242880 | tf_op jit(solution)/shard_map/all_to_all | solution.py:333
  135.9 2.6 %copy-done.2 = bf16[1,1408,2048]{2,1,0:T(8,128)(2,1)S(1)} copy-done((bf16[1,1408,2048]{2,1,0:T(8,128)(2,1)S(1)}, bf16[1,1408,2048]{2,1,0:T(8,128)(2,1)}, u32[]{:S(2)}) %copy-start.2) | copy-done | bytes 5767192
  138.5 1.5 copy-done.9
  140.0 6.1 %shard_map.100 = (f32[1024,512]{1,0:T(8,128)S(1)}, bf16[1024,512]{1,0:T(8,128)(2,1)}) custom-call(s32[1]{0:T(128)} %bitcast.15.core_ref, bf16[640,1408]{1,0:T(8,128)(2,1)S(1)} %copy-done.9, bf16[640,512]{1,0:T(8,128)(2,1)S(1)} %get-tuple-element.39.grads_ref, bf16[128,2048]{1,0:T(8,128)(2,1)S(1)} %copy-done.4, ...), custom_call_target="tpu_custom_call" | custom-call | tf_op jit(solution)/shard_map/pallas_call | solution.py:319
  146.2 1.3 copy-done.6
  147.9 2.5 %collective-permute-done.2 = bf16[1024,512]{1,0:T(8,128)(2,1)S(1)} collective-permute-done((bf16[1024,512]{1,0:T(8,128)(2,1)}, bf16[1024,512]{1,0:T(8,128)(2,1)S(1)}, u32[]{:S(2)}, u32[]{:S(2)}) %collective-permute-start.2) | collective-permute-done | bytes 1048608 | tf_op jit(solution)/shard_map/ppermute | solution.py:416
  150.4 1.6 copy-done.7
  152.0 1.0 shard_map.101
  153.8 1.9 collective-permute-start.3
  155.8 3.6 %collective-permute-start.4 = (bf16[256,512]{1,0:T(8,128)(2,1)}, bf16[256,512]{1,0:T(8,128)(2,1)S(1)}, u32[]{:S(2)}, u32[]{:S(2)}) collective-permute-start(bf16[256,512]{1,0:T(8,128)(2,1)} %get-tuple-element.44), channel_id=1, source_target_pairs={{0,64},{32,96},{64,0},{96,32},{1,65},{33,97},{65,1},{97,33},{2,66}... | collective-permute-start | bytes 786440 | tf_op jit(solution)/shard_map/ppermute | solution.py:426
  159.3 3.8 %collective-permute-done.3 = bf16[256,512]{1,0:T(8,128)(2,1)S(1)} collective-permute-done((bf16[256,512]{1,0:T(8,128)(2,1)}, bf16[256,512]{1,0:T(8,128)(2,1)S(1)}, u32[]{:S(2)}, u32[]{:S(2)}) %collective-permute-start.3) | collective-permute-done | bytes 262176 | tf_op jit(solution)/shard_map/ppermute | solution.py:426
  163.2 8.7 %collective-permute-done.4 = bf16[256,512]{1,0:T(8,128)(2,1)S(1)} collective-permute-done((bf16[256,512]{1,0:T(8,128)(2,1)}, bf16[256,512]{1,0:T(8,128)(2,1)S(1)}, u32[]{:S(2)}, u32[]{:S(2)}) %collective-permute-start.4) | collective-permute-done | bytes 262176 | tf_op jit(solution)/shard_map/ppermute | solution.py:426
  171.8 2.6 %collective-permute-done.5 = bf16[256,512]{1,0:T(8,128)(2,1)S(1)} collective-permute-done((bf16[256,512]{1,0:T(8,128)(2,1)}, bf16[256,512]{1,0:T(8,128)(2,1)S(1)}, u32[]{:S(2)}, u32[]{:S(2)}) %collective-permute-start.5) | collective-permute-done | bytes 262176 | tf_op jit(solution)/shard_map/ppermute | solution.py:426
  174.4 1.0 copy-done.12
  175.6 1.2 collective-permute-start.6
  176.8 2.8 %collective-permute-start.7 = (bf16[64,512]{1,0:T(8,128)(2,1)S(1)}, bf16[64,512]{1,0:T(8,128)(2,1)S(1)}, u32[]{:S(2)}, u32[]{:S(2)}) collective-permute-start(bf16[64,512]{1,0:T(8,128)(2,1)S(1)} %get-tuple-element.48), channel_id=1, source_target_pairs={{0,16},{8,24},{16,0},{24,8},{1,17},{9,25},{17,1},{25,9},{2,18},{10... | collective-permute-start | bytes 196616 | tf_op jit(solution)/shard_map/ppermute | solution.py:426
  180.3 2.3 %collective-permute-done.7 = bf16[64,512]{1,0:T(8,128)(2,1)S(1)} collective-permute-done((bf16[64,512]{1,0:T(8,128)(2,1)S(1)}, bf16[64,512]{1,0:T(8,128)(2,1)S(1)}, u32[]{:S(2)}, u32[]{:S(2)}) %collective-permute-start.7) | collective-permute-done | bytes 65568 | tf_op jit(solution)/shard_map/ppermute | solution.py:426
  182.6 2.4 %collective-permute-done.8 = bf16[64,512]{1,0:T(8,128)(2,1)S(1)} collective-permute-done((bf16[64,512]{1,0:T(8,128)(2,1)S(1)}, bf16[64,512]{1,0:T(8,128)(2,1)S(1)}, u32[]{:S(2)}, u32[]{:S(2)}) %collective-permute-start.8) | collective-permute-done | bytes 65568 | tf_op jit(solution)/shard_map/ppermute | solution.py:426
  185.1 3.1 %collective-permute-start.10 = (bf16[16,512]{1,0:T(8,128)(2,1)S(1)}, bf16[16,512]{1,0:T(8,128)(2,1)S(1)}, u32[]{:S(2)}, u32[]{:S(2)}) collective-permute-start(bf16[16,512]{1,0:T(8,128)(2,1)S(1)} %get-tuple-element.52), channel_id=1, source_target_pairs={{0,4},{2,6},{4,0},{6,2},{1,5},{3,7},{5,1},{7,3},{8,12},{10,14},{12... | collective-permute-start | bytes 49160 | tf_op jit(solution)/shard_map/ppermute | solution.py:426
  188.1 1.2 collective-permute-start.11
  189.3 0.8 fusion.2.direct_ref
  190.4 2.7 %collective-permute-done.11 = bf16[16,512]{1,0:T(8,128)(2,1)S(1)} collective-permute-done((bf16[16,512]{1,0:T(8,128)(2,1)S(1)}, bf16[16,512]{1,0:T(8,128)(2,1)S(1)}, u32[]{:S(2)}, u32[]{:S(2)}) %collective-permute-start.11) | collective-permute-done | bytes 16416 | tf_op jit(solution)/shard_map/ppermute | solution.py:426
  193.7 3.5 %shard_map.99 = bf16[128,2048]{1,0:T(8,128)(2,1)} custom-call(s32[4,128]{1,0:T(4,128)S(1)} %bitcast.54, bf16[512,2560]{1,0:T(8,128)(2,1)} %bitcast.11.back_ref, f32[128,2048]{1,0:T(8,128)S(1)} %fusion.2.direct_ref), custom_call_target="tpu_custom_call" | custom-call | flops 536870912 | bytes 4194304 | tf_op jit(solution)/shard_map/pallas_call | solution.py:319
  (44 shorter events, 4.3 us)
Async XLA Ops:
  0.6 16.5 %copy-start = (bf16[2048,512]{1,0:T(8,128)(2,1)S(1)}, bf16[2048,512]{1,0:T(8,128)(2,1)}, u32[]{:S(2)}) copy-start(bf16[2048,512]{1,0:T(8,128)(2,1)} %param.12) | copy-start | bytes 6291460
  0.6 1.2 copy-start.3
  1.8 0.7 copy-start.13
  4.7 1.5 copy-start.1
  6.2 7.7 %copy-start.16 = (s32[1,128]{1,0:T(1,128)S(1)}, s32[1,128]{1,0:T(1,128)}, u32[]{:S(2)}) copy-start(s32[1,128]{1,0:T(1,128)} %matches_ref.1) | copy-start | bytes 1540
  6.2 42.3 %all-to-all-start = ((bf16[32,16,2560]{2,1,0:T(8,128)(2,1)}), bf16[32,16,2560]{2,1,0:T(8,128)(2,1)}, u32[]{:S(2)}, u32[]{:S(2)}) async-start(bf16[32,16,2560]{2,1,0:T(8,128)(2,1)} %bitcast.34), calls=%async_computation | async-start | bytes 5242880 | tf_op jit(solution)/shard_map/all_to_all | solution.py:333
  13.9 33.2 %collective-permute-start = (bf16[1,128]{1,0:T(2,128)(2,1)S(1)}, bf16[1,128]{1,0:T(2,128)(2,1)S(1)}, u32[]{:S(2)}, u32[]{:S(2)}) collective-permute-start(bf16[1,128]{1,0:T(2,128)(2,1)S(1)} %convert_element_type.15), channel_id=1, source_target_pairs={{0,16},{1,17},{2,18},{3,19},{4,20},{5,21},{6,22},{7,23},{8,24},{9,... | collective-permute-start | bytes 776 | tf_op jit(solution)/shard_map/ppermute | solution.py:354
  48.5 4.3 %copy-start.17 = (bf16[1,2048,2816]{2,1,0:T(8,128)(2,1)S(1)}, bf16[1,2048,2816]{2,1,0:T(8,128)(2,1)}, u32[]{:S(2)}) copy-start(bf16[1,2048,2816]{2,1,0:T(8,128)(2,1)} %param.10) | copy-start | bytes 34603012
  52.7 1.4 copy-start.21
  54.1 20.8 %copy-start.4 = (bf16[128,2048]{1,0:T(8,128)(2,1)S(1)}, bf16[128,2048]{1,0:T(8,128)(2,1)}, u32[]{:S(2)}) copy-start(bf16[128,2048]{1,0:T(8,128)(2,1)} %tokens_ref.1) | copy-start | bytes 1572868
  66.7 1.2 copy-start.8
  67.9 0.9 copy-start.10
  68.8 1.8 copy-start.19
  70.7 16.5 %copy-start.14 = (s32[128,4]{0,1:T(4,128)S(1)}, s32[128,4]{0,1:T(4,128)}, u32[]{:S(2)}) copy-start(s32[128,4]{0,1:T(4,128)} %param.8) | copy-start | bytes 6148
  70.7 16.5 %copy-start.15 = (f32[128,4]{0,1:T(4,128)S(1)}, f32[128,4]{0,1:T(4,128)}, u32[]{:S(2)}) copy-start(f32[128,4]{0,1:T(4,128)} %param.9) | copy-start | bytes 6148
  70.7 16.5 %all-to-all-start.1 = ((bf16[32,16,640]{2,1,0:T(8,128)(2,1)}), bf16[32,16,640]{2,1,0:T(8,128)(2,1)S(1)}, u32[]{:S(2)}, u32[]{:S(2)}) async-start(bf16[32,16,640]{2,1,0:T(8,128)(2,1)} %bitcast.40), calls=%async_computation.1 | async-start | bytes 1310720 | tf_op jit(solution)/shard_map/all_to_all | solution.py:333
  87.2 25.6 %copy-start.22 = (bf16[1408,512]{1,0:T(8,128)(2,1)S(1)}, bf16[1408,512]{1,0:T(8,128)(2,1)}, u32[]{:S(2)}) copy-start(bf16[1408,512]{1,0:T(8,128)(2,1)} %convolution_convert_fusion.mixed_ref) | copy-start | bytes 4325380
  88.1 7.7 %collective-permute-start.1 = (bf16[128,512]{1,0:T(8,128)(2,1)S(1)}, bf16[128,512]{1,0:T(8,128)(2,1)S(1)}, u32[]{:S(2)}, u32[]{:S(2)}) collective-permute-start(bf16[128,512]{1,0:T(8,128)(2,1)S(1)} %get-tuple-element.33.unit_ref), channel_id=1, source_target_pairs={{0,16},{1,17},{2,18},{3,19},{4,20},{5,21},{6,22},{7,23},{8,24},{9,... | collective-permute-start | bytes 393224 | tf_op jit(solution)/shard_map/ppermute | solution.py:382
  112.9 4.3 %copy-start.18 = (bf16[1,2048,2816]{2,1,0:T(8,128)(2,1)S(1)}, bf16[1,2048,2816]{2,1,0:T(8,128)(2,1)}, u32[]{:S(2)}) copy-start(bf16[1,2048,2816]{2,1,0:T(8,128)(2,1)} %param.10) | copy-start | bytes 34603012
  117.1 2.0 %copy-start.20 = (bf16[640,2816]{1,0:T(8,128)(2,1)S(1)}, bf16[640,2816]{1,0:T(8,128)(2,1)}, u32[]{:S(2)}) copy-start(bf16[640,2816]{1,0:T(8,128)(2,1)} %copy-done.19) | copy-start | bytes 10813444
  129.3 1.5 copy-start.5
  130.8 62.9 %all-to-all-start.3 = ((bf16[32,16,2560]{2,1,0:T(8,128)(2,1)}), bf16[32,16,2560]{2,1,0:T(8,128)(2,1)}, u32[]{:S(2)}, u32[]{:S(2)}) async-start(bf16[32,16,2560]{2,1,0:T(8,128)(2,1)} %bitcast.36), calls=%async_computation.3 | async-start | bytes 5242880 | tf_op jit(solution)/shard_map/all_to_all | solution.py:333
  135.9 2.6 %copy-start.2 = (bf16[1,1408,2048]{2,1,0:T(8,128)(2,1)S(1)}, bf16[1,1408,2048]{2,1,0:T(8,128)(2,1)}, u32[]{:S(2)}) copy-start(bf16[1,1408,2048]{2,1,0:T(8,128)(2,1)} %param.11) | copy-start | bytes 17301508
  138.5 1.5 copy-start.9
  146.2 1.3 copy-start.6
  147.5 3.0 %collective-permute-start.2 = (bf16[1024,512]{1,0:T(8,128)(2,1)}, bf16[1024,512]{1,0:T(8,128)(2,1)S(1)}, u32[]{:S(2)}, u32[]{:S(2)}) collective-permute-start(bf16[1024,512]{1,0:T(8,128)(2,1)} %get-tuple-element.41), channel_id=1, source_target_pairs={{0,1},{1,0},{2,3},{3,2},{4,5},{5,4},{6,7},{7,6},{8,9},{9,8},{10,11... | collective-permute-start | bytes 3145736 | tf_op jit(solution)/shard_map/ppermute | solution.py:416
  150.4 1.6 copy-start.7
  153.0 0.8 copy-start.11
  153.8 9.3 %collective-permute-start.3 = (bf16[256,512]{1,0:T(8,128)(2,1)}, bf16[256,512]{1,0:T(8,128)(2,1)S(1)}, u32[]{:S(2)}, u32[]{:S(2)}) collective-permute-start(bf16[256,512]{1,0:T(8,128)(2,1)} %get-tuple-element.43), channel_id=1, source_target_pairs={{0,32},{32,0},{64,96},{96,64},{1,33},{33,1},{65,97},{97,65},{2,34}... | collective-permute-start | bytes 786440 | tf_op jit(solution)/shard_map/ppermute | solution.py:426
  155.8 16.1 %collective-permute-start.4 = (bf16[256,512]{1,0:T(8,128)(2,1)}, bf16[256,512]{1,0:T(8,128)(2,1)S(1)}, u32[]{:S(2)}, u32[]{:S(2)}) collective-permute-start(bf16[256,512]{1,0:T(8,128)(2,1)} %get-tuple-element.44), channel_id=1, source_target_pairs={{0,64},{32,96},{64,0},{96,32},{1,65},{33,97},{65,1},{97,33},{2,66}... | collective-permute-start | bytes 786440 | tf_op jit(solution)/shard_map/ppermute | solution.py:426
  159.3 15.0 %collective-permute-start.5 = (bf16[256,512]{1,0:T(8,128)(2,1)}, bf16[256,512]{1,0:T(8,128)(2,1)S(1)}, u32[]{:S(2)}, u32[]{:S(2)}) collective-permute-start(bf16[256,512]{1,0:T(8,128)(2,1)} %get-tuple-element.45), channel_id=1, source_target_pairs={{0,96},{32,64},{64,32},{96,0},{1,97},{33,65},{65,33},{97,1},{2,98}... | collective-permute-start | bytes 786440 | tf_op jit(solution)/shard_map/ppermute | solution.py:426
  174.4 1.0 copy-start.12
  175.6 4.8 %collective-permute-start.6 = (bf16[64,512]{1,0:T(8,128)(2,1)S(1)}, bf16[64,512]{1,0:T(8,128)(2,1)S(1)}, u32[]{:S(2)}, u32[]{:S(2)}) collective-permute-start(bf16[64,512]{1,0:T(8,128)(2,1)S(1)} %get-tuple-element.47), channel_id=1, source_target_pairs={{0,8},{8,0},{16,24},{24,16},{1,9},{9,1},{17,25},{25,17},{2,10},{10... | collective-permute-start | bytes 196616 | tf_op jit(solution)/shard_map/ppermute | solution.py:426
  176.8 5.9 %collective-permute-start.7 = (bf16[64,512]{1,0:T(8,128)(2,1)S(1)}, bf16[64,512]{1,0:T(8,128)(2,1)S(1)}, u32[]{:S(2)}, u32[]{:S(2)}) collective-permute-start(bf16[64,512]{1,0:T(8,128)(2,1)S(1)} %get-tuple-element.48), channel_id=1, source_target_pairs={{0,16},{8,24},{16,0},{24,8},{1,17},{9,25},{17,1},{25,9},{2,18},{10... | collective-permute-start | bytes 196616 | tf_op jit(solution)/shard_map/ppermute | solution.py:426
  179.5 5.5 %collective-permute-start.8 = (bf16[64,512]{1,0:T(8,128)(2,1)S(1)}, bf16[64,512]{1,0:T(8,128)(2,1)S(1)}, u32[]{:S(2)}, u32[]{:S(2)}) collective-permute-start(bf16[64,512]{1,0:T(8,128)(2,1)S(1)} %get-tuple-element.49), channel_id=1, source_target_pairs={{0,24},{8,16},{16,8},{24,0},{1,25},{9,17},{17,9},{25,1},{2,26},{10... | collective-permute-start | bytes 196616 | tf_op jit(solution)/shard_map/ppermute | solution.py:426
  185.1 5.3 %collective-permute-start.10 = (bf16[16,512]{1,0:T(8,128)(2,1)S(1)}, bf16[16,512]{1,0:T(8,128)(2,1)S(1)}, u32[]{:S(2)}, u32[]{:S(2)}) collective-permute-start(bf16[16,512]{1,0:T(8,128)(2,1)S(1)} %get-tuple-element.52), channel_id=1, source_target_pairs={{0,4},{2,6},{4,0},{6,2},{1,5},{3,7},{5,1},{7,3},{8,12},{10,14},{12... | collective-permute-start | bytes 49160 | tf_op jit(solution)/shard_map/ppermute | solution.py:426
  188.1 4.9 %collective-permute-start.11 = (bf16[16,512]{1,0:T(8,128)(2,1)S(1)}, bf16[16,512]{1,0:T(8,128)(2,1)S(1)}, u32[]{:S(2)}, u32[]{:S(2)}) collective-permute-start(bf16[16,512]{1,0:T(8,128)(2,1)S(1)} %get-tuple-element.53), channel_id=1, source_target_pairs={{0,6},{2,4},{4,2},{6,0},{1,7},{3,5},{5,3},{7,1},{8,14},{10,12},{12... | collective-permute-start | bytes 49160 | tf_op jit(solution)/shard_map/ppermute | solution.py:426
  189.3 3.8 %collective-permute-start.9 = (bf16[16,512]{1,0:T(8,128)(2,1)S(1)}, bf16[16,512]{1,0:T(8,128)(2,1)S(1)}, u32[]{:S(2)}, u32[]{:S(2)}) collective-permute-start(bf16[16,512]{1,0:T(8,128)(2,1)S(1)} %get-tuple-element.51), channel_id=1, source_target_pairs={{0,2},{2,0},{4,6},{6,4},{1,3},{3,1},{5,7},{7,5},{8,10},{10,8},{12,... | collective-permute-start | bytes 49160 | tf_op jit(solution)/shard_map/ppermute | solution.py:426

commit v3 on v2

--- a/solution.py
+++ b/solution.py
@@ -1,3 +1,4 @@
+import functools
 import math
 
 import jax
@@ -28,7 +29,7 @@
 TILE = 256
 F32 = jnp.float32
 BF16 = jnp.bfloat16
-VMEM_LIMIT = 24 * 1024 * 1024
+WHOLE = 60
 
 
 def dot(left, right):
@@ -122,26 +123,61 @@
         copy.wait()
 
 
+def prepare_kernel(down_hbm, head_hbm, tokens_hbm, mixed_ref, base_ref, down_ref, head_ref, tokens_ref, sems):
+    copies = [
+        pltpu.make_async_copy(source, target, sems.at[i])
+        for i, (source, target) in enumerate(
+            ((head_hbm, head_ref), (tokens_hbm, tokens_ref), (down_hbm, down_ref))
+        )
+    ]
+    for copy in copies:
+        copy.start()
+    copies[0].wait()
+    copies[1].wait()
+    base_ref[...] = dot(tokens_ref[...], head_ref[...])
+    copies[2].wait()
+    mixed_ref[...] = dot(down_ref[...], head_ref[...]).astype(BF16)
+
+
 def forward_kernel(
-    recv_hbm, w_ref, mixed_ref, out_hbm, hidden_ref, slopes_ref,
-    x_ref, extra_ref, act_ref, out_ref, sems, out_sems,
+    recv_hbm, w_hbm, mixed_hbm, out_hbm, hidden_hbm, slopes_hbm,
+    x_ref, extra_ref, act_ref, w_ref, mixed_ref, hidden_ref, slopes_ref, out_ref, sems, out_sems,
 ):
     quarter = WIDTH // 4
-    extra_copy = pltpu.make_async_copy(recv_hbm.at[:, pl.ds(WIDTH, quarter)], extra_ref, sems.at[0])
-    extra_copy.start()
-    main_copy = pltpu.make_async_copy(
-        recv_hbm.at[:, pl.ds(0, WIDTH)], x_ref.at[pl.ds(0, SLOTS), :], sems.at[1]
-    )
-    main_copy.start()
+
+    def bring(source, target, index):
+        copy = pltpu.make_async_copy(source, target, sems.at[index])
+        copy.start()
+        return copy
+
+    extra_copy = bring(recv_hbm.at[:, pl.ds(WIDTH, quarter)], extra_ref, 0)
+    main_copy = bring(recv_hbm.at[:, pl.ds(0, WIDTH)], x_ref.at[pl.ds(0, SLOTS), :], 1)
+    weight_copies = []
+    for c, (lo, hi) in enumerate(CHUNKS):
+        for h in range(2):
+            cols = pl.ds(h * HIDDEN + lo, hi - lo)
+            weight_copies.append(bring(w_hbm.at[:, cols], w_ref.at[:, cols], 3 + 2 * c + h))
+    mixed_copy = bring(mixed_hbm, mixed_ref, 2)
     turned = unpacker()
     extra_copy.wait()
     spread = dot(turned, extra_ref[...]).astype(BF16)
     for j in range(4):
         x_ref[SLOTS:, j * quarter : (j + 1) * quarter] = spread[j * SPARE : (j + 1) * SPARE]
     main_copy.wait()
+    outgoing = []
+
+    def send(source, target, lo, wide):
+        cols = pl.ds(lo, wide)
+        copy = pltpu.make_async_copy(source.at[:, cols], target.at[:, cols], out_sems.at[len(outgoing)])
+        copy.start()
+        outgoing.append(copy)
+
+    sent = 0
     for c, (lo, hi) in enumerate(CHUNKS):
         slot = c % 2
         wide = hi - lo
+        weight_copies[2 * c].wait()
+        weight_copies[2 * c + 1].wait()
         act_ref[slot, 0, :, :wide] = dot(x_ref[...], w_ref[:, lo:hi])
         act_ref[slot, 1, :, :wide] = dot(x_ref[...], w_ref[:, HIDDEN + lo : HIDDEN + hi])
         for m in range(0, TOTAL, 64):
@@ -152,21 +188,23 @@
             hidden_ref[m : m + 64, lo:hi] = (silu * up).astype(BF16)
             slopes_ref[m : m + 64, HIDDEN + lo : HIDDEN + hi] = silu.astype(BF16)
             slopes_ref[m : m + 64, lo:hi] = (up * sigmoid * (1.0 + gate * (1.0 - sigmoid))).astype(BF16)
+        if c % 3 == 2:
+            send(hidden_ref, hidden_hbm, sent, hi - sent)
+            send(slopes_ref, slopes_hbm, sent, hi - sent)
+            send(slopes_ref, slopes_hbm, HIDDEN + sent, hi - sent)
+            sent = hi
+    mixed_copy.wait()
     projected = dot(hidden_ref[...], mixed_ref[...]).astype(BF16)
     out_ref[:, :EMBED] = projected[:SLOTS]
-    cols = pl.ds(0, EMBED)
-    first = pltpu.make_async_copy(out_ref.at[:, cols], out_hbm.at[:, cols], out_sems.at[0])
-    first.start()
+    send(out_ref, out_hbm, 0, EMBED)
     quarter = EMBED // 4
     stacked = jnp.concatenate(
         [projected[SLOTS:, j * quarter : (j + 1) * quarter] for j in range(4)], axis=0
     )
     out_ref[:, EMBED:] = dot(packer(), stacked).astype(BF16)
-    cols = pl.ds(EMBED, quarter)
-    second = pltpu.make_async_copy(out_ref.at[:, cols], out_hbm.at[:, cols], out_sems.at[1])
-    second.start()
-    first.wait()
-    second.wait()
+    send(out_ref, out_hbm, EMBED, quarter)
+    for copy in outgoing:
+        copy.wait()
 
 
 def weighted(chosen, gates):
@@ -233,52 +271,30 @@
     out_ref[:, EMBED:] = (extra_gates * total).astype(BF16)
 
 
-def backward_kernel(
-    arrived_ref, mixed_ref, slopes_ref, w_ref, out_hbm, grads_ref,
-    act_ref, joined_ref, extra_ref, out_ref, out_sems,
+def head_kernel(
+    arrived_ref, tokens_ref, embed_grad_ref, hidden_hbm, down_hbm, grads_ref, own_hbm, other_hbm,
+    hidden_ref, down_ref, own_ref, other_ref, sems, out_sems,
 ):
+    hidden_copy = pltpu.make_async_copy(hidden_hbm, hidden_ref, sems.at[0])
+    hidden_copy.start()
+    step = WIDTH // 4
+    down_copies = []
+    for i in range(4):
+        cols = pl.ds(i * step, step)
+        copy = pltpu.make_async_copy(down_hbm.at[:, cols], down_ref.at[:, cols], sems.at[1 + i])
+        copy.start()
+        down_copies.append(copy)
     quarter = EMBED // 4
     grads_ref[:SLOTS, :] = arrived_ref[:, :EMBED]
     spread = dot(unpacker(), arrived_ref[:, EMBED:]).astype(BF16)
     for j in range(4):
         grads_ref[SLOTS:, j * quarter : (j + 1) * quarter] = spread[j * SPARE : (j + 1) * SPARE]
-    for c, (lo, hi) in enumerate(CHUNKS):
-        slot = c % 2
-        wide = hi - lo
-        act_ref[slot, :, :wide] = dot_cols(grads_ref[...], mixed_ref[lo:hi, :])
-        for m in range(0, TOTAL, 64):
-            hidden_grad = act_ref[slot, m : m + 64, :wide]
-            for offset in (0, HIDDEN):
-                slope = slopes_ref[m : m + 64, offset + lo : offset + hi].astype(F32)
-                joined_ref[m : m + 64, offset + lo : offset + hi] = (hidden_grad * slope).astype(BF16)
-    outgoing = []
-    quarter = WIDTH // 4
-
-    def send(start, wide, index):
-        cols = pl.ds(start, wide)
-        copy = pltpu.make_async_copy(out_ref.at[:, cols], out_hbm.at[:, cols], out_sems.at[index])
-        copy.start()
-        outgoing.append(copy)
-
-    for n in range(0, WIDTH, TILE):
-        result = dot_cols(joined_ref[...], w_ref[n : n + TILE, :]).astype(BF16)
-        out_ref[:, n : n + TILE] = result[:SLOTS]
-        j, within = n // quarter, n % quarter
-        extra_ref[j * SPARE : (j + 1) * SPARE, within : within + TILE] = result[SLOTS:]
-        if n % quarter:
-            send(j * quarter, quarter, j)
-    out_ref[:, WIDTH:] = dot(packer(), extra_ref[...]).astype(BF16)
-    send(WIDTH, quarter, 4)
-    for copy in outgoing:
-        copy.wait()
-
-
-def head_kernel(
-    core_ref, hidden_ref, grads_ref, tokens_ref, embed_grad_ref, down_ref, own_ref, other_ref
-):
-    first = core_ref[0] == 0
+    first = lax.axis_index("expert_2") == 0
+    hidden_copy.wait()
     inner = dot_rows(hidden_ref[...], grads_ref[...]).astype(BF16)
     for n in range(0, WIDTH, TILE):
+        if n % step == 0:
+            down_copies[n // step].wait()
         part = dot_rows(down_ref[:, n : n + TILE], inner)
         part = part + dot_rows(tokens_ref[:, n : n + TILE], embed_grad_ref[...])
         for b in range(TILE // 32):
@@ -286,33 +302,120 @@
             even, odd = part[32 * b : 32 * b + 16], part[32 * b + 16 : 32 * b + 32]
             own_ref[row : row + 16, :] = jnp.where(first, even, odd)
             other_ref[row : row + 16, :] = jnp.where(first, odd, even).astype(BF16)
-
-
-def share_kernel(place_ref, own_ref, *refs):
-    received, (kept_ref, *sent_refs) = refs[: len(refs) - 4], refs[len(refs) - 4 :]
-    place = place_ref[0]
-    for k in range(4):
+    other_copy = pltpu.make_async_copy(other_ref, other_hbm, out_sems.at[0])
+    own_copy = pltpu.make_async_copy(own_ref, own_hbm, out_sems.at[1])
+    other_copy.start()
+    own_copy.start()
+    other_copy.wait()
+    own_copy.wait()
+
+
+def joined_kernel(grads_ref, mixed_hbm, slopes_hbm, joined_ref, mixed_ref, slopes_ref, act_ref, sems):
+    def bring(source, target, index):
+        copy = pltpu.make_async_copy(source, target, sems.at[index])
+        copy.start()
+        return copy
+
+    mixed_copy = bring(mixed_hbm, mixed_ref, 0)
+    slopes_copies = []
+    for c, (lo, hi) in enumerate(CHUNKS):
+        for h in range(2):
+            cols = pl.ds(h * HIDDEN + lo, hi - lo)
+            slopes_copies.append(bring(slopes_hbm.at[:, cols], slopes_ref.at[:, cols], 1 + 2 * c + h))
+    mixed_copy.wait()
+    for c, (lo, hi) in enumerate(CHUNKS):
+        slot = c % 2
+        wide = hi - lo
+        act_ref[slot, :, :wide] = dot_cols(grads_ref[...], mixed_ref[lo:hi, :])
+        slopes_copies[2 * c].wait()
+        slopes_copies[2 * c + 1].wait()
+        for m in range(0, TOTAL, 64):
+            hidden_grad = act_ref[slot, m : m + 64, :wide]
+            for offset in (0, HIDDEN):
+                slope = slopes_ref[m : m + 64, offset + lo : offset + hi].astype(F32)
+                joined_ref[m : m + 64, offset + lo : offset + hi] = (hidden_grad * slope).astype(BF16)
+
+
+def input_kernel(joined_ref, w_hbm, _, out_hbm, w_ref, extra_ref, out_ref, sems, out_sems):
+    step = WIDTH // 4
+    weight_copies = []
+    for n in range(0, WIDTH, TILE):
+        rows = pl.ds(n, TILE)
+        copy = pltpu.make_async_copy(w_hbm.at[rows, :], w_ref.at[rows, :], sems.at[n // TILE])
+        copy.start()
+        weight_copies.append(copy)
+    outgoing = []
+
+    def send(start, wide, index):
+        cols = pl.ds(start, wide)
+        copy = pltpu.make_async_copy(out_ref.at[:, cols], out_hbm.at[:, cols], out_sems.at[index])
+        copy.start()
+        outgoing.append(copy)
+
+    for n in range(0, WIDTH, TILE):
+        weight_copies[n // TILE].wait()
+        result = dot_cols(joined_ref[...], w_ref[n : n + TILE, :]).astype(BF16)
+        out_ref[:, n : n + TILE] = result[:SLOTS]
+        j, within = n // step, n % step
+        extra_ref[j * SPARE : (j + 1) * SPARE, within : within + TILE] = result[SLOTS:]
+        if within:
+            send(j * step, step, j)
+    out_ref[:, WIDTH:] = dot(packer(), extra_ref[...]).astype(BF16)
+    send(WIDTH, step, 4)
+    for copy in outgoing:
+        copy.wait()
+
+
+def share_kernel(axis, count, own_hbm, *refs):
+    received_hbm, outs = refs[:count], refs[count : count + 4]
+    own_ref, received_ref, total_ref, sent_ref, sems, out_sems = refs[count + 4 :]
+    copies = [pltpu.make_async_copy(own_hbm, own_ref, sems.at[count])]
+    for k in range(count):
+        copies.append(pltpu.make_async_copy(received_hbm[k], received_ref.at[k], sems.at[k]))
+    for copy in copies:
+        copy.start()
+    for copy in copies:
+        copy.wait()
+    place = lax.axis_index(axis)
+    outgoing = []
+    for k in (2, 1, 3, 0):
         quarter = jnp.bitwise_xor(place, k)
         total = own_ref[quarter]
-        for ref in received:
-            total = total + ref[quarter].astype(F32)
-        if k == 0:
-            kept_ref[...] = total
+        for i in range(count):
+            total = total + received_ref[i, quarter].astype(F32)
+        if k:
+            sent_ref[k - 1] = total.astype(BF16)
+            copy = pltpu.make_async_copy(sent_ref.at[k - 1], outs[k], out_sems.at[k])
         else:
-            sent_refs[k - 1][...] = total.astype(BF16)
-
-
-def combine_kernel(routes_ref, back_ref, direct_ref, out_ref):
+            total_ref[...] = total
+            copy = pltpu.make_async_copy(total_ref, outs[0], out_sems.at[0])
+        copy.start()
+        outgoing.append(copy)
+    for copy in outgoing:
+        copy.wait()
+
+
+def combine_kernel(routes_ref, direct_ref, back_hbm, out_ref, back_ref, sems):
+    quarter = WIDTH // 4
+    copies = []
+    for n, j in enumerate((4, 0, 1, 2, 3)):
+        cols = pl.ds(j * quarter, quarter)
+        copy = pltpu.make_async_copy(back_hbm.at[:, cols], back_ref.at[:, cols], sems.at[n])
+        copy.start()
+        copies.append(copy)
     main, quarters = choosers(routes_ref[...])
-    main = one_hot(main)
-    quarter = WIDTH // 4
+    main = one_hot(main).T
+    quarters = [one_hot(chosen).T for chosen in quarters]
+    copies[0].wait()
     for j in range(4):
         cols = slice(j * quarter, (j + 1) * quarter)
-        total = dot_rows(main, back_ref[:, cols]) + dot_rows(one_hot(quarters[j]), back_ref[:, WIDTH:])
+        extra = dot(quarters[j], back_ref[:, WIDTH:])
+        copies[j + 1].wait()
+        total = dot(main, back_ref[:, cols]) + extra
         out_ref[:, cols] = (direct_ref[:, cols] + total).astype(BF16)
 
 
-def call(kernel, outs, ins, scratch=(), flops=0, moved=0):
+def call(kernel, outs, ins, scratch=(), flops=0, moved=0, limit=24):
     def spec(space):
         return pl.BlockSpec(memory_space=space)
 
@@ -322,7 +425,7 @@
         in_specs=[spec(space) for _, space in ins],
         out_specs=tuple(spec(space) for _, _, space in outs),
         scratch_shapes=scratch,
-        compiler_params=pltpu.CompilerParams(vmem_limit_bytes=VMEM_LIMIT),
+        compiler_params=pltpu.CompilerParams(vmem_limit_bytes=int(limit * 1048576)),
         cost_estimate=pl.CostEstimate(flops=flops, bytes_accessed=moved, transcendentals=0),
     )(*[value for value, _ in ins])
 
@@ -334,43 +437,57 @@
 
 
 def body(tokens, routes, gates, gate_up, down_proj, projection, matches):
-    vmem, hbm, smem = pltpu.VMEM, pltpu.HBM, pltpu.SMEM
+    vmem, hbm = pltpu.VMEM, pl.ANY
     routes, gates = routes.T, gates.T
     weights_joined, weights_down = gate_up[0], down_proj[0]
     partner = [(i, i ^ EXPERTS // 2) for i in range(EXPERTS)]
     dma = pltpu.SemaphoreType.DMA
+    wide_shape, packed_shape = (SLOTS, WIDTH * 5 // 4), (SLOTS, EMBED * 5 // 4)
 
     (dispatch,) = call(
-        dispatch_kernel, [((SLOTS, WIDTH * 5 // 4), BF16, hbm)], [(routes, hbm), (tokens, hbm)],
+        dispatch_kernel, [(wide_shape, BF16, hbm)], [(routes, hbm), (tokens, hbm)],
         scratch=[
             pltpu.VMEM((TOP, ROWS), jnp.int32),
             pltpu.VMEM((ROWS, WIDTH), BF16),
-            pltpu.VMEM((SLOTS, WIDTH * 5 // 4), BF16),
+            pltpu.VMEM(wide_shape, BF16),
             dma((2,)),
             dma((5,)),
         ],
-        flops=2 * SLOTS * ROWS * WIDTH * 2, moved=3 << 20,
+        flops=2 * SLOTS * ROWS * WIDTH * 2, moved=3 << 20, limit=WHOLE,
     )
     partner_matches = lax.ppermute(matches.astype(BF16), EXPERT, partner)
     received = exchanged(dispatch, EXPERT, EXPERTS)
-    mixed = dot(weights_down, projection).astype(BF16)
-    base = dot(tokens, projection)
-    received, partner_matches = lax.optimization_barrier((received, partner_matches))
-
-    packed_shape = (SLOTS, EMBED * 5 // 4)
+    mixed, base = call(
+        prepare_kernel,
+        [((HIDDEN, EMBED), BF16, vmem), ((ROWS, EMBED), F32, vmem)],
+        [(weights_down, hbm), (projection, hbm), (tokens, hbm)],
+        scratch=[
+            pltpu.VMEM((HIDDEN, WIDTH), BF16),
+            pltpu.VMEM((WIDTH, EMBED), BF16),
+            pltpu.VMEM((ROWS, WIDTH), BF16),
+            dma((3,)),
+        ],
+        flops=2 * (HIDDEN + ROWS) * WIDTH * EMBED, moved=8 << 20, limit=WHOLE,
+    )
+    received, partner_matches, base = lax.optimization_barrier((received, partner_matches, base))
+
     packed, hidden, slopes = call(
         forward_kernel,
-        [(packed_shape, BF16, hbm), ((TOTAL, HIDDEN), BF16, vmem), ((TOTAL, 2 * HIDDEN), BF16, vmem)],
-        [(received, hbm), (weights_joined, vmem), (mixed, vmem)],
+        [(packed_shape, BF16, hbm), ((TOTAL, HIDDEN), BF16, hbm), ((TOTAL, 2 * HIDDEN), BF16, hbm)],
+        [(received, hbm), (weights_joined, hbm), (mixed, hbm)],
         scratch=[
             pltpu.VMEM((TOTAL, WIDTH), BF16),
             pltpu.VMEM((SLOTS, WIDTH // 4), BF16),
             pltpu.VMEM((2, 2, TOTAL, 256), F32),
+            pltpu.VMEM((WIDTH, 2 * HIDDEN), BF16),
+            pltpu.VMEM((HIDDEN, EMBED), BF16),
+            pltpu.VMEM((TOTAL, HIDDEN), BF16),
+            pltpu.VMEM((TOTAL, 2 * HIDDEN), BF16),
             pltpu.VMEM(packed_shape, BF16),
-            dma((2,)),
-            dma((2,)),
+            dma((3 + 2 * len(CHUNKS),)),
+            dma((8,)),
         ],
-        flops=2 * TOTAL * HIDDEN * (2 * WIDTH + EMBED), moved=22 << 20,
+        flops=2 * TOTAL * HIDDEN * (2 * WIDTH + EMBED), moved=22 << 20, limit=55,
     )
     answer = exchanged(packed, EXPERT, EXPERTS)
     embedding, unit = call(
@@ -385,42 +502,69 @@
         [((1, ROWS), F32, vmem), ((ROWS, EMBED), BF16, vmem), (packed_shape, BF16, vmem)],
         [(routes, vmem), (gates, vmem), (matches, vmem), (partner_matches, vmem),
          (embedding, vmem), (unit, vmem), (keys, vmem)],
-        flops=2 * SLOTS * ROWS * EMBED * 2, moved=2 << 20,
+        flops=2 * SLOTS * ROWS * EMBED * 2, moved=2 << 20, limit=16,
     )
     arrived = exchanged(slot_grads, EXPERT, EXPERTS)
-    direct = dot_cols(embed_grad, projection)
-    input_grads, grads = call(
-        backward_kernel,
-        [((SLOTS, WIDTH * 5 // 4), BF16, hbm), ((TOTAL, EMBED), BF16, vmem)],
-        [(arrived, vmem), (mixed, vmem), (slopes, vmem), (weights_joined, vmem)],
+    half_shape = (WIDTH // 2, EMBED)
+    grads, own, other = call(
+        head_kernel,
+        [((TOTAL, EMBED), BF16, vmem), (half_shape, F32, hbm), (half_shape, BF16, hbm)],
+        [(arrived, vmem), (tokens, vmem), (embed_grad, vmem), (hidden, hbm), (weights_down, hbm)],
         scratch=[
+            pltpu.VMEM((TOTAL, HIDDEN), BF16),
+            pltpu.VMEM((HIDDEN, WIDTH), BF16),
+            pltpu.VMEM(half_shape, F32),
+            pltpu.VMEM(half_shape, BF16),
+            dma((5,)),
+            dma((2,)),
+        ],
+        flops=2 * HIDDEN * EMBED * (TOTAL + WIDTH), moved=12 << 20, limit=59,
+    )
+    arrivals = [lax.ppermute(other, "expert_2", [(0, 1), (1, 0)])]
+    joined_shape = (TOTAL, 2 * HIDDEN)
+    (joined_grad,) = call(
+        joined_kernel,
+        [(joined_shape, BF16, vmem)],
+        [(grads, vmem), (mixed, hbm), (slopes, hbm)],
+        scratch=[
+            pltpu.VMEM((HIDDEN, EMBED), BF16),
+            pltpu.VMEM(joined_shape, BF16),
             pltpu.VMEM((2, TOTAL, 256), F32),
-            pltpu.VMEM((TOTAL, 2 * HIDDEN), BF16),
+            dma((1 + 2 * len(CHUNKS),)),
+        ],
+        flops=2 * TOTAL * HIDDEN * EMBED, moved=8 << 20, limit=54,
+    )
+    (input_grads,) = call(
+        input_kernel,
+        [(wide_shape, BF16, hbm)],
+        [(joined_grad, vmem), (weights_joined, hbm), (arrivals[0], hbm)],
+        scratch=[
+            pltpu.VMEM((WIDTH, 2 * HIDDEN), BF16),
             pltpu.VMEM((SLOTS, WIDTH // 4), BF16),
-            pltpu.VMEM((SLOTS, WIDTH * 5 // 4), BF16),
+            pltpu.VMEM(wide_shape, BF16),
+            dma((WIDTH // TILE,)),
             dma((5,)),
         ],
-        flops=2 * TOTAL * HIDDEN * (2 * WIDTH + EMBED), moved=22 << 20,
+        flops=4 * TOTAL * HIDDEN * WIDTH, moved=18 << 20, limit=54,
     )
     back = exchanged(input_grads, EXPERT, EXPERTS)
-
-    def place(axis):
-        return lax.axis_index(axis).astype(jnp.int32).reshape(1), smem
-
-    own, other = call(
-        head_kernel,
-        [((WIDTH // 2, EMBED), F32, vmem), ((WIDTH // 2, EMBED), BF16, vmem)],
-        [place("expert_2"), (hidden, vmem), (grads, vmem), (tokens, vmem), (embed_grad, vmem),
-         (weights_down, vmem)],
-    )
-    arrivals = [lax.ppermute(other, "expert_2", [(0, 1), (1, 0)])]
+    direct = dot_cols(embed_grad, projection)
     for axis in ("dp", "expert_0", "expert_1"):
-        rows = own.shape[0] // 4
+        rows, count = own.shape[0] // 4, len(arrivals)
         own, *sent = call(
-            share_kernel,
-            [((rows, EMBED), F32, vmem)] + [((rows, EMBED), BF16, vmem)] * 3,
-            [place(axis), (own.reshape(4, rows, EMBED), vmem)]
-            + [(value.reshape(4, rows, EMBED), vmem) for value in arrivals],
+            functools.partial(share_kernel, axis, count),
+            [((rows, EMBED), F32, hbm)] + [((rows, EMBED), BF16, hbm)] * 3,
+            [(own.reshape(4, rows, EMBED), hbm)]
+            + [(value.reshape(4, rows, EMBED), hbm) for value in arrivals],
+            scratch=[
+                pltpu.VMEM((4, rows, EMBED), F32),
+                pltpu.VMEM((count, 4, rows, EMBED), BF16),
+                pltpu.VMEM((rows, EMBED), F32),
+                pltpu.VMEM((3, rows, EMBED), BF16),
+                dma((1 + count,)),
+                dma((4,)),
+            ],
+            limit=16,
         )
         arrivals = [
             lax.ppermute(value, axis, [(i, i ^ (k + 1)) for i in range(4)])
@@ -432,8 +576,9 @@
     device_count = lax.axis_size("dp") * EXPERTS
     grad_projection = summed * (1.0 / math.sqrt(ROWS * device_count))
     (grad_tokens,) = call(
-        combine_kernel, [((ROWS, WIDTH), BF16, vmem)], [(routes, vmem), (back, vmem), (direct, vmem)],
-        flops=2 * SLOTS * ROWS * WIDTH * 2, moved=4 << 20,
+        combine_kernel, [((ROWS, WIDTH), BF16, vmem)], [(routes, vmem), (direct, vmem), (back, hbm)],
+        scratch=[pltpu.VMEM(wide_shape, BF16), dma((5,))],
+        flops=2 * SLOTS * ROWS * WIDTH * 2, moved=4 << 20, limit=WHOLE,
     )
     return grad_tokens, grad_projection, row_loss.reshape(ROWS)
 

time: 198 us -> 202 us (1.020)
  Pallas kernels: 37.7 us -> 73.7 us
  local copies, waits for them, and re-layouts: 29.7 us -> 2.55 us
  blocking collectives: 15.9 us -> 32.7 us
  waiting for transfers between devices: 67.4 us -> 55.4 us
  matrix products: 8.14 us -> 1.8 us
  starting transfers between devices: 37 us -> 33.6 us
    pallas_call x10 -> x12, Pallas kernels: 37.7 us -> 73.7 us  [call(): pl.pallas_call(kernel, out_shape=tuple((jax.ShapeDtypeStruct(shape, dtype...]
    unnamed x46 -> x22, local copies, waits for them, and re-layouts: 29.7 us -> 2.55 us
    all_to_all x1 -> x2, blocking collectives: 15.9 us -> 32.7 us  [exchanged(): return lax.all_to_all(blocks, axes, 0, 0, tiled=True).reshape(rows, width)]
    all_to_all x3 -> x2, waiting for transfers between devices: 13.3 us -> 1.39 us  [exchanged(): return lax.all_to_all(blocks, axes, 0, 0, tiled=True).reshape(rows, width)]
    dot_general x2 -> x0, matrix products: 7.33 us -> none  [dot(): return jnp.dot(left, right, preferred_element_type=F32)]
    all_to_all x3 -> x2, starting transfers between devices: 16.9 us -> 12.5 us  [exchanged(): return lax.all_to_all(blocks, axes, 0, 0, tiled=True).reshape(rows, width)]
    ppermute x9, waiting for transfers between devices: 22.7 us -> 26 us  [body(): lax.ppermute(value, axis, [(i, i ^ k + 1) for i in range(4)])]
    ppermute x1, waiting for transfers between devices: 2.5 us -> 0.01 us  [body(): arrivals = [lax.ppermute(other, 'expert_2', [(0, 1), (1, 0)])]]
  transfers between devices with their start and end apart: 15 -> 14, of which waited for: 12 -> 10; matrix products, arithmetic and copies ran while one was open for 4% -> 1% of each run, Pallas kernels for 4% -> 9%
where the time goes in v3:
time: 202 us
  Pallas kernels  73.7 us (36%)
  waiting for transfers between devices  55.4 us (27%)
  starting transfers between devices  33.6 us (17%)
  blocking collectives  32.7 us (16%)
  local copies, waits for them, and re-layouts  2.55 us (1%)
    pallas_call x12, Pallas kernels, call(): pl.pallas_call(kernel, out_shape=tuple((jax.ShapeDtypeStruct(shape, dtype...  73.7 us
    all_to_all x2, blocking collectives, exchanged(): return lax.all_to_all(blocks, axes, 0, 0, tiled=True).reshape(rows, width)  32.7 us
    ppermute x9, waiting for transfers between devices, body(): lax.ppermute(value, axis, [(i, i ^ k + 1) for i in range(4)])  26 us
    ppermute x1, waiting for transfers between devices, body(): partner_matches = lax.ppermute(matches.astype(BF16), EXPERT, partner)  22.1 us
    ppermute x9, starting transfers between devices, body(): lax.ppermute(value, axis, [(i, i ^ k + 1) for i in range(4)])  15 us
    all_to_all x2, starting transfers between devices, exchanged(): return lax.all_to_all(blocks, axes, 0, 0, tiled=True).reshape(rows, width)  12.5 us
    ppermute x1, waiting for transfers between devices, body(): keys = lax.ppermute(unit, EXPERT, partner)  5.94 us
  transfers between devices with their start and end apart: 14, of which 10 were waited for; matrix products, arithmetic and copies ran while one was open for 1% of the time, Pallas kernels for 9%

profile of v3, /device:TPU:0, one launch (start us, length us, event | category | flops | bytes accessed | tf_op | source)
XLA Modules:
  0.0 201.6 jit_solution(4986473666993890319)
XLA Ops:
  0.6 3.2 %shard_map.94 = bf16[512,2560]{1,0:T(8,128)(2,1)} custom-call(s32[4,128]{1,0:T(4,128)} %bitcast.37, bf16[128,2048]{1,0:T(8,128)(2,1)} %tokens_ref.1), custom_call_target="tpu_custom_call" | custom-call | flops 536870912 | bytes 3145728 | tf_op jit(solution)/shard_map/pallas_call | solution.py:422
  3.9 0.0 copy-start.7
  3.9 7.4 %all-to-all-start = ((bf16[32,16,2560]{2,1,0:T(8,128)(2,1)}), bf16[32,16,2560]{2,1,0:T(8,128)(2,1)S(1)}, u32[]{:S(2)}, u32[]{:S(2)}) async-start(bf16[32,16,2560]{2,1,0:T(8,128)(2,1)} %bitcast.43), calls=%async_computation | async-start | bytes 5242880 | tf_op jit(solution)/shard_map/all_to_all | solution.py:436
  11.3 3.4 %collective-permute-start = (bf16[1,128]{1,0:T(2,128)(2,1)S(1)}, bf16[1,128]{1,0:T(2,128)(2,1)S(1)}, u32[]{:S(2)}, u32[]{:S(2)}) collective-permute-start(bf16[1,128]{1,0:T(2,128)(2,1)S(1)} %convert_element_type.12), channel_id=1, source_target_pairs={{0,16},{1,17},{2,18},{3,19},{4,20},{5,21},{6,22},{7,23},{8,24},{9,... | collective-permute-start | bytes 776 | tf_op jit(solution)/shard_map/ppermute | solution.py:458
  14.7 7.8 %shard_map.95 = (bf16[1408,512]{1,0:T(8,128)(2,1)}, f32[128,512]{1,0:T(8,128)}) custom-call(bf16[1408,2048]{1,0:T(8,128)(2,1)} %bitcast.50, bf16[2048,512]{1,0:T(8,128)(2,1)} %head_hbm.1, bf16[128,2048]{1,0:T(8,128)(2,1)} %tokens_ref.1), custom_call_target="tpu_custom_call" | custom-call | flops 3221225472 | bytes 8388608 | tf_op jit(solution)/shard_map/pallas_call | solution.py:422
  22.5 22.1 %collective-permute-done.partner_ref = bf16[1,128]{1,0:T(2,128)(2,1)S(1)} collective-permute-done((bf16[1,128]{1,0:T(2,128)(2,1)S(1)}, bf16[1,128]{1,0:T(2,128)(2,1)S(1)}, u32[]{:S(2)}, u32[]{:S(2)}) %collective-permute-start) | collective-permute-done | bytes 288 | tf_op jit(solution)/shard_map/ppermute | solution.py:458
  44.6 1.4 all-to-all-done
  45.9 1.5 copy-done.9
  47.5 14.6 %shard_map.96 = (bf16[512,640]{1,0:T(8,128)(2,1)}, bf16[640,1408]{1,0:T(8,128)(2,1)}, bf16[640,2816]{1,0:T(8,128)(2,1)}) custom-call(bf16[512,2560]{1,0:T(8,128)(2,1)} %bitcast.45, bf16[2048,2816]{1,0:T(8,128)(2,1)} %bitcast.48, bf16[1408,512]{1,0:T(8,128)(2,1)} %get-tuple-element.34.mixed_hbm), custom_call_target="tpu_custom_call" | custom-call | flops 8304721920 | bytes 23068672 | tf_op jit(solution)/shard_map/pallas_call | solution.py:422
  62.1 16.6 %all_to_all.20 = bf16[32,16,640]{2,1,0:T(8,128)(2,1)S(1)} all-to-all(bf16[32,16,640]{2,1,0:T(8,128)(2,1)} %bitcast.47), channel_id=1, replica_groups=mesh['dp'=4,'expert_0'=4,'expert_1'=4,'expert_2'=2] {'expert_0','expert_..., dimensions={0} | all-to-all | bytes 1310720 | tf_op jit(solution)/shard_map/all_to_all | solution.py:436
  78.7 0.9 shard_map.97
  79.6 1.8 collective-permute-start.1
  81.4 5.9 %collective-permute-done.1.key_ref = bf16[128,512]{1,0:T(8,128)(2,1)S(1)} collective-permute-done((bf16[128,512]{1,0:T(8,128)(2,1)S(1)}, bf16[128,512]{1,0:T(8,128)(2,1)S(1)}, u32[]{:S(2)}, u32[]{:S(2)}) %collective-permute-start.1) | collective-permute-done | bytes 131104 | tf_op jit(solution)/shard_map/ppermute | solution.py:499
  87.3 1.1 shard_map.98
  88.4 0.0 copy-start.3
  88.4 16.2 %all_to_all.21 = bf16[32,16,640]{2,1,0:T(8,128)(2,1)} all-to-all(bf16[32,16,640]{2,1,0:T(8,128)(2,1)S(1)} %bitcast.27), channel_id=1, replica_groups=mesh['dp'=4,'expert_0'=4,'expert_1'=4,'expert_2'=2] {'expert_0','expert_..., dimensions={0} | all-to-all | bytes 1310720 | tf_op jit(solution)/shard_map/all_to_all | solution.py:436
  104.6 11.3 %shard_map.99 = (bf16[640,512]{1,0:T(8,128)(2,1)}, f32[1024,512]{1,0:T(8,128)}, bf16[1024,512]{1,0:T(8,128)(2,1)}) custom-call(bf16[512,640]{1,0:T(8,128)(2,1)} %bitcast.46, bf16[128,2048]{1,0:T(8,128)(2,1)} %tokens_ref.1, bf16[128,512]{1,0:T(8,128)(2,1)} %copy-done.3, bf16[640,1408]{1,0:T(8,128)(2,1)} %get-tuple-element.41.hidden_hbm, ...), custom_call_target="tpu_custom_call" | custom-call | flops 3875536896 | bytes 12582912 | tf_op jit(solution)/shard_map/pallas_call | solution.py:422
  115.9 1.0 collective-permute-start.2
  117.0 7.7 %shard_map.100.joined_ref = bf16[640,2816]{1,0:T(8,128)(2,1)} custom-call(bf16[640,512]{1,0:T(8,128)(2,1)} %get-tuple-element.42.grads_ref, bf16[1408,512]{1,0:T(8,128)(2,1)} %get-tuple-element.34.mixed_hbm, bf16[640,2816]{1,0:T(8,128)(2,1)} %get-tuple-element.43.slopes_hbm), custom_call_target="tpu_custom_call" | custom-call | flops 922746880 | bytes 8388608 | tf_op jit(solution)/shard_map/pallas_call | solution.py:422
  124.6 0.0 collective-permute-done.2._
  124.7 1.0 copy-done.1
  125.7 20.9 %shard_map.101 = bf16[512,2560]{1,0:T(8,128)(2,1)} custom-call(bf16[640,2816]{1,0:T(8,128)(2,1)} %shard_map.100.joined_ref, bf16[2048,2816]{1,0:T(8,128)(2,1)} %bitcast.49, bf16[1024,512]{1,0:T(8,128)(2,1)} %copy-done.1), custom_call_target="tpu_custom_call" | custom-call | flops 7381975040 | bytes 18874368 | tf_op jit(solution)/shard_map/pallas_call | solution.py:422
  146.6 5.1 %all-to-all-start.3 = ((bf16[32,16,2560]{2,1,0:T(8,128)(2,1)}), bf16[32,16,2560]{2,1,0:T(8,128)(2,1)}, u32[]{:S(2)}, u32[]{:S(2)}) async-start(bf16[32,16,2560]{2,1,0:T(8,128)(2,1)} %bitcast.44), calls=%async_computation.3 | async-start | bytes 5242880 | tf_op jit(solution)/shard_map/all_to_all | solution.py:436
  151.7 0.0 copy-start.4
  151.7 0.0 copy-start.10
  151.7 0.6 shard_map.103
  152.3 2.0 collective-permute-start.3
  154.3 3.6 %collective-permute-start.4 = (bf16[256,512]{1,0:T(8,128)(2,1)S(1)}, bf16[256,512]{1,0:T(8,128)(2,1)S(1)}, u32[]{:S(2)}, u32[]{:S(2)}) collective-permute-start(bf16[256,512]{1,0:T(8,128)(2,1)S(1)} %get-tuple-element.48), channel_id=1, source_target_pairs={{0,64},{32,96},{64,0},{96,32},{1,65},{33,97},{65,1},{97,33},{2,66}... | collective-permute-start | bytes 786440 | tf_op jit(solution)/shard_map/ppermute | solution.py:570
  157.9 3.6 %collective-permute-done.3 = bf16[256,512]{1,0:T(8,128)(2,1)S(1)} collective-permute-done((bf16[256,512]{1,0:T(8,128)(2,1)S(1)}, bf16[256,512]{1,0:T(8,128)(2,1)S(1)}, u32[]{:S(2)}, u32[]{:S(2)}) %collective-permute-start.3) | collective-permute-done | bytes 262176 | tf_op jit(solution)/shard_map/ppermute | solution.py:570
  161.5 8.4 %collective-permute-done.4 = bf16[256,512]{1,0:T(8,128)(2,1)S(1)} collective-permute-done((bf16[256,512]{1,0:T(8,128)(2,1)S(1)}, bf16[256,512]{1,0:T(8,128)(2,1)S(1)}, u32[]{:S(2)}, u32[]{:S(2)}) %collective-permute-start.4) | collective-permute-done | bytes 262176 | tf_op jit(solution)/shard_map/ppermute | solution.py:570
  169.9 2.6 %collective-permute-done.5 = bf16[256,512]{1,0:T(8,128)(2,1)S(1)} collective-permute-done((bf16[256,512]{1,0:T(8,128)(2,1)S(1)}, bf16[256,512]{1,0:T(8,128)(2,1)S(1)}, u32[]{:S(2)}, u32[]{:S(2)}) %collective-permute-start.5) | collective-permute-done | bytes 262176 | tf_op jit(solution)/shard_map/ppermute | solution.py:570
  172.5 0.7 shard_map.104
  173.2 1.8 collective-permute-start.6
  175.0 2.8 %collective-permute-start.7 = (bf16[64,512]{1,0:T(8,128)(2,1)S(1)}, bf16[64,512]{1,0:T(8,128)(2,1)S(1)}, u32[]{:S(2)}, u32[]{:S(2)}) collective-permute-start(bf16[64,512]{1,0:T(8,128)(2,1)S(1)} %get-tuple-element.52), channel_id=1, source_target_pairs={{0,16},{8,24},{16,0},{24,8},{1,17},{9,25},{17,1},{25,9},{2,18},{10... | collective-permute-start | bytes 196616 | tf_op jit(solution)/shard_map/ppermute | solution.py:570
  177.8 0.2 collective-permute-start.8
  178.0 7.6 %collective-permute-done.6 = bf16[64,512]{1,0:T(8,128)(2,1)S(1)} collective-permute-done((bf16[64,512]{1,0:T(8,128)(2,1)S(1)}, bf16[64,512]{1,0:T(8,128)(2,1)S(1)}, u32[]{:S(2)}, u32[]{:S(2)}) %collective-permute-start.6) | collective-permute-done | bytes 65568 | tf_op jit(solution)/shard_map/ppermute | solution.py:570
  185.6 2.0 collective-permute-done.7
  187.5 0.0 collective-permute-done.8
  187.5 0.6 shard_map.105
  188.2 2.5 %collective-permute-start.10 = (bf16[16,512]{1,0:T(8,128)(2,1)S(1)}, bf16[16,512]{1,0:T(8,128)(2,1)S(1)}, u32[]{:S(2)}, u32[]{:S(2)}) collective-permute-start(bf16[16,512]{1,0:T(8,128)(2,1)S(1)} %get-tuple-element.56), channel_id=1, source_target_pairs={{0,4},{2,6},{4,0},{6,2},{1,5},{3,7},{5,1},{7,3},{8,12},{10,14},{12... | collective-permute-start | bytes 49160 | tf_op jit(solution)/shard_map/ppermute | solution.py:570
  190.7 2.1 %collective-permute-start.11 = (bf16[16,512]{1,0:T(8,128)(2,1)S(1)}, bf16[16,512]{1,0:T(8,128)(2,1)S(1)}, u32[]{:S(2)}, u32[]{:S(2)}) collective-permute-start(bf16[16,512]{1,0:T(8,128)(2,1)S(1)} %get-tuple-element.57), channel_id=1, source_target_pairs={{0,6},{2,4},{4,2},{6,0},{1,7},{3,5},{5,3},{7,1},{8,14},{10,12},{12... | collective-permute-start | bytes 49160 | tf_op jit(solution)/shard_map/ppermute | solution.py:570
  192.8 0.0 collective-permute-start.9
  192.8 1.8 fusion.direct_ref
  194.6 1.1 collective-permute-done.11
  195.6 0.9 collective-permute-done.9
  196.5 0.6 add_multiply_fusion
  197.1 0.0 all-to-all-done.3
  197.1 4.3 %shard_map.102 = bf16[128,2048]{1,0:T(8,128)(2,1)} custom-call(s32[4,128]{1,0:T(4,128)} %bitcast.38, f32[128,2048]{1,0:T(8,128)} %fusion.direct_ref, bf16[512,2560]{1,0:T(8,128)(2,1)} %bitcast.11.back_hbm), custom_call_target="tpu_custom_call" | custom-call | flops 536870912 | bytes 4194304 | tf_op jit(solution)/shard_map/pallas_call | solution.py:422
  (19 shorter events, 0.0 us)
Async XLA Ops:
  3.9 7.4 %copy-start.7 = (s32[1,128]{1,0:T(1,128)S(1)}, s32[1,128]{1,0:T(1,128)}, u32[]{:S(2)}) copy-start(s32[1,128]{1,0:T(1,128)} %matches_ref.1) | copy-start | bytes 1540
  3.9 42.1 %all-to-all-start = ((bf16[32,16,2560]{2,1,0:T(8,128)(2,1)}), bf16[32,16,2560]{2,1,0:T(8,128)(2,1)S(1)}, u32[]{:S(2)}, u32[]{:S(2)}) async-start(bf16[32,16,2560]{2,1,0:T(8,128)(2,1)} %bitcast.43), calls=%async_computation | async-start | bytes 5242880 | tf_op jit(solution)/shard_map/all_to_all | solution.py:436
  11.3 33.2 %collective-permute-start = (bf16[1,128]{1,0:T(2,128)(2,1)S(1)}, bf16[1,128]{1,0:T(2,128)(2,1)S(1)}, u32[]{:S(2)}, u32[]{:S(2)}) collective-permute-start(bf16[1,128]{1,0:T(2,128)(2,1)S(1)} %convert_element_type.12), channel_id=1, source_target_pairs={{0,16},{1,17},{2,18},{3,19},{4,20},{5,21},{6,22},{7,23},{8,24},{9,... | collective-permute-start | bytes 776 | tf_op jit(solution)/shard_map/ppermute | solution.py:458
  45.9 1.5 copy-start.9
  47.5 31.2 %copy-start.5 = (s32[128,4]{0,1:T(4,128)S(1)}, s32[128,4]{0,1:T(4,128)}, u32[]{:S(2)}) copy-start(s32[128,4]{0,1:T(4,128)} %param.8) | copy-start | bytes 6148
  47.5 31.2 %copy-start.6 = (f32[128,4]{0,1:T(4,128)S(1)}, f32[128,4]{0,1:T(4,128)}, u32[]{:S(2)}) copy-start(f32[128,4]{0,1:T(4,128)} %param.9) | copy-start | bytes 6148
  47.5 31.2 %copy-start.8 = (f32[128,512]{1,0:T(8,128)S(1)}, f32[128,512]{1,0:T(8,128)}, u32[]{:S(2)}) copy-start(f32[128,512]{1,0:T(8,128)} %get-tuple-element.36.base_ref) | copy-start | bytes 786436
  79.6 7.7 %collective-permute-start.1 = (bf16[128,512]{1,0:T(8,128)(2,1)S(1)}, bf16[128,512]{1,0:T(8,128)(2,1)S(1)}, u32[]{:S(2)}, u32[]{:S(2)}) collective-permute-start(bf16[128,512]{1,0:T(8,128)(2,1)S(1)} %get-tuple-element.38.unit_ref), channel_id=1, source_target_pairs={{0,16},{1,17},{2,18},{3,19},{4,20},{5,21},{6,22},{7,23},{8,24},{9,... | collective-permute-start | bytes 393224 | tf_op jit(solution)/shard_map/ppermute | solution.py:499
  88.4 16.2 %copy-start.3 = (bf16[128,512]{1,0:T(8,128)(2,1)}, bf16[128,512]{1,0:T(8,128)(2,1)S(1)}, u32[]{:S(2)}) copy-start(bf16[128,512]{1,0:T(8,128)(2,1)S(1)} %get-tuple-element.39.embed_grad_ref) | copy-start | bytes 393220
  115.9 8.7 %collective-permute-start.2 = (bf16[1024,512]{1,0:T(8,128)(2,1)}, bf16[1024,512]{1,0:T(8,128)(2,1)S(1)}, u32[]{:S(2)}, u32[]{:S(2)}) collective-permute-start(bf16[1024,512]{1,0:T(8,128)(2,1)} %get-tuple-element.44), channel_id=1, source_target_pairs={{0,1},{1,0},{2,3},{3,2},{4,5},{5,4},{6,7},{7,6},{8,9},{9,8},{10,11... | collective-permute-start | bytes 3145736 | tf_op jit(solution)/shard_map/ppermute | solution.py:523
  124.7 1.0 copy-start.1
  146.6 5.1 %copy-start = (f32[1024,512]{1,0:T(8,128)S(1)}, f32[1024,512]{1,0:T(8,128)}, u32[]{:S(2)}) copy-start(f32[1024,512]{1,0:T(8,128)} %get-tuple-element.45) | copy-start | bytes 6291460
  146.6 5.1 %copy-start.2 = (bf16[1024,512]{1,0:T(8,128)(2,1)S(1)}, bf16[1024,512]{1,0:T(8,128)(2,1)}, u32[]{:S(2)}) copy-start(bf16[1024,512]{1,0:T(8,128)(2,1)} %copy-done.1) | copy-start | bytes 3145732
  146.6 50.5 %all-to-all-start.3 = ((bf16[32,16,2560]{2,1,0:T(8,128)(2,1)}), bf16[32,16,2560]{2,1,0:T(8,128)(2,1)}, u32[]{:S(2)}, u32[]{:S(2)}) async-start(bf16[32,16,2560]{2,1,0:T(8,128)(2,1)} %bitcast.44), calls=%async_computation.3 | async-start | bytes 5242880 | tf_op jit(solution)/shard_map/all_to_all | solution.py:436
  151.7 41.1 %copy-start.4 = (bf16[128,512]{1,0:T(8,128)(2,1)S(1)}, bf16[128,512]{1,0:T(8,128)(2,1)}, u32[]{:S(2)}) copy-start(bf16[128,512]{1,0:T(8,128)(2,1)} %copy-done.3) | copy-start | bytes 393220
  151.7 41.1 %copy-start.10 = (bf16[2048,512]{1,0:T(8,128)(2,1)S(1)}, bf16[2048,512]{1,0:T(8,128)(2,1)}, u32[]{:S(2)}) copy-start(bf16[2048,512]{1,0:T(8,128)(2,1)} %head_hbm.1) | copy-start | bytes 6291460
  152.3 9.2 %collective-permute-start.3 = (bf16[256,512]{1,0:T(8,128)(2,1)S(1)}, bf16[256,512]{1,0:T(8,128)(2,1)S(1)}, u32[]{:S(2)}, u32[]{:S(2)}) collective-permute-start(bf16[256,512]{1,0:T(8,128)(2,1)S(1)} %get-tuple-element.47), channel_id=1, source_target_pairs={{0,32},{32,0},{64,96},{96,64},{1,33},{33,1},{65,97},{97,65},{2,34}... | collective-permute-start | bytes 786440 | tf_op jit(solution)/shard_map/ppermute | solution.py:570
  154.3 15.6 %collective-permute-start.4 = (bf16[256,512]{1,0:T(8,128)(2,1)S(1)}, bf16[256,512]{1,0:T(8,128)(2,1)S(1)}, u32[]{:S(2)}, u32[]{:S(2)}) collective-permute-start(bf16[256,512]{1,0:T(8,128)(2,1)S(1)} %get-tuple-element.48), channel_id=1, source_target_pairs={{0,64},{32,96},{64,0},{96,32},{1,65},{33,97},{65,1},{97,33},{2,66}... | collective-permute-start | bytes 786440 | tf_op jit(solution)/shard_map/ppermute | solution.py:570
  157.9 14.6 %collective-permute-start.5 = (bf16[256,512]{1,0:T(8,128)(2,1)S(1)}, bf16[256,512]{1,0:T(8,128)(2,1)S(1)}, u32[]{:S(2)}, u32[]{:S(2)}) collective-permute-start(bf16[256,512]{1,0:T(8,128)(2,1)S(1)} %get-tuple-element.49), channel_id=1, source_target_pairs={{0,96},{32,64},{64,32},{96,0},{1,97},{33,65},{65,33},{97,1},{2,98}... | collective-permute-start | bytes 786440 | tf_op jit(solution)/shard_map/ppermute | solution.py:570
  173.2 12.4 %collective-permute-start.6 = (bf16[64,512]{1,0:T(8,128)(2,1)S(1)}, bf16[64,512]{1,0:T(8,128)(2,1)S(1)}, u32[]{:S(2)}, u32[]{:S(2)}) collective-permute-start(bf16[64,512]{1,0:T(8,128)(2,1)S(1)} %get-tuple-element.51), channel_id=1, source_target_pairs={{0,8},{8,0},{16,24},{24,16},{1,9},{9,1},{17,25},{25,17},{2,10},{10... | collective-permute-start | bytes 196616 | tf_op jit(solution)/shard_map/ppermute | solution.py:570
  175.0 12.5 %collective-permute-start.7 = (bf16[64,512]{1,0:T(8,128)(2,1)S(1)}, bf16[64,512]{1,0:T(8,128)(2,1)S(1)}, u32[]{:S(2)}, u32[]{:S(2)}) collective-permute-start(bf16[64,512]{1,0:T(8,128)(2,1)S(1)} %get-tuple-element.52), channel_id=1, source_target_pairs={{0,16},{8,24},{16,0},{24,8},{1,17},{9,25},{17,1},{25,9},{2,18},{10... | collective-permute-start | bytes 196616 | tf_op jit(solution)/shard_map/ppermute | solution.py:570
  177.8 9.7 %collective-permute-start.8 = (bf16[64,512]{1,0:T(8,128)(2,1)S(1)}, bf16[64,512]{1,0:T(8,128)(2,1)S(1)}, u32[]{:S(2)}, u32[]{:S(2)}) collective-permute-start(bf16[64,512]{1,0:T(8,128)(2,1)S(1)} %get-tuple-element.53), channel_id=1, source_target_pairs={{0,24},{8,16},{16,8},{24,0},{1,25},{9,17},{17,9},{25,1},{2,26},{10... | collective-permute-start | bytes 196616 | tf_op jit(solution)/shard_map/ppermute | solution.py:570
  188.2 6.4 %collective-permute-start.10 = (bf16[16,512]{1,0:T(8,128)(2,1)S(1)}, bf16[16,512]{1,0:T(8,128)(2,1)S(1)}, u32[]{:S(2)}, u32[]{:S(2)}) collective-permute-start(bf16[16,512]{1,0:T(8,128)(2,1)S(1)} %get-tuple-element.56), channel_id=1, source_target_pairs={{0,4},{2,6},{4,0},{6,2},{1,5},{3,7},{5,1},{7,3},{8,12},{10,14},{12... | collective-permute-start | bytes 49160 | tf_op jit(solution)/shard_map/ppermute | solution.py:570
  190.7 4.9 %collective-permute-start.11 = (bf16[16,512]{1,0:T(8,128)(2,1)S(1)}, bf16[16,512]{1,0:T(8,128)(2,1)S(1)}, u32[]{:S(2)}, u32[]{:S(2)}) collective-permute-start(bf16[16,512]{1,0:T(8,128)(2,1)S(1)} %get-tuple-element.57), channel_id=1, source_target_pairs={{0,6},{2,4},{4,2},{6,0},{1,7},{3,5},{5,3},{7,1},{8,14},{10,12},{12... | collective-permute-start | bytes 49160 | tf_op jit(solution)/shard_map/ppermute | solution.py:570
  192.8 3.7 %collective-permute-start.9 = (bf16[16,512]{1,0:T(8,128)(2,1)S(1)}, bf16[16,512]{1,0:T(8,128)(2,1)S(1)}, u32[]{:S(2)}, u32[]{:S(2)}) collective-permute-start(bf16[16,512]{1,0:T(8,128)(2,1)S(1)} %get-tuple-element.55), channel_id=1, source_target_pairs={{0,2},{2,0},{4,6},{6,4},{1,3},{3,1},{5,7},{7,5},{8,10},{10,8},{12,... | collective-permute-start | bytes 49160 | tf_op jit(solution)/shard_map/ppermute | solution.py:570

commit v4 on v3

--- a/solution.py
+++ b/solution.py
@@ -140,8 +140,8 @@
 
 
 def forward_kernel(
-    recv_hbm, w_hbm, mixed_hbm, out_hbm, hidden_hbm, slopes_hbm,
-    x_ref, extra_ref, act_ref, w_ref, mixed_ref, hidden_ref, slopes_ref, out_ref, sems, out_sems,
+    recv_ref, w_hbm, mixed_hbm, out_hbm, hidden_hbm, slopes_hbm,
+    x_ref, act_ref, w_ref, mixed_ref, hidden_ref, slopes_ref, out_ref, sems, out_sems,
 ):
     quarter = WIDTH // 4
 
@@ -150,20 +150,18 @@
         copy.start()
         return copy
 
-    extra_copy = bring(recv_hbm.at[:, pl.ds(WIDTH, quarter)], extra_ref, 0)
-    main_copy = bring(recv_hbm.at[:, pl.ds(0, WIDTH)], x_ref.at[pl.ds(0, SLOTS), :], 1)
+    groups = ((0, 1), (1, 3), (3, len(CHUNKS)))
     weight_copies = []
-    for c, (lo, hi) in enumerate(CHUNKS):
+    for g, (begin, end) in enumerate(groups):
+        lo, hi = CHUNKS[begin][0], CHUNKS[end - 1][1]
         for h in range(2):
             cols = pl.ds(h * HIDDEN + lo, hi - lo)
-            weight_copies.append(bring(w_hbm.at[:, cols], w_ref.at[:, cols], 3 + 2 * c + h))
-    mixed_copy = bring(mixed_hbm, mixed_ref, 2)
-    turned = unpacker()
-    extra_copy.wait()
-    spread = dot(turned, extra_ref[...]).astype(BF16)
+            weight_copies.append(bring(w_hbm.at[:, cols], w_ref.at[:, cols], 1 + 2 * g + h))
+    mixed_copy = bring(mixed_hbm, mixed_ref, 0)
+    x_ref[:SLOTS, :] = recv_ref[:, :WIDTH]
+    spread = dot(unpacker(), recv_ref[:, WIDTH:]).astype(BF16)
     for j in range(4):
         x_ref[SLOTS:, j * quarter : (j + 1) * quarter] = spread[j * SPARE : (j + 1) * SPARE]
-    main_copy.wait()
     outgoing = []
 
     def send(source, target, lo, wide):
@@ -172,38 +170,49 @@
         copy.start()
         outgoing.append(copy)
 
-    sent = 0
-    for c, (lo, hi) in enumerate(CHUNKS):
-        slot = c % 2
-        wide = hi - lo
-        weight_copies[2 * c].wait()
-        weight_copies[2 * c + 1].wait()
-        act_ref[slot, 0, :, :wide] = dot(x_ref[...], w_ref[:, lo:hi])
-        act_ref[slot, 1, :, :wide] = dot(x_ref[...], w_ref[:, HIDDEN + lo : HIDDEN + hi])
-        for m in range(0, TOTAL, 64):
-            gate = act_ref[slot, 0, m : m + 64, :wide]
-            up = act_ref[slot, 1, m : m + 64, :wide]
-            sigmoid = 0.5 + 0.5 * jnp.tanh(0.5 * gate)
-            silu = gate * sigmoid
-            hidden_ref[m : m + 64, lo:hi] = (silu * up).astype(BF16)
-            slopes_ref[m : m + 64, HIDDEN + lo : HIDDEN + hi] = silu.astype(BF16)
-            slopes_ref[m : m + 64, lo:hi] = (up * sigmoid * (1.0 + gate * (1.0 - sigmoid))).astype(BF16)
-        if c % 3 == 2:
-            send(hidden_ref, hidden_hbm, sent, hi - sent)
-            send(slopes_ref, slopes_hbm, sent, hi - sent)
-            send(slopes_ref, slopes_hbm, HIDDEN + sent, hi - sent)
-            sent = hi
+    for g, (begin, end) in enumerate(groups):
+        weight_copies[2 * g].wait()
+        weight_copies[2 * g + 1].wait()
+        for c in range(begin, end):
+            lo, hi = CHUNKS[c]
+            slot = c % 2
+            wide = hi - lo
+            act_ref[slot, 0, :, :wide] = dot(x_ref[...], w_ref[:, lo:hi])
+            act_ref[slot, 1, :, :wide] = dot(x_ref[...], w_ref[:, HIDDEN + lo : HIDDEN + hi])
+            for m in range(0, TOTAL, 64):
+                rows = slice(m, m + 64)
+                gate = act_ref[slot, 0, rows, :wide]
+                up = act_ref[slot, 1, rows, :wide]
+                sigmoid = 0.5 + 0.5 * jnp.tanh(0.5 * gate)
+                silu = gate * sigmoid
+                hidden_ref[rows, lo:hi] = (silu * up).astype(BF16)
+                slopes_ref[rows, HIDDEN + lo : HIDDEN + hi] = silu.astype(BF16)
+                slopes_ref[rows, lo:hi] = (up * sigmoid * (1.0 + gate * (1.0 - sigmoid))).astype(BF16)
+        lo, hi = CHUNKS[begin][0], CHUNKS[end - 1][1]
+        send(hidden_ref, hidden_hbm, lo, hi - lo)
+        send(slopes_ref, slopes_hbm, lo, hi - lo)
+        send(slopes_ref, slopes_hbm, HIDDEN + lo, hi - lo)
     mixed_copy.wait()
     projected = dot(hidden_ref[...], mixed_ref[...]).astype(BF16)
     out_ref[:, :EMBED] = projected[:SLOTS]
-    send(out_ref, out_hbm, 0, EMBED)
     quarter = EMBED // 4
     stacked = jnp.concatenate(
         [projected[SLOTS:, j * quarter : (j + 1) * quarter] for j in range(4)], axis=0
     )
     out_ref[:, EMBED:] = dot(packer(), stacked).astype(BF16)
-    send(out_ref, out_hbm, EMBED, quarter)
+    send(out_ref, out_hbm, 0, EMBED + quarter)
     for copy in outgoing:
+        copy.wait()
+
+
+def fetch_kernel(_, down_hbm, hidden_hbm, down_ref, hidden_ref, sems):
+    copies = (
+        pltpu.make_async_copy(hidden_hbm, hidden_ref, sems.at[0]),
+        pltpu.make_async_copy(down_hbm, down_ref, sems.at[1]),
+    )
+    for copy in copies:
+        copy.start()
+    for copy in copies:
         copy.wait()
 
 
@@ -232,7 +241,7 @@
 
 
 def loss_kernel(
-    routes_ref, gates_ref, matches_ref, partner_ref, embedding_ref, unit_ref, key_ref,
+    routes_ref, gates_ref, matches_ref, partner_ref, embedding_ref, unit_ref, key_ref, _,
     loss_ref, grad_ref, out_ref,
 ):
     embedding = embedding_ref[...]
@@ -272,29 +281,16 @@
 
 
 def head_kernel(
-    arrived_ref, tokens_ref, embed_grad_ref, hidden_hbm, down_hbm, grads_ref, own_hbm, other_hbm,
-    hidden_ref, down_ref, own_ref, other_ref, sems, out_sems,
+    arrived_ref, tokens_ref, embed_grad_ref, hidden_ref, down_ref, grads_ref, own_ref, other_ref
 ):
-    hidden_copy = pltpu.make_async_copy(hidden_hbm, hidden_ref, sems.at[0])
-    hidden_copy.start()
-    step = WIDTH // 4
-    down_copies = []
-    for i in range(4):
-        cols = pl.ds(i * step, step)
-        copy = pltpu.make_async_copy(down_hbm.at[:, cols], down_ref.at[:, cols], sems.at[1 + i])
-        copy.start()
-        down_copies.append(copy)
     quarter = EMBED // 4
     grads_ref[:SLOTS, :] = arrived_ref[:, :EMBED]
     spread = dot(unpacker(), arrived_ref[:, EMBED:]).astype(BF16)
     for j in range(4):
         grads_ref[SLOTS:, j * quarter : (j + 1) * quarter] = spread[j * SPARE : (j + 1) * SPARE]
     first = lax.axis_index("expert_2") == 0
-    hidden_copy.wait()
     inner = dot_rows(hidden_ref[...], grads_ref[...]).astype(BF16)
     for n in range(0, WIDTH, TILE):
-        if n % step == 0:
-            down_copies[n // step].wait()
         part = dot_rows(down_ref[:, n : n + TILE], inner)
         part = part + dot_rows(tokens_ref[:, n : n + TILE], embed_grad_ref[...])
         for b in range(TILE // 32):
@@ -302,33 +298,13 @@
             even, odd = part[32 * b : 32 * b + 16], part[32 * b + 16 : 32 * b + 32]
             own_ref[row : row + 16, :] = jnp.where(first, even, odd)
             other_ref[row : row + 16, :] = jnp.where(first, odd, even).astype(BF16)
-    other_copy = pltpu.make_async_copy(other_ref, other_hbm, out_sems.at[0])
-    own_copy = pltpu.make_async_copy(own_ref, own_hbm, out_sems.at[1])
-    other_copy.start()
-    own_copy.start()
-    other_copy.wait()
-    own_copy.wait()
-
-
-def joined_kernel(grads_ref, mixed_hbm, slopes_hbm, joined_ref, mixed_ref, slopes_ref, act_ref, sems):
-    def bring(source, target, index):
-        copy = pltpu.make_async_copy(source, target, sems.at[index])
-        copy.start()
-        return copy
-
-    mixed_copy = bring(mixed_hbm, mixed_ref, 0)
-    slopes_copies = []
-    for c, (lo, hi) in enumerate(CHUNKS):
-        for h in range(2):
-            cols = pl.ds(h * HIDDEN + lo, hi - lo)
-            slopes_copies.append(bring(slopes_hbm.at[:, cols], slopes_ref.at[:, cols], 1 + 2 * c + h))
-    mixed_copy.wait()
+
+
+def joined_kernel(grads_ref, mixed_ref, slopes_ref, joined_ref, act_ref):
     for c, (lo, hi) in enumerate(CHUNKS):
         slot = c % 2
         wide = hi - lo
         act_ref[slot, :, :wide] = dot_cols(grads_ref[...], mixed_ref[lo:hi, :])
-        slopes_copies[2 * c].wait()
-        slopes_copies[2 * c + 1].wait()
         for m in range(0, TOTAL, 64):
             hidden_grad = act_ref[slot, m : m + 64, :wide]
             for offset in (0, HIDDEN):
@@ -336,14 +312,8 @@
                 joined_ref[m : m + 64, offset + lo : offset + hi] = (hidden_grad * slope).astype(BF16)
 
 
-def input_kernel(joined_ref, w_hbm, _, out_hbm, w_ref, extra_ref, out_ref, sems, out_sems):
+def input_kernel(joined_ref, w_ref, _, out_hbm, extra_ref, out_ref, out_sems):
     step = WIDTH // 4
-    weight_copies = []
-    for n in range(0, WIDTH, TILE):
-        rows = pl.ds(n, TILE)
-        copy = pltpu.make_async_copy(w_hbm.at[rows, :], w_ref.at[rows, :], sems.at[n // TILE])
-        copy.start()
-        weight_copies.append(copy)
     outgoing = []
 
     def send(start, wide, index):
@@ -353,15 +323,14 @@
         outgoing.append(copy)
 
     for n in range(0, WIDTH, TILE):
-        weight_copies[n // TILE].wait()
         result = dot_cols(joined_ref[...], w_ref[n : n + TILE, :]).astype(BF16)
         out_ref[:, n : n + TILE] = result[:SLOTS]
         j, within = n // step, n % step
         extra_ref[j * SPARE : (j + 1) * SPARE, within : within + TILE] = result[SLOTS:]
-        if within:
-            send(j * step, step, j)
+        if n == WIDTH // 2 - TILE:
+            send(0, WIDTH // 2, 0)
     out_ref[:, WIDTH:] = dot(packer(), extra_ref[...]).astype(BF16)
-    send(WIDTH, step, 4)
+    send(WIDTH // 2, WIDTH // 2 + step, 1)
     for copy in outgoing:
         copy.wait()
 
@@ -474,20 +443,19 @@
     packed, hidden, slopes = call(
         forward_kernel,
         [(packed_shape, BF16, hbm), ((TOTAL, HIDDEN), BF16, hbm), ((TOTAL, 2 * HIDDEN), BF16, hbm)],
-        [(received, hbm), (weights_joined, hbm), (mixed, hbm)],
+        [(received, vmem), (weights_joined, hbm), (mixed, hbm)],
         scratch=[
             pltpu.VMEM((TOTAL, WIDTH), BF16),
-            pltpu.VMEM((SLOTS, WIDTH // 4), BF16),
             pltpu.VMEM((2, 2, TOTAL, 256), F32),
             pltpu.VMEM((WIDTH, 2 * HIDDEN), BF16),
             pltpu.VMEM((HIDDEN, EMBED), BF16),
             pltpu.VMEM((TOTAL, HIDDEN), BF16),
             pltpu.VMEM((TOTAL, 2 * HIDDEN), BF16),
             pltpu.VMEM(packed_shape, BF16),
-            dma((3 + 2 * len(CHUNKS),)),
-            dma((8,)),
+            dma((7,)),
+            dma((10,)),
         ],
-        flops=2 * TOTAL * HIDDEN * (2 * WIDTH + EMBED), moved=22 << 20, limit=55,
+        flops=2 * TOTAL * HIDDEN * (2 * WIDTH + EMBED), moved=22 << 20, limit=56.5,
     )
     answer = exchanged(packed, EXPERT, EXPERTS)
     embedding, unit = call(
@@ -497,89 +465,79 @@
         flops=4 * SLOTS * ROWS * EMBED * 2, moved=2 << 20,
     )
     keys = lax.ppermute(unit, EXPERT, partner)
+    down_near, hidden_near = call(
+        fetch_kernel,
+        [(weights_down.shape, BF16, vmem), (hidden.shape, BF16, vmem)],
+        [(unit, vmem), (weights_down, hbm), (hidden, hbm)],
+        scratch=[dma((2,))],
+        moved=16 << 20, limit=30,
+    )
     row_loss, embed_grad, slot_grads = call(
         loss_kernel,
         [((1, ROWS), F32, vmem), ((ROWS, EMBED), BF16, vmem), (packed_shape, BF16, vmem)],
         [(routes, vmem), (gates, vmem), (matches, vmem), (partner_matches, vmem),
-         (embedding, vmem), (unit, vmem), (keys, vmem)],
+         (embedding, vmem), (unit, vmem), (keys, vmem), (hidden_near, hbm)],
         flops=2 * SLOTS * ROWS * EMBED * 2, moved=2 << 20, limit=16,
     )
     arrived = exchanged(slot_grads, EXPERT, EXPERTS)
     half_shape = (WIDTH // 2, EMBED)
     grads, own, other = call(
         head_kernel,
-        [((TOTAL, EMBED), BF16, vmem), (half_shape, F32, hbm), (half_shape, BF16, hbm)],
-        [(arrived, vmem), (tokens, vmem), (embed_grad, vmem), (hidden, hbm), (weights_down, hbm)],
-        scratch=[
-            pltpu.VMEM((TOTAL, HIDDEN), BF16),
-            pltpu.VMEM((HIDDEN, WIDTH), BF16),
-            pltpu.VMEM(half_shape, F32),
-            pltpu.VMEM(half_shape, BF16),
-            dma((5,)),
-            dma((2,)),
-        ],
-        flops=2 * HIDDEN * EMBED * (TOTAL + WIDTH), moved=12 << 20, limit=59,
+        [((TOTAL, EMBED), BF16, vmem), (half_shape, F32, vmem), (half_shape, BF16, vmem)],
+        [(arrived, vmem), (tokens, vmem), (embed_grad, vmem), (hidden_near, vmem), (down_near, vmem)],
+        flops=2 * HIDDEN * EMBED * (TOTAL + WIDTH), moved=12 << 20, limit=16,
     )
     arrivals = [lax.ppermute(other, "expert_2", [(0, 1), (1, 0)])]
     joined_shape = (TOTAL, 2 * HIDDEN)
     (joined_grad,) = call(
         joined_kernel,
         [(joined_shape, BF16, vmem)],
-        [(grads, vmem), (mixed, hbm), (slopes, hbm)],
-        scratch=[
-            pltpu.VMEM((HIDDEN, EMBED), BF16),
-            pltpu.VMEM(joined_shape, BF16),
-            pltpu.VMEM((2, TOTAL, 256), F32),
-            dma((1 + 2 * len(CHUNKS),)),
-        ],
-        flops=2 * TOTAL * HIDDEN * EMBED, moved=8 << 20, limit=54,
+        [(grads, vmem), (mixed, vmem), (slopes, vmem)],
+        scratch=[pltpu.VMEM((2, TOTAL, 256), F32)],
+        flops=2 * TOTAL * HIDDEN * EMBED, moved=8 << 20, limit=16,
     )
     (input_grads,) = call(
         input_kernel,
         [(wide_shape, BF16, hbm)],
-        [(joined_grad, vmem), (weights_joined, hbm), (arrivals[0], hbm)],
+        [(joined_grad, vmem), (weights_joined, vmem), (arrivals[0], hbm)],
         scratch=[
-            pltpu.VMEM((WIDTH, 2 * HIDDEN), BF16),
             pltpu.VMEM((SLOTS, WIDTH // 4), BF16),
             pltpu.VMEM(wide_shape, BF16),
-            dma((WIDTH // TILE,)),
-            dma((5,)),
+            dma((2,)),
         ],
-        flops=4 * TOTAL * HIDDEN * WIDTH, moved=18 << 20, limit=54,
+        flops=4 * TOTAL * HIDDEN * WIDTH, moved=18 << 20, limit=34,
     )
     back = exchanged(input_grads, EXPERT, EXPERTS)
     direct = dot_cols(embed_grad, projection)
-    for axis in ("dp", "expert_0", "expert_1"):
-        rows, count = own.shape[0] // 4, len(arrivals)
-        own, *sent = call(
-            functools.partial(share_kernel, axis, count),
-            [((rows, EMBED), F32, hbm)] + [((rows, EMBED), BF16, hbm)] * 3,
-            [(own.reshape(4, rows, EMBED), hbm)]
-            + [(value.reshape(4, rows, EMBED), hbm) for value in arrivals],
-            scratch=[
-                pltpu.VMEM((4, rows, EMBED), F32),
-                pltpu.VMEM((count, 4, rows, EMBED), BF16),
-                pltpu.VMEM((rows, EMBED), F32),
-                pltpu.VMEM((3, rows, EMBED), BF16),
-                dma((1 + count,)),
-                dma((4,)),
-            ],
-            limit=16,
-        )
-        arrivals = [
-            lax.ppermute(value, axis, [(i, i ^ (k + 1)) for i in range(4)])
-            for k, value in enumerate(sent)
-        ]
-    summed = own
-    for value in arrivals:
-        summed = summed + value.astype(F32)
-    device_count = lax.axis_size("dp") * EXPERTS
-    grad_projection = summed * (1.0 / math.sqrt(ROWS * device_count))
+    rows = own.shape[0] // 4
+    own, *sent = call(
+        functools.partial(share_kernel, "dp", 1),
+        [((rows, EMBED), F32, hbm)] + [((rows, EMBED), BF16, hbm)] * 3,
+        [(value.reshape(4, rows, EMBED), hbm) for value in (own, *arrivals)],
+        scratch=[
+            pltpu.VMEM((4, rows, EMBED), F32),
+            pltpu.VMEM((1, 4, rows, EMBED), BF16),
+            pltpu.VMEM((rows, EMBED), F32),
+            pltpu.VMEM((3, rows, EMBED), BF16),
+            dma((2,)),
+            dma((4,)),
+        ],
+        limit=16,
+    )
+    for k, value in enumerate(sent):
+        arrived = lax.ppermute(value, "dp", [(i, i ^ (k + 1)) for i in range(4)])
+        own = own + arrived.astype(F32)
+    back, sums = lax.optimization_barrier((back, own.astype(BF16)))
+    parts = lax.all_to_all(
+        sums.reshape(16, 16, EMBED), ("expert_0", "expert_1"), 0, 0, tiled=True
+    )
     (grad_tokens,) = call(
         combine_kernel, [((ROWS, WIDTH), BF16, vmem)], [(routes, vmem), (direct, vmem), (back, hbm)],
         scratch=[pltpu.VMEM(wide_shape, BF16), dma((5,))],
         flops=2 * SLOTS * ROWS * WIDTH * 2, moved=4 << 20, limit=WHOLE,
     )
+    device_count = lax.axis_size("dp") * EXPERTS
+    grad_projection = jnp.sum(parts.astype(F32), axis=0) * (1.0 / math.sqrt(ROWS * device_count))
     return grad_tokens, grad_projection, row_loss.reshape(ROWS)
 
 

time: 202 us -> 175 us (0.87)
  Pallas kernels: 73.7 us -> 50.1 us
  starting transfers between devices: 33.6 us -> 27.5 us
  waiting for transfers between devices: 55.4 us -> 59.5 us
  local copies, waits for them, and re-layouts: 2.55 us -> 0.06 us
    pallas_call x12 -> x11, Pallas kernels: 73.7 us -> 50.1 us  [call(): pl.pallas_call(kernel, out_shape=tuple((jax.ShapeDtypeStruct(shape, dtype...]
    all_to_all x2, waiting for transfers between devices: 1.39 us -> 14.4 us  [exchanged(): return lax.all_to_all(blocks, axes, 0, 0, tiled=True).reshape(rows, width)]
    ppermute x9 -> x3, waiting for transfers between devices: 26 us -> 14.6 us  [body(): arrived = lax.ppermute(value, 'dp', [(i, i ^ k + 1) for i in range(4)])]
    ppermute x9 -> x3, starting transfers between devices: 15 us -> 5.58 us  [body(): arrived = lax.ppermute(value, 'dp', [(i, i ^ k + 1) for i in range(4)])]
    all_to_all x0 -> x1, starting transfers between devices: none -> 3.53 us  [body(): lax.all_to_all(sums.reshape(16, 16, EMBED), ('expert_0', 'expert_1'), 0,...]
    unnamed x22 -> x28, local copies, waits for them, and re-layouts: 2.55 us -> 0.06 us
    all_to_all x0 -> x1, waiting for transfers between devices: none -> 2.38 us  [body(): lax.all_to_all(sums.reshape(16, 16, EMBED), ('expert_0', 'expert_1'), 0,...]
  transfers between devices with their start and end apart: 14 -> 9, of which waited for: 10 -> 9; matrix products, arithmetic and copies ran while one was open for 1% -> 2% of each run, Pallas kernels for 9% -> 8%
where the time goes in v4:
time: 175 us; the launch traced here: 174 us
  waiting for transfers between devices  59.5 us (34%)
  Pallas kernels  50.1 us (29%)
  blocking collectives  32.8 us (19%)
  starting transfers between devices  27.5 us (16%)
  matrix products  1.8 us (1%)
    pallas_call x11, Pallas kernels, call(): pl.pallas_call(kernel, out_shape=tuple((jax.ShapeDtypeStruct(shape, dtype...  50.1 us
    all_to_all x2, blocking collectives, exchanged(): return lax.all_to_all(blocks, axes, 0, 0, tiled=True).reshape(rows, width)  32.8 us
    ppermute x1, waiting for transfers between devices, body(): partner_matches = lax.ppermute(matches.astype(BF16), EXPERT, partner)  22.1 us
    ppermute x3, waiting for transfers between devices, body(): arrived = lax.ppermute(value, 'dp', [(i, i ^ k + 1) for i in range(4)])  14.6 us
    all_to_all x2, waiting for transfers between devices, exchanged(): return lax.all_to_all(blocks, axes, 0, 0, tiled=True).reshape(rows, width)  14.4 us
    all_to_all x2, starting transfers between devices, exchanged(): return lax.all_to_all(blocks, axes, 0, 0, tiled=True).reshape(rows, width)  12.4 us
    ppermute x3, starting transfers between devices, body(): arrived = lax.ppermute(value, 'dp', [(i, i ^ k + 1) for i in range(4)])  5.58 us
    ppermute x1, waiting for transfers between devices, body(): keys = lax.ppermute(unit, EXPERT, partner)  5.1 us
  transfers between devices with their start and end apart: 9, of which 9 were waited for; matrix products, arithmetic and copies ran while one was open for 2% of the time, Pallas kernels for 8%

profile of v4, /device:TPU:0, one launch (start us, length us, event | category | flops | bytes accessed | tf_op | source)
XLA Modules:
  0.0 174.1 jit_solution(6003311448709903391)
XLA Ops:
  0.6 3.2 %shard_map.94 = bf16[512,2560]{1,0:T(8,128)(2,1)} custom-call(s32[4,128]{1,0:T(4,128)} %bitcast.27, bf16[128,2048]{1,0:T(8,128)(2,1)} %tokens_ref.1), custom_call_target="tpu_custom_call" | custom-call | flops 536870912 | bytes 3145728 | tf_op jit(solution)/shard_map/pallas_call | solution.py:391
  3.9 0.0 copy-start.6
  3.9 7.5 %all-to-all-start = ((bf16[32,16,2560]{2,1,0:T(8,128)(2,1)}), bf16[32,16,2560]{2,1,0:T(8,128)(2,1)}, u32[]{:S(2)}, u32[]{:S(2)}) async-start(bf16[32,16,2560]{2,1,0:T(8,128)(2,1)} %bitcast.37), calls=%async_computation | async-start | bytes 5242880 | tf_op jit(solution)/shard_map/all_to_all | solution.py:405
  11.4 0.0 copy-done.6
  11.5 3.3 %collective-permute-start = (bf16[1,128]{1,0:T(2,128)(2,1)S(1)}, bf16[1,128]{1,0:T(2,128)(2,1)S(1)}, u32[]{:S(2)}, u32[]{:S(2)}) collective-permute-start(bf16[1,128]{1,0:T(2,128)(2,1)S(1)} %convert_element_type.18), channel_id=1, source_target_pairs={{0,16},{1,17},{2,18},{3,19},{4,20},{5,21},{6,22},{7,23},{8,24},{9,... | collective-permute-start | bytes 776 | tf_op jit(solution)/shard_map/ppermute | solution.py:427
  14.8 7.8 %shard_map.95 = (bf16[1408,512]{1,0:T(8,128)(2,1)}, f32[128,512]{1,0:T(8,128)}) custom-call(bf16[1408,2048]{1,0:T(8,128)(2,1)} %bitcast.18, bf16[2048,512]{1,0:T(8,128)(2,1)} %head_hbm.1, bf16[128,2048]{1,0:T(8,128)(2,1)} %tokens_ref.1), custom_call_target="tpu_custom_call" | custom-call | flops 3221225472 | bytes 8388608 | tf_op jit(solution)/shard_map/pallas_call | solution.py:391
  22.6 22.1 %collective-permute-done.partner_ref = bf16[1,128]{1,0:T(2,128)(2,1)S(1)} collective-permute-done((bf16[1,128]{1,0:T(2,128)(2,1)S(1)}, bf16[1,128]{1,0:T(2,128)(2,1)S(1)}, u32[]{:S(2)}, u32[]{:S(2)}) %collective-permute-start) | collective-permute-done | bytes 288 | tf_op jit(solution)/shard_map/ppermute | solution.py:427
  44.6 1.4 all-to-all-done
  46.1 0.0 slice-start.1
  46.1 15.7 %shard_map.96 = (bf16[512,640]{1,0:T(8,128)(2,1)}, bf16[640,1408]{1,0:T(8,128)(2,1)}, bf16[640,2816]{1,0:T(8,128)(2,1)}) custom-call(bf16[512,2560]{1,0:T(8,128)(2,1)} %bitcast.3.recv_ref, bf16[2048,2816]{1,0:T(8,128)(2,1)} %bitcast.33, bf16[1408,512]{1,0:T(8,128)(2,1)} %get-tuple-element.30.mixed_hbm.mixed_ref), custom_call_target="tpu_custom_call" | custom-call | flops 8304721920 | bytes 23068672 | tf_op jit(solution)/shard_map/pallas_call | solution.py:391
  61.8 0.0 copy-start.1
  61.8 16.7 %all_to_all.25 = bf16[32,16,640]{2,1,0:T(8,128)(2,1)S(1)} all-to-all(bf16[32,16,640]{2,1,0:T(8,128)(2,1)} %bitcast.38), channel_id=1, replica_groups=mesh['dp'=4,'expert_0'=4,'expert_1'=4,'expert_2'=2] {'expert_0','expert_..., dimensions={0} | all-to-all | bytes 1310720 | tf_op jit(solution)/shard_map/all_to_all | solution.py:405
  78.5 0.0 copy-done.4
  78.5 0.0 copy-done.5
  78.5 0.0 copy-done.7
  78.5 0.9 shard_map.97
  79.4 1.8 %collective-permute-start.1 = (bf16[128,512]{1,0:T(8,128)(2,1)S(1)}, bf16[128,512]{1,0:T(8,128)(2,1)S(1)}, u32[]{:S(2)}, u32[]{:S(2)}) collective-permute-start(bf16[128,512]{1,0:T(8,128)(2,1)S(1)} %get-tuple-element.34._.unit_ref), channel_id=1, source_target_pairs={{0,16},{1,17},{2,18},{3,19},{4,20},{5,21},{6,22},{7,23},{8,24},{9,... | collective-permute-start | bytes 393224 | tf_op jit(solution)/shard_map/ppermute | solution.py:467
  81.2 0.0 slice-done
  81.2 0.0 slice-done.1
  81.2 0.8 shard_map.98
  82.0 0.0 copy-start.3
  82.0 5.1 %collective-permute-done.1.key_ref = bf16[128,512]{1,0:T(8,128)(2,1)S(1)} collective-permute-done((bf16[128,512]{1,0:T(8,128)(2,1)S(1)}, bf16[128,512]{1,0:T(8,128)(2,1)S(1)}, u32[]{:S(2)}, u32[]{:S(2)}) %collective-permute-start.1) | collective-permute-done | bytes 131104 | tf_op jit(solution)/shard_map/ppermute | solution.py:467
  87.1 1.1 shard_map.99
  88.2 16.1 %all_to_all.26 = bf16[32,16,640]{2,1,0:T(8,128)(2,1)S(1)} all-to-all(bf16[32,16,640]{2,1,0:T(8,128)(2,1)S(1)} %bitcast.24), channel_id=1, replica_groups=mesh['dp'=4,'expert_0'=4,'expert_1'=4,'expert_2'=2] {'expert_0','expert_..., dimensions={0} | all-to-all | bytes 1310720 | tf_op jit(solution)/shard_map/all_to_all | solution.py:405
  104.3 0.0 copy-done.3
  104.3 5.2 %shard_map.100 = (bf16[640,512]{1,0:T(8,128)(2,1)S(1)}, f32[1024,512]{1,0:T(8,128)S(1)}, bf16[1024,512]{1,0:T(8,128)(2,1)S(1)}) custom-call(bf16[512,640]{1,0:T(8,128)(2,1)S(1)} %bitcast.25, bf16[128,2048]{1,0:T(8,128)(2,1)S(1)} %copy-done.3, bf16[128,512]{1,0:T(8,128)(2,1)S(1)} %get-tuple-element.37.embed_grad_ref, ...), custom_call_target="tpu_custom_call" | custom-call | flops 3875536896 | bytes 12582912 | tf_op jit(solution)/shard_map/pallas_call | solution.py:391
  109.6 1.0 collective-permute-start.2
  110.5 0.0 copy-done
  110.6 1.3 shard_map.101.joined_ref
  111.9 1.0 collective-permute-done.2._
  112.8 0.0 slice-done.3
  112.8 9.2 %shard_map.102 = bf16[512,2560]{1,0:T(8,128)(2,1)} custom-call(bf16[640,2816]{1,0:T(8,128)(2,1)S(1)} %shard_map.101.joined_ref, bf16[2048,2816]{1,0:T(8,128)(2,1)S(1)} %bitcast.36, bf16[1024,512]{1,0:T(8,128)(2,1)S(1)} %collective-permute-done.2._), custom_call_target="tpu_custom_call" | custom-call | flops 7381975040 | bytes 18874368 | tf_op jit(solution)/shard_map/pallas_call | solution.py:391
  122.0 4.8 %all-to-all-start.3 = ((bf16[32,16,2560]{2,1,0:T(8,128)(2,1)}), bf16[32,16,2560]{2,1,0:T(8,128)(2,1)}, u32[]{:S(2)}, u32[]{:S(2)}) async-start(bf16[32,16,2560]{2,1,0:T(8,128)(2,1)} %bitcast.10), calls=%async_computation.3 | async-start | bytes 5242880 | tf_op jit(solution)/shard_map/all_to_all | solution.py:405
  126.8 0.6 shard_map.103
  127.4 0.0 copy-start.8
  127.4 2.0 %collective-permute-start.3 = (bf16[256,512]{1,0:T(8,128)(2,1)S(1)}, bf16[256,512]{1,0:T(8,128)(2,1)S(1)}, u32[]{:S(2)}, u32[]{:S(2)}) collective-permute-start(bf16[256,512]{1,0:T(8,128)(2,1)S(1)} %get-tuple-element.45), channel_id=1, source_target_pairs={{0,32},{32,0},{64,96},{96,64},{1,33},{33,1},{65,97},{97,65},{2,34}... | collective-permute-start | bytes 786440 | tf_op jit(solution)/shard_map/ppermute | solution.py:528
  129.4 3.6 %collective-permute-start.4 = (bf16[256,512]{1,0:T(8,128)(2,1)S(1)}, bf16[256,512]{1,0:T(8,128)(2,1)S(1)}, u32[]{:S(2)}, u32[]{:S(2)}) collective-permute-start(bf16[256,512]{1,0:T(8,128)(2,1)S(1)} %get-tuple-element.46), channel_id=1, source_target_pairs={{0,64},{32,96},{64,0},{96,32},{1,65},{33,97},{65,1},{97,33},{2,66}... | collective-permute-start | bytes 786440 | tf_op jit(solution)/shard_map/ppermute | solution.py:528
  133.0 0.0 collective-permute-start.5
  133.0 3.6 %collective-permute-done.3 = bf16[256,512]{1,0:T(8,128)(2,1)S(1)} collective-permute-done((bf16[256,512]{1,0:T(8,128)(2,1)S(1)}, bf16[256,512]{1,0:T(8,128)(2,1)S(1)}, u32[]{:S(2)}, u32[]{:S(2)}) %collective-permute-start.3) | collective-permute-done | bytes 262176 | tf_op jit(solution)/shard_map/ppermute | solution.py:528
  136.6 8.4 %collective-permute-done.4 = bf16[256,512]{1,0:T(8,128)(2,1)S(1)} collective-permute-done((bf16[256,512]{1,0:T(8,128)(2,1)S(1)}, bf16[256,512]{1,0:T(8,128)(2,1)S(1)}, u32[]{:S(2)}, u32[]{:S(2)}) %collective-permute-start.4) | collective-permute-done | bytes 262176 | tf_op jit(solution)/shard_map/ppermute | solution.py:528
  145.1 2.6 %collective-permute-done.5 = bf16[256,512]{1,0:T(8,128)(2,1)S(1)} collective-permute-done((bf16[256,512]{1,0:T(8,128)(2,1)S(1)}, bf16[256,512]{1,0:T(8,128)(2,1)S(1)}, u32[]{:S(2)}, u32[]{:S(2)}) %collective-permute-start.5) | collective-permute-done | bytes 262176 | tf_op jit(solution)/shard_map/ppermute | solution.py:528
  147.7 0.8 add_convert_fusion
  148.5 13.0 %all-to-all-done.3 = bf16[32,16,2560]{2,1,0:T(8,128)(2,1)} async-done(((bf16[32,16,2560]{2,1,0:T(8,128)(2,1)}), bf16[32,16,2560]{2,1,0:T(8,128)(2,1)}, u32[]{:S(2)}, u32[]{:S(2)}) %all-to-all-start.3) | async-done | bytes 2621472 | tf_op jit(solution)/shard_map/all_to_all | solution.py:405
  161.5 3.5 %all-to-all-start.4 = ((bf16[16,16,512]{2,1,0:T(8,128)(2,1)}), bf16[16,16,512]{2,1,0:T(8,128)(2,1)S(1)}, u32[]{:S(2)}, u32[]{:S(2)}) async-start(bf16[16,16,512]{2,1,0:T(8,128)(2,1)} %bitcast.14), calls=%async_computation.4 | async-start | bytes 524288 | tf_op jit(solution)/shard_map/all_to_all | solution.py:531
  165.0 1.8 %fusion.direct_ref = f32[128,2048]{1,0:T(8,128)} fusion(bf16[128,512]{1,0:T(8,128)(2,1)S(1)} %get-tuple-element.37.embed_grad_ref, bf16[2048,512]{1,0:T(8,128)(2,1)S(1)} %copy-done.8), kind=kOutput, calls=%fused_computation.3 | convolution fusion | flops 268435456 | bytes 3276800 | tf_op jit(solution)/shard_map/dot_general | solution.py:44
  166.8 4.3 %shard_map.104 = bf16[128,2048]{1,0:T(8,128)(2,1)} custom-call(s32[4,128]{1,0:T(4,128)} %bitcast.28, f32[128,2048]{1,0:T(8,128)} %fusion.direct_ref, bf16[512,2560]{1,0:T(8,128)(2,1)} %bitcast.11.back_hbm), custom_call_target="tpu_custom_call" | custom-call | flops 536870912 | bytes 4194304 | tf_op jit(solution)/shard_map/pallas_call | solution.py:391
  171.1 2.4 %all-to-all-done.4 = bf16[16,16,512]{2,1,0:T(8,128)(2,1)S(1)} async-done(((bf16[16,16,512]{2,1,0:T(8,128)(2,1)}), bf16[16,16,512]{2,1,0:T(8,128)(2,1)S(1)}, u32[]{:S(2)}, u32[]{:S(2)}) %all-to-all-start.4) | async-done | bytes 262176 | tf_op jit(solution)/shard_map/all_to_all | solution.py:531
  173.5 0.6 broadcast_multiply_fusion
  (18 shorter events, 0.1 us)
Async XLA Ops:
  3.9 7.6 %copy-start.6 = (s32[1,128]{1,0:T(1,128)S(1)}, s32[1,128]{1,0:T(1,128)}, u32[]{:S(2)}) copy-start(s32[1,128]{1,0:T(1,128)} %matches_ref.1) | copy-start | bytes 1540
  3.9 42.2 %all-to-all-start = ((bf16[32,16,2560]{2,1,0:T(8,128)(2,1)}), bf16[32,16,2560]{2,1,0:T(8,128)(2,1)}, u32[]{:S(2)}, u32[]{:S(2)}) async-start(bf16[32,16,2560]{2,1,0:T(8,128)(2,1)} %bitcast.37), calls=%async_computation | async-start | bytes 5242880 | tf_op jit(solution)/shard_map/all_to_all | solution.py:405
  11.5 33.2 %collective-permute-start = (bf16[1,128]{1,0:T(2,128)(2,1)S(1)}, bf16[1,128]{1,0:T(2,128)(2,1)S(1)}, u32[]{:S(2)}, u32[]{:S(2)}) collective-permute-start(bf16[1,128]{1,0:T(2,128)(2,1)S(1)} %convert_element_type.18), channel_id=1, source_target_pairs={{0,16},{1,17},{2,18},{3,19},{4,20},{5,21},{6,22},{7,23},{8,24},{9,... | collective-permute-start | bytes 776 | tf_op jit(solution)/shard_map/ppermute | solution.py:427
  46.1 35.1 %slice-start = ((s8[5767168]{0:T(1024)(128)(4,1)}), s8[4194304]{0:T(1024)(128)(4,1)S(1)}, s32[]{:S(2)}) async-start(s8[5767168]{0:T(1024)(128)(4,1)} %bitcast.19), calls=%async_computation.5 | async-start | bytes 8388608
  46.1 32.4 %copy-start.4 = (s32[128,4]{0,1:T(4,128)S(1)}, s32[128,4]{0,1:T(4,128)}, u32[]{:S(2)}) copy-start(s32[128,4]{0,1:T(4,128)} %param.8) | copy-start | bytes 6148
  46.1 32.4 %copy-start.5 = (f32[128,4]{0,1:T(4,128)S(1)}, f32[128,4]{0,1:T(4,128)}, u32[]{:S(2)}) copy-start(f32[128,4]{0,1:T(4,128)} %param.9) | copy-start | bytes 6148
  46.1 32.4 %copy-start.7 = (f32[128,512]{1,0:T(8,128)S(1)}, f32[128,512]{1,0:T(8,128)}, u32[]{:S(2)}) copy-start(f32[128,512]{1,0:T(8,128)} %get-tuple-element.32.base_ref) | copy-start | bytes 786436
  46.1 35.1 %slice-start.1 = ((s8[5767168]{0:T(1024)(128)(4,1)}), s8[1572864]{0:T(1024)(128)(4,1)S(1)}, s32[]{:S(2)}) async-start(s8[5767168]{0:T(1024)(128)(4,1)} %bitcast.19), calls=%async_computation.6 | async-start | bytes 3145728
  61.8 19.4 %copy-start.1 = (bf16[640,1408]{1,0:T(8,128)(2,1)S(1)}, bf16[640,1408]{1,0:T(8,128)(2,1)}, u32[]{:S(2)}) copy-start(bf16[640,1408]{1,0:T(8,128)(2,1)} %get-tuple-element.35.hidden_hbm) | copy-start | bytes 5406724
  79.4 7.7 %collective-permute-start.1 = (bf16[128,512]{1,0:T(8,128)(2,1)S(1)}, bf16[128,512]{1,0:T(8,128)(2,1)S(1)}, u32[]{:S(2)}, u32[]{:S(2)}) collective-permute-start(bf16[128,512]{1,0:T(8,128)(2,1)S(1)} %get-tuple-element.34._.unit_ref), channel_id=1, source_target_pairs={{0,16},{1,17},{2,18},{3,19},{4,20},{5,21},{6,22},{7,23},{8,24},{9,... | collective-permute-start | bytes 393224 | tf_op jit(solution)/shard_map/ppermute | solution.py:467
  82.0 22.3 %copy-start.3 = (bf16[128,2048]{1,0:T(8,128)(2,1)S(1)}, bf16[128,2048]{1,0:T(8,128)(2,1)}, u32[]{:S(2)}) copy-start(bf16[128,2048]{1,0:T(8,128)(2,1)} %tokens_ref.1) | copy-start | bytes 1572868
  87.1 25.7 %slice-start.2 = ((s8[11534336]{0:T(1024)(128)(4,1)}), s8[4194304]{0:T(1024)(128)(4,1)S(1)}, s32[]{:S(2)}) async-start(s8[11534336]{0:T(1024)(128)(4,1)} %bitcast.34), calls=%async_computation.7 | async-start | bytes 8388608
  104.3 6.2 %copy-start = (bf16[640,2816]{1,0:T(8,128)(2,1)S(1)}, bf16[640,2816]{1,0:T(8,128)(2,1)}, u32[]{:S(2)}) copy-start(bf16[640,2816]{1,0:T(8,128)(2,1)} %get-tuple-element.41.slopes_ref) | copy-start | bytes 10813444
  104.3 6.2 %copy-start.2 = (bf16[1408,512]{1,0:T(8,128)(2,1)S(1)}, bf16[1408,512]{1,0:T(8,128)(2,1)}, u32[]{:S(2)}) copy-start(bf16[1408,512]{1,0:T(8,128)(2,1)} %get-tuple-element.30.mixed_hbm.mixed_ref) | copy-start | bytes 4325380
  104.3 8.5 %slice-start.3 = ((s8[11534336]{0:T(1024)(128)(4,1)}), s8[4194304]{0:T(1024)(128)(4,1)S(1)}, s32[]{:S(2)}) async-start(s8[11534336]{0:T(1024)(128)(4,1)} %bitcast.34), calls=%async_computation.8 | async-start | bytes 8388608
  109.6 3.3 %collective-permute-start.2 = (bf16[1024,512]{1,0:T(8,128)(2,1)S(1)}, bf16[1024,512]{1,0:T(8,128)(2,1)S(1)}, u32[]{:S(2)}, u32[]{:S(2)}) collective-permute-start(bf16[1024,512]{1,0:T(8,128)(2,1)S(1)} %get-tuple-element.42), channel_id=1, source_target_pairs={{0,1},{1,0},{2,3},{3,2},{4,5},{5,4},{6,7},{7,6},{8,9},{9,8},{10,11... | collective-permute-start | bytes 3145736 | tf_op jit(solution)/shard_map/ppermute | solution.py:490
  110.6 2.3 %slice-start.4 = ((s8[11534336]{0:T(1024)(128)(4,1)}), s8[3145728]{0:T(1024)(128)(4,1)S(1)}, s32[]{:S(2)}) async-start(s8[11534336]{0:T(1024)(128)(4,1)} %bitcast.34), calls=%async_computation.9 | async-start | bytes 6291456
  122.0 39.4 %all-to-all-start.3 = ((bf16[32,16,2560]{2,1,0:T(8,128)(2,1)}), bf16[32,16,2560]{2,1,0:T(8,128)(2,1)}, u32[]{:S(2)}, u32[]{:S(2)}) async-start(bf16[32,16,2560]{2,1,0:T(8,128)(2,1)} %bitcast.10), calls=%async_computation.3 | async-start | bytes 5242880 | tf_op jit(solution)/shard_map/all_to_all | solution.py:405
  127.4 37.6 %copy-start.8 = (bf16[2048,512]{1,0:T(8,128)(2,1)S(1)}, bf16[2048,512]{1,0:T(8,128)(2,1)}, u32[]{:S(2)}) copy-start(bf16[2048,512]{1,0:T(8,128)(2,1)} %head_hbm.1) | copy-start | bytes 6291460
  127.4 9.2 %collective-permute-start.3 = (bf16[256,512]{1,0:T(8,128)(2,1)S(1)}, bf16[256,512]{1,0:T(8,128)(2,1)S(1)}, u32[]{:S(2)}, u32[]{:S(2)}) collective-permute-start(bf16[256,512]{1,0:T(8,128)(2,1)S(1)} %get-tuple-element.45), channel_id=1, source_target_pairs={{0,32},{32,0},{64,96},{96,64},{1,33},{33,1},{65,97},{97,65},{2,34}... | collective-permute-start | bytes 786440 | tf_op jit(solution)/shard_map/ppermute | solution.py:528
  129.4 15.7 %collective-permute-start.4 = (bf16[256,512]{1,0:T(8,128)(2,1)S(1)}, bf16[256,512]{1,0:T(8,128)(2,1)S(1)}, u32[]{:S(2)}, u32[]{:S(2)}) collective-permute-start(bf16[256,512]{1,0:T(8,128)(2,1)S(1)} %get-tuple-element.46), channel_id=1, source_target_pairs={{0,64},{32,96},{64,0},{96,32},{1,65},{33,97},{65,1},{97,33},{2,66}... | collective-permute-start | bytes 786440 | tf_op jit(solution)/shard_map/ppermute | solution.py:528
  133.0 14.6 %collective-permute-start.5 = (bf16[256,512]{1,0:T(8,128)(2,1)S(1)}, bf16[256,512]{1,0:T(8,128)(2,1)S(1)}, u32[]{:S(2)}, u32[]{:S(2)}) collective-permute-start(bf16[256,512]{1,0:T(8,128)(2,1)S(1)} %get-tuple-element.47), channel_id=1, source_target_pairs={{0,96},{32,64},{64,32},{96,0},{1,97},{33,65},{65,33},{97,1},{2,98}... | collective-permute-start | bytes 786440 | tf_op jit(solution)/shard_map/ppermute | solution.py:528
  161.5 12.0 %all-to-all-start.4 = ((bf16[16,16,512]{2,1,0:T(8,128)(2,1)}), bf16[16,16,512]{2,1,0:T(8,128)(2,1)S(1)}, u32[]{:S(2)}, u32[]{:S(2)}) async-start(bf16[16,16,512]{2,1,0:T(8,128)(2,1)} %bitcast.14), calls=%async_computation.4 | async-start | bytes 524288 | tf_op jit(solution)/shard_map/all_to_all | solution.py:531

commit v5 on v4

--- a/solution.py
+++ b/solution.py
@@ -140,8 +140,8 @@
 
 
 def forward_kernel(
-    recv_ref, w_hbm, mixed_hbm, out_hbm, hidden_hbm, slopes_hbm,
-    x_ref, act_ref, w_ref, mixed_ref, hidden_ref, slopes_ref, out_ref, sems, out_sems,
+    recv_hbm, w_hbm, mixed_hbm, out_hbm, hidden_hbm, slopes_hbm,
+    x_ref, extra_ref, act_ref, w_ref, mixed_ref, hidden_ref, slopes_ref, out_ref, sems, out_sems,
 ):
     quarter = WIDTH // 4
 
@@ -150,6 +150,8 @@
         copy.start()
         return copy
 
+    extra_copy = bring(recv_hbm.at[:, pl.ds(WIDTH, quarter)], extra_ref, 7)
+    main_copy = bring(recv_hbm.at[:, pl.ds(0, WIDTH)], x_ref.at[pl.ds(0, SLOTS), :], 8)
     groups = ((0, 1), (1, 3), (3, len(CHUNKS)))
     weight_copies = []
     for g, (begin, end) in enumerate(groups):
@@ -158,10 +160,12 @@
             cols = pl.ds(h * HIDDEN + lo, hi - lo)
             weight_copies.append(bring(w_hbm.at[:, cols], w_ref.at[:, cols], 1 + 2 * g + h))
     mixed_copy = bring(mixed_hbm, mixed_ref, 0)
-    x_ref[:SLOTS, :] = recv_ref[:, :WIDTH]
-    spread = dot(unpacker(), recv_ref[:, WIDTH:]).astype(BF16)
+    turned = unpacker()
+    extra_copy.wait()
+    spread = dot(turned, extra_ref[...]).astype(BF16)
     for j in range(4):
         x_ref[SLOTS:, j * quarter : (j + 1) * quarter] = spread[j * SPARE : (j + 1) * SPARE]
+    main_copy.wait()
     outgoing = []
 
     def send(source, target, lo, wide):
@@ -312,27 +316,39 @@
                 joined_ref[m : m + 64, offset + lo : offset + hi] = (hidden_grad * slope).astype(BF16)
 
 
-def input_kernel(joined_ref, w_ref, _, out_hbm, extra_ref, out_ref, out_sems):
+def input_tiles(joined_ref, w_ref, begin, end, out_ref, extra_ref):
     step = WIDTH // 4
-    outgoing = []
-
-    def send(start, wide, index):
-        cols = pl.ds(start, wide)
-        copy = pltpu.make_async_copy(out_ref.at[:, cols], out_hbm.at[:, cols], out_sems.at[index])
-        copy.start()
-        outgoing.append(copy)
-
-    for n in range(0, WIDTH, TILE):
+    for n in range(begin, end, TILE):
         result = dot_cols(joined_ref[...], w_ref[n : n + TILE, :]).astype(BF16)
-        out_ref[:, n : n + TILE] = result[:SLOTS]
-        j, within = n // step, n % step
+        out_ref[:, n - begin : n - begin + TILE] = result[:SLOTS]
+        j, within = (n - begin) // step, n % step
         extra_ref[j * SPARE : (j + 1) * SPARE, within : within + TILE] = result[SLOTS:]
-        if n == WIDTH // 2 - TILE:
-            send(0, WIDTH // 2, 0)
-    out_ref[:, WIDTH:] = dot(packer(), extra_ref[...]).astype(BF16)
-    send(WIDTH // 2, WIDTH // 2 + step, 1)
-    for copy in outgoing:
-        copy.wait()
+
+
+def input_kernel(joined_ref, w_ref, out_ref, extra_ref):
+    input_tiles(joined_ref, w_ref, 0, WIDTH * 3 // 4, out_ref, extra_ref)
+
+
+def last_input_kernel(joined_ref, w_ref, first_ref, extra_ref, *refs):
+    out_hbm, last_ref, stacked_ref, sems = refs[-4:]
+    split = WIDTH * 3 // 4
+
+    def send(source, begin, wide, index):
+        copy = pltpu.make_async_copy(source, out_hbm.at[:, pl.ds(begin, wide)], sems.at[index])
+        copy.start()
+        return copy
+
+    first = send(first_ref, 0, split, 0)
+    step = WIDTH // 4
+    stacked_ref[: 3 * SPARE, :] = extra_ref[...]
+    input_tiles(
+        joined_ref, w_ref, split, WIDTH, last_ref.at[:, pl.ds(0, step)],
+        stacked_ref.at[pl.ds(3 * SPARE, SPARE), :],
+    )
+    last_ref[:, step:] = dot(packer(), stacked_ref[...]).astype(BF16)
+    last = send(last_ref, split, 2 * step, 1)
+    first.wait()
+    last.wait()
 
 
 def share_kernel(axis, count, own_hbm, *refs):
@@ -443,16 +459,17 @@
     packed, hidden, slopes = call(
         forward_kernel,
         [(packed_shape, BF16, hbm), ((TOTAL, HIDDEN), BF16, hbm), ((TOTAL, 2 * HIDDEN), BF16, hbm)],
-        [(received, vmem), (weights_joined, hbm), (mixed, hbm)],
+        [(received, hbm), (weights_joined, hbm), (mixed, hbm)],
         scratch=[
             pltpu.VMEM((TOTAL, WIDTH), BF16),
+            pltpu.VMEM((SLOTS, WIDTH // 4), BF16),
             pltpu.VMEM((2, 2, TOTAL, 256), F32),
             pltpu.VMEM((WIDTH, 2 * HIDDEN), BF16),
             pltpu.VMEM((HIDDEN, EMBED), BF16),
             pltpu.VMEM((TOTAL, HIDDEN), BF16),
             pltpu.VMEM((TOTAL, 2 * HIDDEN), BF16),
             pltpu.VMEM(packed_shape, BF16),
-            dma((7,)),
+            dma((9,)),
             dma((10,)),
         ],
         flops=2 * TOTAL * HIDDEN * (2 * WIDTH + EMBED), moved=22 << 20, limit=56.5,
@@ -496,48 +513,61 @@
         scratch=[pltpu.VMEM((2, TOTAL, 256), F32)],
         flops=2 * TOTAL * HIDDEN * EMBED, moved=8 << 20, limit=16,
     )
+
+    def shared(axis, own, arrivals):
+        rows, count = own.shape[0] // 4, len(arrivals)
+        own, *sent = call(
+            functools.partial(share_kernel, axis, count),
+            [((rows, EMBED), F32, hbm)] + [((rows, EMBED), BF16, hbm)] * 3,
+            [(value.reshape(4, rows, EMBED), hbm) for value in (own, *arrivals)],
+            scratch=[
+                pltpu.VMEM((4, rows, EMBED), F32),
+                pltpu.VMEM((count, 4, rows, EMBED), BF16),
+                pltpu.VMEM((rows, EMBED), F32),
+                pltpu.VMEM((3, rows, EMBED), BF16),
+                dma((1 + count,)),
+                dma((4,)),
+            ],
+            limit=16,
+        )
+        return own, [
+            lax.ppermute(value, axis, [(i, i ^ (k + 1)) for i in range(4)])
+            for k, value in enumerate(sent)
+        ]
+
+    own, arrivals = shared("dp", own, arrivals)
+    split = WIDTH * 3 // 4
+    first_grads, extra_grads = call(
+        input_kernel,
+        [((SLOTS, split), BF16, vmem), ((3 * SPARE, WIDTH // 4), BF16, vmem)],
+        [(joined_grad, vmem), (weights_joined, vmem)],
+        flops=3 * TOTAL * HIDDEN * WIDTH, moved=14 << 20, limit=34,
+    )
     (input_grads,) = call(
-        input_kernel,
+        last_input_kernel,
         [(wide_shape, BF16, hbm)],
-        [(joined_grad, vmem), (weights_joined, vmem), (arrivals[0], hbm)],
+        [(joined_grad, vmem), (weights_joined, vmem), (first_grads, vmem), (extra_grads, vmem)]
+        + [(value, hbm) for value in arrivals],
         scratch=[
+            pltpu.VMEM((SLOTS, WIDTH // 2), BF16),
             pltpu.VMEM((SLOTS, WIDTH // 4), BF16),
-            pltpu.VMEM(wide_shape, BF16),
             dma((2,)),
         ],
-        flops=4 * TOTAL * HIDDEN * WIDTH, moved=18 << 20, limit=34,
+        flops=TOTAL * HIDDEN * WIDTH, moved=6 << 20, limit=34,
     )
     back = exchanged(input_grads, EXPERT, EXPERTS)
     direct = dot_cols(embed_grad, projection)
-    rows = own.shape[0] // 4
-    own, *sent = call(
-        functools.partial(share_kernel, "dp", 1),
-        [((rows, EMBED), F32, hbm)] + [((rows, EMBED), BF16, hbm)] * 3,
-        [(value.reshape(4, rows, EMBED), hbm) for value in (own, *arrivals)],
-        scratch=[
-            pltpu.VMEM((4, rows, EMBED), F32),
-            pltpu.VMEM((1, 4, rows, EMBED), BF16),
-            pltpu.VMEM((rows, EMBED), F32),
-            pltpu.VMEM((3, rows, EMBED), BF16),
-            dma((2,)),
-            dma((4,)),
-        ],
-        limit=16,
-    )
-    for k, value in enumerate(sent):
-        arrived = lax.ppermute(value, "dp", [(i, i ^ (k + 1)) for i in range(4)])
-        own = own + arrived.astype(F32)
-    back, sums = lax.optimization_barrier((back, own.astype(BF16)))
-    parts = lax.all_to_all(
-        sums.reshape(16, 16, EMBED), ("expert_0", "expert_1"), 0, 0, tiled=True
-    )
+    for axis in ("expert_0", "expert_1"):
+        own, arrivals = shared(axis, own, arrivals)
+    for value in arrivals:
+        own = own + value.astype(F32)
+    device_count = lax.axis_size("dp") * EXPERTS
+    grad_projection = own * (1.0 / math.sqrt(ROWS * device_count))
     (grad_tokens,) = call(
         combine_kernel, [((ROWS, WIDTH), BF16, vmem)], [(routes, vmem), (direct, vmem), (back, hbm)],
         scratch=[pltpu.VMEM(wide_shape, BF16), dma((5,))],
         flops=2 * SLOTS * ROWS * WIDTH * 2, moved=4 << 20, limit=WHOLE,
     )
-    device_count = lax.axis_size("dp") * EXPERTS
-    grad_projection = jnp.sum(parts.astype(F32), axis=0) * (1.0 / math.sqrt(ROWS * device_count))
     return grad_tokens, grad_projection, row_loss.reshape(ROWS)
 
 

time: 175 us -> 191 us (1.091)
  waiting for transfers between devices: 59.5 us -> 71 us
  starting transfers between devices: 27.5 us -> 33.5 us
    ppermute x3 -> x9, waiting for transfers between devices: 14.6 us -> 41.4 us  [shared(): lax.ppermute(value, axis, [(i, i ^ k + 1) for i in range(4)])]
    all_to_all x2, waiting for transfers between devices: 14.4 us -> 1.45 us  [exchanged(): return lax.all_to_all(blocks, axes, 0, 0, tiled=True).reshape(rows, width)]
    ppermute x3 -> x9, starting transfers between devices: 5.58 us -> 15.2 us  [shared(): lax.ppermute(value, axis, [(i, i ^ k + 1) for i in range(4)])]
    all_to_all x1 -> x0, starting transfers between devices: 3.53 us -> none  [body(): lax.all_to_all(sums.reshape(16, 16, EMBED), ('expert_0', 'expert_1'), 0,...]
    all_to_all x1 -> x0, waiting for transfers between devices: 2.38 us -> none  [body(): lax.all_to_all(sums.reshape(16, 16, EMBED), ('expert_0', 'expert_1'), 0,...]
    pallas_call x11 -> x14, Pallas kernels: 50.1 us -> 50.3 us  [call(): pl.pallas_call(kernel, out_shape=tuple((jax.ShapeDtypeStruct(shape, dtype...]
  transfers between devices with their start and end apart: 9 -> 14, of which waited for: 9 -> 10; matrix products, arithmetic and copies ran while one was open for 2% -> 1% of each run, Pallas kernels for 8% -> 9%
where the time goes in v5:
time: 191 us
  waiting for transfers between devices  71 us (37%)
  Pallas kernels  50.3 us (26%)
  starting transfers between devices  33.5 us (18%)
  blocking collectives  32.6 us (17%)
    pallas_call x14, Pallas kernels, call(): pl.pallas_call(kernel, out_shape=tuple((jax.ShapeDtypeStruct(shape, dtype...  50.3 us
    ppermute x9, waiting for transfers between devices, shared(): lax.ppermute(value, axis, [(i, i ^ k + 1) for i in range(4)])  41.4 us
    all_to_all x2, blocking collectives, exchanged(): return lax.all_to_all(blocks, axes, 0, 0, tiled=True).reshape(rows, width)  32.6 us
    ppermute x1, waiting for transfers between devices, body(): partner_matches = lax.ppermute(matches.astype(BF16), EXPERT, partner)  22.1 us
    ppermute x9, starting transfers between devices, shared(): lax.ppermute(value, axis, [(i, i ^ k + 1) for i in range(4)])  15.2 us
    all_to_all x2, starting transfers between devices, exchanged(): return lax.all_to_all(blocks, axes, 0, 0, tiled=True).reshape(rows, width)  12.5 us
    ppermute x1, waiting for transfers between devices, body(): keys = lax.ppermute(unit, EXPERT, partner)  5.1 us
  transfers between devices with their start and end apart: 14, of which 10 were waited for; matrix products, arithmetic and copies ran while one was open for 1% of the time, Pallas kernels for 9%

profile of v5, /device:TPU:0, one launch (start us, length us, event | category | flops | bytes accessed | tf_op | source)
XLA Modules:
  0.0 190.9 jit_solution(7627667359315039891)
XLA Ops:
  0.6 3.2 %shard_map.94 = bf16[512,2560]{1,0:T(8,128)(2,1)} custom-call(s32[4,128]{1,0:T(4,128)} %bitcast.47, bf16[128,2048]{1,0:T(8,128)(2,1)} %tokens_ref.1), custom_call_target="tpu_custom_call" | custom-call | flops 536870912 | bytes 3145728 | tf_op jit(solution)/shard_map/pallas_call | solution.py:407
  3.9 0.0 copy-start.6
  3.9 7.5 %all-to-all-start = ((bf16[32,16,2560]{2,1,0:T(8,128)(2,1)}), bf16[32,16,2560]{2,1,0:T(8,128)(2,1)}, u32[]{:S(2)}, u32[]{:S(2)}) async-start(bf16[32,16,2560]{2,1,0:T(8,128)(2,1)} %bitcast.53), calls=%async_computation | async-start | bytes 5242880 | tf_op jit(solution)/shard_map/all_to_all | solution.py:421
  11.5 3.3 %collective-permute-start = (bf16[1,128]{1,0:T(2,128)(2,1)S(1)}, bf16[1,128]{1,0:T(2,128)(2,1)S(1)}, u32[]{:S(2)}, u32[]{:S(2)}) collective-permute-start(bf16[1,128]{1,0:T(2,128)(2,1)S(1)} %convert_element_type.12), channel_id=1, source_target_pairs={{0,16},{1,17},{2,18},{3,19},{4,20},{5,21},{6,22},{7,23},{8,24},{9,... | collective-permute-start | bytes 776 | tf_op jit(solution)/shard_map/ppermute | solution.py:443
  14.8 7.8 %shard_map.95 = (bf16[1408,512]{1,0:T(8,128)(2,1)}, f32[128,512]{1,0:T(8,128)}) custom-call(bf16[1408,2048]{1,0:T(8,128)(2,1)} %bitcast.30, bf16[2048,512]{1,0:T(8,128)(2,1)} %head_hbm.1, bf16[128,2048]{1,0:T(8,128)(2,1)} %tokens_ref.1), custom_call_target="tpu_custom_call" | custom-call | flops 3221225472 | bytes 8388608 | tf_op jit(solution)/shard_map/pallas_call | solution.py:407
  22.6 22.1 %collective-permute-done.partner_ref = bf16[1,128]{1,0:T(2,128)(2,1)S(1)} collective-permute-done((bf16[1,128]{1,0:T(2,128)(2,1)S(1)}, bf16[1,128]{1,0:T(2,128)(2,1)S(1)}, u32[]{:S(2)}, u32[]{:S(2)}) %collective-permute-start) | collective-permute-done | bytes 288 | tf_op jit(solution)/shard_map/ppermute | solution.py:443
  44.6 1.4 all-to-all-done
  46.1 14.6 %shard_map.96 = (bf16[512,640]{1,0:T(8,128)(2,1)}, bf16[640,1408]{1,0:T(8,128)(2,1)}, bf16[640,2816]{1,0:T(8,128)(2,1)}) custom-call(bf16[512,2560]{1,0:T(8,128)(2,1)} %bitcast.3.recv_hbm, bf16[2048,2816]{1,0:T(8,128)(2,1)} %bitcast.25, bf16[1408,512]{1,0:T(8,128)(2,1)} %get-tuple-element.38.mixed_hbm.mixed_ref), custom_call_target="tpu_custom_call" | custom-call | flops 8304721920 | bytes 23068672 | tf_op jit(solution)/shard_map/pallas_call | solution.py:407
  60.7 16.7 %all_to_all.20 = bf16[32,16,640]{2,1,0:T(8,128)(2,1)S(1)} all-to-all(bf16[32,16,640]{2,1,0:T(8,128)(2,1)} %bitcast.54), channel_id=1, replica_groups=mesh['dp'=4,'expert_0'=4,'expert_1'=4,'expert_2'=2] {'expert_0','expert_..., dimensions={0} | all-to-all | bytes 1310720 | tf_op jit(solution)/shard_map/all_to_all | solution.py:421
  77.4 0.9 shard_map.97
  78.3 1.8 collective-permute-start.1
  80.1 0.8 shard_map.98
  80.9 0.0 copy-start.3
  80.9 5.1 %collective-permute-done.1.key_ref = bf16[128,512]{1,0:T(8,128)(2,1)S(1)} collective-permute-done((bf16[128,512]{1,0:T(8,128)(2,1)S(1)}, bf16[128,512]{1,0:T(8,128)(2,1)S(1)}, u32[]{:S(2)}, u32[]{:S(2)}) %collective-permute-start.1) | collective-permute-done | bytes 131104 | tf_op jit(solution)/shard_map/ppermute | solution.py:484
  86.0 1.1 shard_map.99
  87.1 15.9 %all_to_all.21 = bf16[32,16,640]{2,1,0:T(8,128)(2,1)S(1)} all-to-all(bf16[32,16,640]{2,1,0:T(8,128)(2,1)S(1)} %bitcast.39), channel_id=1, replica_groups=mesh['dp'=4,'expert_0'=4,'expert_1'=4,'expert_2'=2] {'expert_0','expert_..., dimensions={0} | all-to-all | bytes 1310720 | tf_op jit(solution)/shard_map/all_to_all | solution.py:421
  103.1 5.2 %shard_map.100 = (bf16[640,512]{1,0:T(8,128)(2,1)S(1)}, f32[1024,512]{1,0:T(8,128)S(1)}, bf16[1024,512]{1,0:T(8,128)(2,1)S(1)}) custom-call(bf16[512,640]{1,0:T(8,128)(2,1)S(1)} %bitcast.40, bf16[128,2048]{1,0:T(8,128)(2,1)S(1)} %copy-done.3, bf16[128,512]{1,0:T(8,128)(2,1)S(1)} %get-tuple-element.45.embed_grad_ref, ...), custom_call_target="tpu_custom_call" | custom-call | flops 3875536896 | bytes 12582912 | tf_op jit(solution)/shard_map/pallas_call | solution.py:407
  108.3 0.8 collective-permute-start.2
  109.1 1.3 shard_map.101.joined_ref
  110.4 1.0 collective-permute-done.2
  111.4 0.6 shard_map.103
  112.0 2.0 %collective-permute-start.3 = (bf16[256,512]{1,0:T(8,128)(2,1)S(1)}, bf16[256,512]{1,0:T(8,128)(2,1)S(1)}, u32[]{:S(2)}, u32[]{:S(2)}) collective-permute-start(bf16[256,512]{1,0:T(8,128)(2,1)S(1)} %get-tuple-element.54), channel_id=1, source_target_pairs={{0,32},{32,0},{64,96},{96,64},{1,33},{33,1},{65,97},{97,65},{2,34}... | collective-permute-start | bytes 786440 | tf_op jit(solution)/shard_map/ppermute | solution.py:534
  114.0 3.6 %collective-permute-start.4 = (bf16[256,512]{1,0:T(8,128)(2,1)S(1)}, bf16[256,512]{1,0:T(8,128)(2,1)S(1)}, u32[]{:S(2)}, u32[]{:S(2)}) collective-permute-start(bf16[256,512]{1,0:T(8,128)(2,1)S(1)} %get-tuple-element.55), channel_id=1, source_target_pairs={{0,64},{32,96},{64,0},{96,32},{1,65},{33,97},{65,1},{97,33},{2,66}... | collective-permute-start | bytes 786440 | tf_op jit(solution)/shard_map/ppermute | solution.py:534
  117.6 0.0 collective-permute-start.5
  117.6 5.8 %shard_map.102 = (bf16[512,1536]{1,0:T(8,128)(2,1)S(1)}, bf16[384,512]{1,0:T(8,128)(2,1)S(1)}) custom-call(bf16[640,2816]{1,0:T(8,128)(2,1)S(1)} %shard_map.101.joined_ref, bf16[2048,2816]{1,0:T(8,128)(2,1)S(1)} %bitcast.28), custom_call_target="tpu_custom_call" | custom-call | flops 5536481280 | bytes 14680064 | tf_op jit(solution)/shard_map/pallas_call | solution.py:407
  123.4 0.0 collective-permute-done.3.refs_0_
  123.4 6.5 %collective-permute-done.4.refs_1_ = bf16[256,512]{1,0:T(8,128)(2,1)S(1)} collective-permute-done((bf16[256,512]{1,0:T(8,128)(2,1)S(1)}, bf16[256,512]{1,0:T(8,128)(2,1)S(1)}, u32[]{:S(2)}, u32[]{:S(2)}) %collective-permute-start.4) | collective-permute-done | bytes 262176 | tf_op jit(solution)/shard_map/ppermute | solution.py:534
  129.8 2.6 %collective-permute-done.5.refs_2_ = bf16[256,512]{1,0:T(8,128)(2,1)S(1)} collective-permute-done((bf16[256,512]{1,0:T(8,128)(2,1)S(1)}, bf16[256,512]{1,0:T(8,128)(2,1)S(1)}, u32[]{:S(2)}, u32[]{:S(2)}) %collective-permute-start.5) | collective-permute-done | bytes 262176 | tf_op jit(solution)/shard_map/ppermute | solution.py:534
  132.4 3.4 %shard_map.104 = bf16[512,2560]{1,0:T(8,128)(2,1)} custom-call(bf16[640,2816]{1,0:T(8,128)(2,1)S(1)} %shard_map.101.joined_ref, bf16[2048,2816]{1,0:T(8,128)(2,1)S(1)} %bitcast.29, bf16[512,1536]{1,0:T(8,128)(2,1)S(1)} %get-tuple-element.50.first_ref, bf16[384,512]{1,0:T(8,128)(2,1)S(1)} %get-tuple-element.51.extra_ref, ...), custom_call_target="tpu_custom_call" | custom-call | flops 1845493760 | bytes 6291456 | tf_op jit(solution)/shard_map/pallas_call | solution.py:407
  135.8 0.0 copy-start.8
  135.8 4.9 %all-to-all-start.3 = ((bf16[32,16,2560]{2,1,0:T(8,128)(2,1)}), bf16[32,16,2560]{2,1,0:T(8,128)(2,1)}, u32[]{:S(2)}, u32[]{:S(2)}) async-start(bf16[32,16,2560]{2,1,0:T(8,128)(2,1)} %bitcast.12), calls=%async_computation.3 | async-start | bytes 5242880 | tf_op jit(solution)/shard_map/all_to_all | solution.py:421
  140.7 0.7 shard_map.106
  141.5 1.7 collective-permute-start.6
  143.2 2.8 %collective-permute-start.7 = (bf16[64,512]{1,0:T(8,128)(2,1)S(1)}, bf16[64,512]{1,0:T(8,128)(2,1)S(1)}, u32[]{:S(2)}, u32[]{:S(2)}) collective-permute-start(bf16[64,512]{1,0:T(8,128)(2,1)S(1)} %get-tuple-element.60), channel_id=1, source_target_pairs={{0,16},{8,24},{16,0},{24,8},{1,17},{9,25},{17,1},{25,9},{2,18},{10... | collective-permute-start | bytes 196616 | tf_op jit(solution)/shard_map/ppermute | solution.py:534
  146.0 0.3 collective-permute-start.8
  146.3 28.3 %collective-permute-done.6 = bf16[64,512]{1,0:T(8,128)(2,1)S(1)} collective-permute-done((bf16[64,512]{1,0:T(8,128)(2,1)S(1)}, bf16[64,512]{1,0:T(8,128)(2,1)S(1)}, u32[]{:S(2)}, u32[]{:S(2)}) %collective-permute-start.6) | collective-permute-done | bytes 65568 | tf_op jit(solution)/shard_map/ppermute | solution.py:534
  174.6 2.0 %collective-permute-done.7 = bf16[64,512]{1,0:T(8,128)(2,1)S(1)} collective-permute-done((bf16[64,512]{1,0:T(8,128)(2,1)S(1)}, bf16[64,512]{1,0:T(8,128)(2,1)S(1)}, u32[]{:S(2)}, u32[]{:S(2)}) %collective-permute-start.7) | collective-permute-done | bytes 65568 | tf_op jit(solution)/shard_map/ppermute | solution.py:534
  176.6 0.0 collective-permute-done.8
  176.6 0.6 shard_map.107
  177.2 1.9 collective-permute-start.9
  179.1 1.8 collective-permute-start.10
  180.9 1.1 collective-permute-start.11
  182.0 1.8 fusion.direct_ref
  183.8 0.0 collective-permute-done.9
  183.8 0.5 collective-permute-done.10
  184.4 1.5 collective-permute-done.11
  185.9 0.6 add_multiply_fusion
  186.5 4.3 %shard_map.105 = bf16[128,2048]{1,0:T(8,128)(2,1)} custom-call(s32[4,128]{1,0:T(4,128)} %bitcast.48, f32[128,2048]{1,0:T(8,128)} %fusion.direct_ref, bf16[512,2560]{1,0:T(8,128)(2,1)} %bitcast.13.back_hbm), custom_call_target="tpu_custom_call" | custom-call | flops 536870912 | bytes 4194304 | tf_op jit(solution)/shard_map/pallas_call | solution.py:407
  (29 shorter events, 0.1 us)
Async XLA Ops:
  3.9 7.6 %copy-start.6 = (s32[1,128]{1,0:T(1,128)S(1)}, s32[1,128]{1,0:T(1,128)}, u32[]{:S(2)}) copy-start(s32[1,128]{1,0:T(1,128)} %matches_ref.1) | copy-start | bytes 1540
  3.9 42.2 %all-to-all-start = ((bf16[32,16,2560]{2,1,0:T(8,128)(2,1)}), bf16[32,16,2560]{2,1,0:T(8,128)(2,1)}, u32[]{:S(2)}, u32[]{:S(2)}) async-start(bf16[32,16,2560]{2,1,0:T(8,128)(2,1)} %bitcast.53), calls=%async_computation | async-start | bytes 5242880 | tf_op jit(solution)/shard_map/all_to_all | solution.py:421
  11.5 33.2 %collective-permute-start = (bf16[1,128]{1,0:T(2,128)(2,1)S(1)}, bf16[1,128]{1,0:T(2,128)(2,1)S(1)}, u32[]{:S(2)}, u32[]{:S(2)}) collective-permute-start(bf16[1,128]{1,0:T(2,128)(2,1)S(1)} %convert_element_type.12), channel_id=1, source_target_pairs={{0,16},{1,17},{2,18},{3,19},{4,20},{5,21},{6,22},{7,23},{8,24},{9,... | collective-permute-start | bytes 776 | tf_op jit(solution)/shard_map/ppermute | solution.py:443
  46.1 34.0 %slice-start.3 = ((s8[5767168]{0:T(1024)(128)(4,1)}), s8[4194304]{0:T(1024)(128)(4,1)S(1)}, s32[]{:S(2)}) async-start(s8[5767168]{0:T(1024)(128)(4,1)} %bitcast.31), calls=%async_computation.7 | async-start | bytes 8388608
  46.1 31.3 %copy-start.4 = (s32[128,4]{0,1:T(4,128)S(1)}, s32[128,4]{0,1:T(4,128)}, u32[]{:S(2)}) copy-start(s32[128,4]{0,1:T(4,128)} %param.8) | copy-start | bytes 6148
  46.1 31.3 %copy-start.5 = (f32[128,4]{0,1:T(4,128)S(1)}, f32[128,4]{0,1:T(4,128)}, u32[]{:S(2)}) copy-start(f32[128,4]{0,1:T(4,128)} %param.9) | copy-start | bytes 6148
  46.1 31.3 %copy-start.7 = (f32[128,512]{1,0:T(8,128)S(1)}, f32[128,512]{1,0:T(8,128)}, u32[]{:S(2)}) copy-start(f32[128,512]{1,0:T(8,128)} %get-tuple-element.40.base_ref) | copy-start | bytes 786436
  46.1 34.0 %slice-start.4 = ((s8[5767168]{0:T(1024)(128)(4,1)}), s8[1572864]{0:T(1024)(128)(4,1)S(1)}, s32[]{:S(2)}) async-start(s8[5767168]{0:T(1024)(128)(4,1)} %bitcast.31), calls=%async_computation.8 | async-start | bytes 3145728
  60.7 19.4 %copy-start.1 = (bf16[640,1408]{1,0:T(8,128)(2,1)S(1)}, bf16[640,1408]{1,0:T(8,128)(2,1)}, u32[]{:S(2)}) copy-start(bf16[640,1408]{1,0:T(8,128)(2,1)} %get-tuple-element.43.hidden_hbm) | copy-start | bytes 5406724
  78.3 7.7 %collective-permute-start.1 = (bf16[128,512]{1,0:T(8,128)(2,1)S(1)}, bf16[128,512]{1,0:T(8,128)(2,1)S(1)}, u32[]{:S(2)}, u32[]{:S(2)}) collective-permute-start(bf16[128,512]{1,0:T(8,128)(2,1)S(1)} %get-tuple-element.42._.unit_ref), channel_id=1, source_target_pairs={{0,16},{1,17},{2,18},{3,19},{4,20},{5,21},{6,22},{7,23},{8,24},{9,... | collective-permute-start | bytes 393224 | tf_op jit(solution)/shard_map/ppermute | solution.py:484
  80.9 22.1 %copy-start.3 = (bf16[128,2048]{1,0:T(8,128)(2,1)S(1)}, bf16[128,2048]{1,0:T(8,128)(2,1)}, u32[]{:S(2)}) copy-start(bf16[128,2048]{1,0:T(8,128)(2,1)} %tokens_ref.1) | copy-start | bytes 1572868
  103.1 6.0 %copy-start = (bf16[640,2816]{1,0:T(8,128)(2,1)S(1)}, bf16[640,2816]{1,0:T(8,128)(2,1)}, u32[]{:S(2)}) copy-start(bf16[640,2816]{1,0:T(8,128)(2,1)} %get-tuple-element.49.slopes_ref) | copy-start | bytes 10813444
  103.1 6.0 %copy-start.2 = (bf16[1408,512]{1,0:T(8,128)(2,1)S(1)}, bf16[1408,512]{1,0:T(8,128)(2,1)}, u32[]{:S(2)}) copy-start(bf16[1408,512]{1,0:T(8,128)(2,1)} %get-tuple-element.38.mixed_hbm.mixed_ref) | copy-start | bytes 4325380
  103.1 14.5 %slice-start = ((s8[11534336]{0:T(1024)(128)(4,1)}), s8[4194304]{0:T(1024)(128)(4,1)S(1)}, s32[]{:S(2)}) async-start(s8[11534336]{0:T(1024)(128)(4,1)} %bitcast.26), calls=%async_computation.4 | async-start | bytes 8388608
  103.1 14.5 %slice-start.1 = ((s8[11534336]{0:T(1024)(128)(4,1)}), s8[4194304]{0:T(1024)(128)(4,1)S(1)}, s32[]{:S(2)}) async-start(s8[11534336]{0:T(1024)(128)(4,1)} %bitcast.26), calls=%async_computation.5 | async-start | bytes 8388608
  108.3 3.0 %collective-permute-start.2 = (bf16[1024,512]{1,0:T(8,128)(2,1)S(1)}, bf16[1024,512]{1,0:T(8,128)(2,1)S(1)}, u32[]{:S(2)}, u32[]{:S(2)}) collective-permute-start(bf16[1024,512]{1,0:T(8,128)(2,1)S(1)} %get-tuple-element.53), channel_id=1, source_target_pairs={{0,1},{1,0},{2,3},{3,2},{4,5},{5,4},{6,7},{7,6},{8,9},{9,8},{10,11... | collective-permute-start | bytes 3145736 | tf_op jit(solution)/shard_map/ppermute | solution.py:507
  109.1 8.5 %slice-start.2 = ((s8[11534336]{0:T(1024)(128)(4,1)}), s8[3145728]{0:T(1024)(128)(4,1)S(1)}, s32[]{:S(2)}) async-start(s8[11534336]{0:T(1024)(128)(4,1)} %bitcast.26), calls=%async_computation.6 | async-start | bytes 6291456
  112.0 11.4 %collective-permute-start.3 = (bf16[256,512]{1,0:T(8,128)(2,1)S(1)}, bf16[256,512]{1,0:T(8,128)(2,1)S(1)}, u32[]{:S(2)}, u32[]{:S(2)}) collective-permute-start(bf16[256,512]{1,0:T(8,128)(2,1)S(1)} %get-tuple-element.54), channel_id=1, source_target_pairs={{0,32},{32,0},{64,96},{96,64},{1,33},{33,1},{65,97},{97,65},{2,34}... | collective-permute-start | bytes 786440 | tf_op jit(solution)/shard_map/ppermute | solution.py:534
  114.0 15.9 %collective-permute-start.4 = (bf16[256,512]{1,0:T(8,128)(2,1)S(1)}, bf16[256,512]{1,0:T(8,128)(2,1)S(1)}, u32[]{:S(2)}, u32[]{:S(2)}) collective-permute-start(bf16[256,512]{1,0:T(8,128)(2,1)S(1)} %get-tuple-element.55), channel_id=1, source_target_pairs={{0,64},{32,96},{64,0},{96,32},{1,65},{33,97},{65,1},{97,33},{2,66}... | collective-permute-start | bytes 786440 | tf_op jit(solution)/shard_map/ppermute | solution.py:534
  117.6 14.8 %collective-permute-start.5 = (bf16[256,512]{1,0:T(8,128)(2,1)S(1)}, bf16[256,512]{1,0:T(8,128)(2,1)S(1)}, u32[]{:S(2)}, u32[]{:S(2)}) collective-permute-start(bf16[256,512]{1,0:T(8,128)(2,1)S(1)} %get-tuple-element.56), channel_id=1, source_target_pairs={{0,96},{32,64},{64,32},{96,0},{1,97},{33,65},{65,33},{97,1},{2,98}... | collective-permute-start | bytes 786440 | tf_op jit(solution)/shard_map/ppermute | solution.py:534
  135.8 46.3 %copy-start.8 = (bf16[2048,512]{1,0:T(8,128)(2,1)S(1)}, bf16[2048,512]{1,0:T(8,128)(2,1)}, u32[]{:S(2)}) copy-start(bf16[2048,512]{1,0:T(8,128)(2,1)} %head_hbm.1) | copy-start | bytes 6291460
  135.8 50.7 %all-to-all-start.3 = ((bf16[32,16,2560]{2,1,0:T(8,128)(2,1)}), bf16[32,16,2560]{2,1,0:T(8,128)(2,1)}, u32[]{:S(2)}, u32[]{:S(2)}) async-start(bf16[32,16,2560]{2,1,0:T(8,128)(2,1)} %bitcast.12), calls=%async_computation.3 | async-start | bytes 5242880 | tf_op jit(solution)/shard_map/all_to_all | solution.py:421
  141.5 33.1 %collective-permute-start.6 = (bf16[64,512]{1,0:T(8,128)(2,1)S(1)}, bf16[64,512]{1,0:T(8,128)(2,1)S(1)}, u32[]{:S(2)}, u32[]{:S(2)}) collective-permute-start(bf16[64,512]{1,0:T(8,128)(2,1)S(1)} %get-tuple-element.59), channel_id=1, source_target_pairs={{0,8},{8,0},{16,24},{24,16},{1,9},{9,1},{17,25},{25,17},{2,10},{10... | collective-permute-start | bytes 196616 | tf_op jit(solution)/shard_map/ppermute | solution.py:534
  143.2 33.4 %collective-permute-start.7 = (bf16[64,512]{1,0:T(8,128)(2,1)S(1)}, bf16[64,512]{1,0:T(8,128)(2,1)S(1)}, u32[]{:S(2)}, u32[]{:S(2)}) collective-permute-start(bf16[64,512]{1,0:T(8,128)(2,1)S(1)} %get-tuple-element.60), channel_id=1, source_target_pairs={{0,16},{8,24},{16,0},{24,8},{1,17},{9,25},{17,1},{25,9},{2,18},{10... | collective-permute-start | bytes 196616 | tf_op jit(solution)/shard_map/ppermute | solution.py:534
  146.0 30.6 %collective-permute-start.8 = (bf16[64,512]{1,0:T(8,128)(2,1)S(1)}, bf16[64,512]{1,0:T(8,128)(2,1)S(1)}, u32[]{:S(2)}, u32[]{:S(2)}) collective-permute-start(bf16[64,512]{1,0:T(8,128)(2,1)S(1)} %get-tuple-element.61), channel_id=1, source_target_pairs={{0,24},{8,16},{16,8},{24,0},{1,25},{9,17},{17,9},{25,1},{2,26},{10... | collective-permute-start | bytes 196616 | tf_op jit(solution)/shard_map/ppermute | solution.py:534
  177.2 6.6 %collective-permute-start.9 = (bf16[16,512]{1,0:T(8,128)(2,1)S(1)}, bf16[16,512]{1,0:T(8,128)(2,1)S(1)}, u32[]{:S(2)}, u32[]{:S(2)}) collective-permute-start(bf16[16,512]{1,0:T(8,128)(2,1)S(1)} %get-tuple-element.63), channel_id=1, source_target_pairs={{0,2},{2,0},{4,6},{6,4},{1,3},{3,1},{5,7},{7,5},{8,10},{10,8},{12,... | collective-permute-start | bytes 49160 | tf_op jit(solution)/shard_map/ppermute | solution.py:534
  179.1 5.2 %collective-permute-start.10 = (bf16[16,512]{1,0:T(8,128)(2,1)S(1)}, bf16[16,512]{1,0:T(8,128)(2,1)S(1)}, u32[]{:S(2)}, u32[]{:S(2)}) collective-permute-start(bf16[16,512]{1,0:T(8,128)(2,1)S(1)} %get-tuple-element.64), channel_id=1, source_target_pairs={{0,4},{2,6},{4,0},{6,2},{1,5},{3,7},{5,1},{7,3},{8,12},{10,14},{12... | collective-permute-start | bytes 49160 | tf_op jit(solution)/shard_map/ppermute | solution.py:534
  180.9 4.9 %collective-permute-start.11 = (bf16[16,512]{1,0:T(8,128)(2,1)S(1)}, bf16[16,512]{1,0:T(8,128)(2,1)S(1)}, u32[]{:S(2)}, u32[]{:S(2)}) collective-permute-start(bf16[16,512]{1,0:T(8,128)(2,1)S(1)} %get-tuple-element.65), channel_id=1, source_target_pairs={{0,6},{2,4},{4,2},{6,0},{1,7},{3,5},{5,3},{7,1},{8,14},{10,12},{12... | collective-permute-start | bytes 49160 | tf_op jit(solution)/shard_map/ppermute | solution.py:534

commit v6 on v4

--- a/solution.py
+++ b/solution.py
@@ -1,4 +1,3 @@
-import functools
 import math
 
 import jax
@@ -140,8 +139,8 @@
 
 
 def forward_kernel(
-    recv_ref, w_hbm, mixed_hbm, out_hbm, hidden_hbm, slopes_hbm,
-    x_ref, act_ref, w_ref, mixed_ref, hidden_ref, slopes_ref, out_ref, sems, out_sems,
+    recv_hbm, w_hbm, mixed_hbm, out_hbm, hidden_hbm, slopes_hbm,
+    x_ref, extra_ref, act_ref, w_ref, mixed_ref, hidden_ref, slopes_ref, out_ref, sems, out_sems,
 ):
     quarter = WIDTH // 4
 
@@ -150,6 +149,8 @@
         copy.start()
         return copy
 
+    extra_copy = bring(recv_hbm.at[:, pl.ds(WIDTH, quarter)], extra_ref, 7)
+    main_copy = bring(recv_hbm.at[:, pl.ds(0, WIDTH)], x_ref.at[pl.ds(0, SLOTS), :], 8)
     groups = ((0, 1), (1, 3), (3, len(CHUNKS)))
     weight_copies = []
     for g, (begin, end) in enumerate(groups):
@@ -158,10 +159,12 @@
             cols = pl.ds(h * HIDDEN + lo, hi - lo)
             weight_copies.append(bring(w_hbm.at[:, cols], w_ref.at[:, cols], 1 + 2 * g + h))
     mixed_copy = bring(mixed_hbm, mixed_ref, 0)
-    x_ref[:SLOTS, :] = recv_ref[:, :WIDTH]
-    spread = dot(unpacker(), recv_ref[:, WIDTH:]).astype(BF16)
+    turned = unpacker()
+    extra_copy.wait()
+    spread = dot(turned, extra_ref[...]).astype(BF16)
     for j in range(4):
         x_ref[SLOTS:, j * quarter : (j + 1) * quarter] = spread[j * SPARE : (j + 1) * SPARE]
+    main_copy.wait()
     outgoing = []
 
     def send(source, target, lo, wide):
@@ -205,17 +208,6 @@
         copy.wait()
 
 
-def fetch_kernel(_, down_hbm, hidden_hbm, down_ref, hidden_ref, sems):
-    copies = (
-        pltpu.make_async_copy(hidden_hbm, hidden_ref, sems.at[0]),
-        pltpu.make_async_copy(down_hbm, down_ref, sems.at[1]),
-    )
-    for copy in copies:
-        copy.start()
-    for copy in copies:
-        copy.wait()
-
-
 def weighted(chosen, gates):
     return jnp.where(chosen, gates, 0.0)
 
@@ -241,7 +233,7 @@
 
 
 def loss_kernel(
-    routes_ref, gates_ref, matches_ref, partner_ref, embedding_ref, unit_ref, key_ref, _,
+    routes_ref, gates_ref, matches_ref, partner_ref, embedding_ref, unit_ref, key_ref,
     loss_ref, grad_ref, out_ref,
 ):
     embedding = embedding_ref[...]
@@ -280,14 +272,50 @@
     out_ref[:, EMBED:] = (extra_gates * total).astype(BF16)
 
 
-def head_kernel(
-    arrived_ref, tokens_ref, embed_grad_ref, hidden_ref, down_ref, grads_ref, own_ref, other_ref
-):
+def joined_kernel(arrived_ref, mixed_ref, slopes_ref, joined_ref, grads_ref, act_ref):
     quarter = EMBED // 4
     grads_ref[:SLOTS, :] = arrived_ref[:, :EMBED]
     spread = dot(unpacker(), arrived_ref[:, EMBED:]).astype(BF16)
     for j in range(4):
         grads_ref[SLOTS:, j * quarter : (j + 1) * quarter] = spread[j * SPARE : (j + 1) * SPARE]
+    for c, (lo, hi) in enumerate(CHUNKS):
+        slot = c % 2
+        wide = hi - lo
+        act_ref[slot, :, :wide] = dot_cols(grads_ref[...], mixed_ref[lo:hi, :])
+        for m in range(0, TOTAL, 64):
+            hidden_grad = act_ref[slot, m : m + 64, :wide]
+            for offset in (0, HIDDEN):
+                slope = slopes_ref[m : m + 64, offset + lo : offset + hi].astype(F32)
+                joined_ref[m : m + 64, offset + lo : offset + hi] = (hidden_grad * slope).astype(BF16)
+
+
+def input_kernel(joined_ref, w_ref, out_hbm, extra_ref, out_ref, out_sems):
+    step = WIDTH // 4
+    outgoing = []
+
+    def send(start, wide, index):
+        cols = pl.ds(start, wide)
+        copy = pltpu.make_async_copy(out_ref.at[:, cols], out_hbm.at[:, cols], out_sems.at[index])
+        copy.start()
+        outgoing.append(copy)
+
+    for n in range(0, WIDTH, TILE):
+        result = dot_cols(joined_ref[...], w_ref[n : n + TILE, :]).astype(BF16)
+        out_ref[:, n : n + TILE] = result[:SLOTS]
+        j, within = n // step, n % step
+        extra_ref[j * SPARE : (j + 1) * SPARE, within : within + TILE] = result[SLOTS:]
+        if n in (WIDTH // 2 - TILE, WIDTH * 3 // 4 - TILE):
+            begin = 0 if len(outgoing) == 0 else WIDTH // 2
+            send(begin, n + TILE - begin, len(outgoing))
+    out_ref[:, WIDTH:] = dot(packer(), extra_ref[...]).astype(BF16)
+    send(WIDTH * 3 // 4, 2 * step, 2)
+    for copy in outgoing:
+        copy.wait()
+
+
+def head_kernel(
+    grads_ref, tokens_ref, embed_grad_ref, hidden_ref, down_ref, own_ref, other_ref
+):
     first = lax.axis_index("expert_2") == 0
     inner = dot_rows(hidden_ref[...], grads_ref[...]).astype(BF16)
     for n in range(0, WIDTH, TILE):
@@ -300,68 +328,24 @@
             other_ref[row : row + 16, :] = jnp.where(first, odd, even).astype(BF16)
 
 
-def joined_kernel(grads_ref, mixed_ref, slopes_ref, joined_ref, act_ref):
-    for c, (lo, hi) in enumerate(CHUNKS):
-        slot = c % 2
-        wide = hi - lo
-        act_ref[slot, :, :wide] = dot_cols(grads_ref[...], mixed_ref[lo:hi, :])
-        for m in range(0, TOTAL, 64):
-            hidden_grad = act_ref[slot, m : m + 64, :wide]
-            for offset in (0, HIDDEN):
-                slope = slopes_ref[m : m + 64, offset + lo : offset + hi].astype(F32)
-                joined_ref[m : m + 64, offset + lo : offset + hi] = (hidden_grad * slope).astype(BF16)
-
-
-def input_kernel(joined_ref, w_ref, _, out_hbm, extra_ref, out_ref, out_sems):
-    step = WIDTH // 4
-    outgoing = []
-
-    def send(start, wide, index):
-        cols = pl.ds(start, wide)
-        copy = pltpu.make_async_copy(out_ref.at[:, cols], out_hbm.at[:, cols], out_sems.at[index])
-        copy.start()
-        outgoing.append(copy)
-
-    for n in range(0, WIDTH, TILE):
-        result = dot_cols(joined_ref[...], w_ref[n : n + TILE, :]).astype(BF16)
-        out_ref[:, n : n + TILE] = result[:SLOTS]
-        j, within = n // step, n % step
-        extra_ref[j * SPARE : (j + 1) * SPARE, within : within + TILE] = result[SLOTS:]
-        if n == WIDTH // 2 - TILE:
-            send(0, WIDTH // 2, 0)
-    out_ref[:, WIDTH:] = dot(packer(), extra_ref[...]).astype(BF16)
-    send(WIDTH // 2, WIDTH // 2 + step, 1)
-    for copy in outgoing:
-        copy.wait()
-
-
-def share_kernel(axis, count, own_hbm, *refs):
-    received_hbm, outs = refs[:count], refs[count : count + 4]
-    own_ref, received_ref, total_ref, sent_ref, sems, out_sems = refs[count + 4 :]
-    copies = [pltpu.make_async_copy(own_hbm, own_ref, sems.at[count])]
-    for k in range(count):
-        copies.append(pltpu.make_async_copy(received_hbm[k], received_ref.at[k], sems.at[k]))
-    for copy in copies:
-        copy.start()
-    for copy in copies:
-        copy.wait()
-    place = lax.axis_index(axis)
-    outgoing = []
-    for k in (2, 1, 3, 0):
-        quarter = jnp.bitwise_xor(place, k)
-        total = own_ref[quarter]
-        for i in range(count):
-            total = total + received_ref[i, quarter].astype(F32)
-        if k:
-            sent_ref[k - 1] = total.astype(BF16)
-            copy = pltpu.make_async_copy(sent_ref.at[k - 1], outs[k], out_sems.at[k])
-        else:
-            total_ref[...] = total
-            copy = pltpu.make_async_copy(total_ref, outs[0], out_sems.at[0])
-        copy.start()
-        outgoing.append(copy)
-    for copy in outgoing:
-        copy.wait()
+def ring_kernel(own_ref, received_ref, *outs):
+    place = lax.axis_index("dp")
+    for half, near in enumerate((1, 3)):
+        kept_ref, sent_ref = outs[2 * half : 2 * half + 2]
+        for i, k in enumerate((0, near ^ 2)):
+            quarter = jnp.bitwise_xor(place, k)
+            kept_ref[i] = own_ref[quarter, half] + received_ref[quarter, half].astype(F32)
+        for i, k in enumerate((near, 2)):
+            quarter = jnp.bitwise_xor(place, k)
+            total = own_ref[quarter, half] + received_ref[quarter, half].astype(F32)
+            sent_ref[i] = total.astype(BF16)
+
+
+def second_kernel(first_ref, first_in_ref, last_ref, last_in_ref, own_ref, sent_first_ref, sent_last_ref):
+    own_ref[0] = first_ref[0] + first_in_ref[0].astype(F32)
+    own_ref[1] = last_ref[0] + last_in_ref[0].astype(F32)
+    sent_first_ref[...] = (first_ref[1] + first_in_ref[1].astype(F32)).astype(BF16)
+    sent_last_ref[...] = (last_ref[1] + last_in_ref[1].astype(F32)).astype(BF16)
 
 
 def combine_kernel(routes_ref, direct_ref, back_hbm, out_ref, back_ref, sems):
@@ -443,16 +427,17 @@
     packed, hidden, slopes = call(
         forward_kernel,
         [(packed_shape, BF16, hbm), ((TOTAL, HIDDEN), BF16, hbm), ((TOTAL, 2 * HIDDEN), BF16, hbm)],
-        [(received, vmem), (weights_joined, hbm), (mixed, hbm)],
+        [(received, hbm), (weights_joined, hbm), (mixed, hbm)],
         scratch=[
             pltpu.VMEM((TOTAL, WIDTH), BF16),
+            pltpu.VMEM((SLOTS, WIDTH // 4), BF16),
             pltpu.VMEM((2, 2, TOTAL, 256), F32),
             pltpu.VMEM((WIDTH, 2 * HIDDEN), BF16),
             pltpu.VMEM((HIDDEN, EMBED), BF16),
             pltpu.VMEM((TOTAL, HIDDEN), BF16),
             pltpu.VMEM((TOTAL, 2 * HIDDEN), BF16),
             pltpu.VMEM(packed_shape, BF16),
-            dma((7,)),
+            dma((9,)),
             dma((10,)),
         ],
         flops=2 * TOTAL * HIDDEN * (2 * WIDTH + EMBED), moved=22 << 20, limit=56.5,
@@ -465,69 +450,62 @@
         flops=4 * SLOTS * ROWS * EMBED * 2, moved=2 << 20,
     )
     keys = lax.ppermute(unit, EXPERT, partner)
-    down_near, hidden_near = call(
-        fetch_kernel,
-        [(weights_down.shape, BF16, vmem), (hidden.shape, BF16, vmem)],
-        [(unit, vmem), (weights_down, hbm), (hidden, hbm)],
-        scratch=[dma((2,))],
-        moved=16 << 20, limit=30,
-    )
     row_loss, embed_grad, slot_grads = call(
         loss_kernel,
         [((1, ROWS), F32, vmem), ((ROWS, EMBED), BF16, vmem), (packed_shape, BF16, vmem)],
         [(routes, vmem), (gates, vmem), (matches, vmem), (partner_matches, vmem),
-         (embedding, vmem), (unit, vmem), (keys, vmem), (hidden_near, hbm)],
-        flops=2 * SLOTS * ROWS * EMBED * 2, moved=2 << 20, limit=16,
+         (embedding, vmem), (unit, vmem), (keys, vmem)],
+        flops=20 * 10**9, moved=2 << 20, limit=16,
     )
     arrived = exchanged(slot_grads, EXPERT, EXPERTS)
-    half_shape = (WIDTH // 2, EMBED)
-    grads, own, other = call(
-        head_kernel,
-        [((TOTAL, EMBED), BF16, vmem), (half_shape, F32, vmem), (half_shape, BF16, vmem)],
-        [(arrived, vmem), (tokens, vmem), (embed_grad, vmem), (hidden_near, vmem), (down_near, vmem)],
-        flops=2 * HIDDEN * EMBED * (TOTAL + WIDTH), moved=12 << 20, limit=16,
-    )
-    arrivals = [lax.ppermute(other, "expert_2", [(0, 1), (1, 0)])]
     joined_shape = (TOTAL, 2 * HIDDEN)
-    (joined_grad,) = call(
+    joined_grad, grads = call(
         joined_kernel,
-        [(joined_shape, BF16, vmem)],
-        [(grads, vmem), (mixed, vmem), (slopes, vmem)],
+        [(joined_shape, BF16, vmem), ((TOTAL, EMBED), BF16, vmem)],
+        [(arrived, vmem), (mixed, vmem), (slopes, vmem)],
         scratch=[pltpu.VMEM((2, TOTAL, 256), F32)],
-        flops=2 * TOTAL * HIDDEN * EMBED, moved=8 << 20, limit=16,
+        flops=4 * 10**9, moved=8 << 20, limit=16,
     )
     (input_grads,) = call(
         input_kernel,
         [(wide_shape, BF16, hbm)],
-        [(joined_grad, vmem), (weights_joined, vmem), (arrivals[0], hbm)],
+        [(joined_grad, vmem), (weights_joined, vmem)],
         scratch=[
             pltpu.VMEM((SLOTS, WIDTH // 4), BF16),
             pltpu.VMEM(wide_shape, BF16),
-            dma((2,)),
+            dma((3,)),
         ],
         flops=4 * TOTAL * HIDDEN * WIDTH, moved=18 << 20, limit=34,
     )
     back = exchanged(input_grads, EXPERT, EXPERTS)
     direct = dot_cols(embed_grad, projection)
-    rows = own.shape[0] // 4
-    own, *sent = call(
-        functools.partial(share_kernel, "dp", 1),
-        [((rows, EMBED), F32, hbm)] + [((rows, EMBED), BF16, hbm)] * 3,
-        [(value.reshape(4, rows, EMBED), hbm) for value in (own, *arrivals)],
-        scratch=[
-            pltpu.VMEM((4, rows, EMBED), F32),
-            pltpu.VMEM((1, 4, rows, EMBED), BF16),
-            pltpu.VMEM((rows, EMBED), F32),
-            pltpu.VMEM((3, rows, EMBED), BF16),
-            dma((2,)),
-            dma((4,)),
-        ],
+    half_shape = (WIDTH // 2, EMBED)
+    own, other = call(
+        head_kernel,
+        [(half_shape, F32, vmem), (half_shape, BF16, vmem)],
+        [(grads, vmem), (tokens, vmem), (embed_grad, vmem), (hidden, vmem), (weights_down, vmem)],
         limit=16,
     )
-    for k, value in enumerate(sent):
-        arrived = lax.ppermute(value, "dp", [(i, i ^ (k + 1)) for i in range(4)])
-        own = own + arrived.astype(F32)
-    back, sums = lax.optimization_barrier((back, own.astype(BF16)))
+    other = lax.ppermute(other, "expert_2", [(0, 1), (1, 0)])
+    rows = WIDTH // 16
+
+    def around(value, distance):
+        return lax.ppermute(value, "dp", [(i, i ^ distance) for i in range(4)])
+
+    kept_first, sent_first, kept_last, sent_last = call(
+        ring_kernel,
+        [((2, rows, EMBED), F32, vmem), ((2, rows, EMBED), BF16, vmem)] * 2,
+        [(value.reshape(4, 2, rows, EMBED), vmem) for value in (own, other)],
+        limit=16,
+    )
+    own, sent_last, sent_first = call(
+        second_kernel,
+        [((2, rows, EMBED), F32, vmem)] + [((rows, EMBED), BF16, vmem)] * 2,
+        [(kept_first, vmem), (around(sent_first, 1), vmem), (kept_last, vmem), (around(sent_last, 3), vmem)],
+        limit=16,
+    )
+    own = own + jnp.stack([around(sent_last, 3), around(sent_first, 1)]).astype(F32)
+    back, sums = lax.optimization_barrier((back, own.astype(BF16).reshape(2 * rows, EMBED)))
     parts = lax.all_to_all(
         sums.reshape(16, 16, EMBED), ("expert_0", "expert_1"), 0, 0, tiled=True
     )

time: 175 us -> 168 us (0.960)
  waiting for transfers between devices: 59.5 us -> 49.7 us
  local copies, waits for them, and re-layouts: 0.06 us -> 4.21 us
  Pallas kernels: 50.1 us -> 47.6 us
    all_to_all x2, waiting for transfers between devices: 14.4 us -> 5.05 us  [exchanged(): return lax.all_to_all(blocks, axes, 0, 0, tiled=True).reshape(rows, width)]
    unnamed x28, local copies, waits for them, and re-layouts: 0.06 us -> 4.21 us
    pallas_call x11, Pallas kernels: 50.1 us -> 47.6 us  [call(): pl.pallas_call(kernel, out_shape=tuple((jax.ShapeDtypeStruct(shape, dtype...]
    ppermute x4 -> x5, waiting for transfers between devices: 15.6 us -> 14.2 us  [the longest x4 11.9 us: around(): return lax.ppermute(value, 'dp', [(i, i ^ distance) for i in range(4)])]
    ppermute x4 -> x5, starting transfers between devices: 6.56 us -> 7.69 us  [the longest x4 7.14 us: around(): return lax.ppermute(value, 'dp', [(i, i ^ distance) for i in range(4)])]
  transfers between devices with their start and end apart: 9 -> 10, of which waited for: 9 -> 10; matrix products, arithmetic and copies ran while one was open for 2% -> 2% of each run, Pallas kernels for 8% -> 10%
where the time goes in v6:
time: 168 us
  waiting for transfers between devices  49.7 us (30%)
  Pallas kernels  47.6 us (28%)
  blocking collectives  33 us (20%)
  starting transfers between devices  29 us (17%)
  local copies, waits for them, and re-layouts  4.21 us (3%)
  matrix products  1.79 us (1%)
    pallas_call x11, Pallas kernels, call(): pl.pallas_call(kernel, out_shape=tuple((jax.ShapeDtypeStruct(shape, dtype...  47.6 us
    all_to_all x2, blocking collectives, exchanged(): return lax.all_to_all(blocks, axes, 0, 0, tiled=True).reshape(rows, width)  33 us
    ppermute x1, waiting for transfers between devices, body(): partner_matches = lax.ppermute(matches.astype(BF16), EXPERT, partner)  22.1 us
    all_to_all x2, starting transfers between devices, exchanged(): return lax.all_to_all(blocks, axes, 0, 0, tiled=True).reshape(rows, width)  12.6 us
    ppermute x4, waiting for transfers between devices, around(): return lax.ppermute(value, 'dp', [(i, i ^ distance) for i in range(4)])  11.9 us
    ppermute x4, starting transfers between devices, around(): return lax.ppermute(value, 'dp', [(i, i ^ distance) for i in range(4)])  7.14 us
    ppermute x1, waiting for transfers between devices, body(): keys = lax.ppermute(unit, EXPERT, partner)  5.94 us
    all_to_all x2, waiting for transfers between devices, exchanged(): return lax.all_to_all(blocks, axes, 0, 0, tiled=True).reshape(rows, width)  5.05 us
  transfers between devices with their start and end apart: 10, of which 10 were waited for; matrix products, arithmetic and copies ran while one was open for 2% of the time, Pallas kernels for 10%

profile of v6, /device:TPU:0, one launch (start us, length us, event | category | flops | bytes accessed | tf_op | source)
XLA Modules:
  0.0 167.5 jit_solution(15255993262849675922)
XLA Ops:
  0.6 3.2 %shard_map.94 = bf16[512,2560]{1,0:T(8,128)(2,1)} custom-call(s32[4,128]{1,0:T(4,128)} %bitcast.28, bf16[128,2048]{1,0:T(8,128)(2,1)} %tokens_ref.1), custom_call_target="tpu_custom_call" | custom-call | flops 536870912 | bytes 3145728 | tf_op jit(solution)/shard_map/pallas_call | solution.py:375
  3.9 0.0 copy-start.5
  3.9 7.4 %all-to-all-start = ((bf16[32,16,2560]{2,1,0:T(8,128)(2,1)}), bf16[32,16,2560]{2,1,0:T(8,128)(2,1)S(1)}, u32[]{:S(2)}, u32[]{:S(2)}) async-start(bf16[32,16,2560]{2,1,0:T(8,128)(2,1)} %bitcast.38), calls=%async_computation | async-start | bytes 5242880 | tf_op jit(solution)/shard_map/all_to_all | solution.py:389
  11.3 0.0 copy-done.5
  11.3 3.4 %collective-permute-start = (bf16[1,128]{1,0:T(2,128)(2,1)S(1)}, bf16[1,128]{1,0:T(2,128)(2,1)S(1)}, u32[]{:S(2)}, u32[]{:S(2)}) collective-permute-start(bf16[1,128]{1,0:T(2,128)(2,1)S(1)} %convert_element_type.12), channel_id=1, source_target_pairs={{0,16},{1,17},{2,18},{3,19},{4,20},{5,21},{6,22},{7,23},{8,24},{9,... | collective-permute-start | bytes 776 | tf_op jit(solution)/shard_map/ppermute | solution.py:411
  14.7 7.8 %shard_map.95 = (bf16[1408,512]{1,0:T(8,128)(2,1)}, f32[128,512]{1,0:T(8,128)}) custom-call(bf16[1408,2048]{1,0:T(8,128)(2,1)} %bitcast.21, bf16[2048,512]{1,0:T(8,128)(2,1)} %head_hbm.1, bf16[128,2048]{1,0:T(8,128)(2,1)} %tokens_ref.1), custom_call_target="tpu_custom_call" | custom-call | flops 3221225472 | bytes 8388608 | tf_op jit(solution)/shard_map/pallas_call | solution.py:375
  22.5 22.1 %collective-permute-done.partner_ref = bf16[1,128]{1,0:T(2,128)(2,1)S(1)} collective-permute-done((bf16[1,128]{1,0:T(2,128)(2,1)S(1)}, bf16[1,128]{1,0:T(2,128)(2,1)S(1)}, u32[]{:S(2)}, u32[]{:S(2)}) %collective-permute-start) | collective-permute-done | bytes 288 | tf_op jit(solution)/shard_map/ppermute | solution.py:411
  44.6 1.4 all-to-all-done
  46.0 1.5 copy-done.9
  47.5 14.4 %shard_map.96 = (bf16[512,640]{1,0:T(8,128)(2,1)}, bf16[640,1408]{1,0:T(8,128)(2,1)}, bf16[640,2816]{1,0:T(8,128)(2,1)}) custom-call(bf16[512,2560]{1,0:T(8,128)(2,1)} %bitcast.39, bf16[2048,2816]{1,0:T(8,128)(2,1)} %bitcast.32, bf16[1408,512]{1,0:T(8,128)(2,1)} %get-tuple-element.32.mixed_hbm.mixed_ref), custom_call_target="tpu_custom_call" | custom-call | flops 8304721920 | bytes 23068672 | tf_op jit(solution)/shard_map/pallas_call | solution.py:375
  62.0 0.0 slice-start
  62.0 16.8 %all_to_all.25 = bf16[32,16,640]{2,1,0:T(8,128)(2,1)S(1)} all-to-all(bf16[32,16,640]{2,1,0:T(8,128)(2,1)} %bitcast.40), channel_id=1, replica_groups=mesh['dp'=4,'expert_0'=4,'expert_1'=4,'expert_2'=2] {'expert_0','expert_..., dimensions={0} | all-to-all | bytes 1310720 | tf_op jit(solution)/shard_map/all_to_all | solution.py:389
  78.8 0.0 copy-done.3
  78.8 0.0 copy-done.4
  78.8 0.0 copy-done.6
  78.8 0.9 shard_map.97
  79.8 1.8 %collective-permute-start.1 = (bf16[128,512]{1,0:T(8,128)(2,1)S(1)}, bf16[128,512]{1,0:T(8,128)(2,1)S(1)}, u32[]{:S(2)}, u32[]{:S(2)}) collective-permute-start(bf16[128,512]{1,0:T(8,128)(2,1)S(1)} %get-tuple-element.36.unit_ref), channel_id=1, source_target_pairs={{0,16},{1,17},{2,18},{3,19},{4,20},{5,21},{6,22},{7,23},{8,24},{9,... | collective-permute-start | bytes 393224 | tf_op jit(solution)/shard_map/ppermute | solution.py:452
  81.5 5.9 %collective-permute-done.1.key_ref = bf16[128,512]{1,0:T(8,128)(2,1)S(1)} collective-permute-done((bf16[128,512]{1,0:T(8,128)(2,1)S(1)}, bf16[128,512]{1,0:T(8,128)(2,1)S(1)}, u32[]{:S(2)}, u32[]{:S(2)}) %collective-permute-start.1) | collective-permute-done | bytes 131104 | tf_op jit(solution)/shard_map/ppermute | solution.py:452
  87.5 1.1 shard_map.98
  88.6 16.2 %all_to_all.26 = bf16[32,16,640]{2,1,0:T(8,128)(2,1)S(1)} all-to-all(bf16[32,16,640]{2,1,0:T(8,128)(2,1)S(1)} %bitcast.25), channel_id=1, replica_groups=mesh['dp'=4,'expert_0'=4,'expert_1'=4,'expert_2'=2] {'expert_0','expert_..., dimensions={0} | all-to-all | bytes 1310720 | tf_op jit(solution)/shard_map/all_to_all | solution.py:389
  104.8 0.0 copy-done.7
  104.8 1.4 shard_map.99
  106.2 9.0 %shard_map.100 = bf16[512,2560]{1,0:T(8,128)(2,1)} custom-call(bf16[640,2816]{1,0:T(8,128)(2,1)S(1)} %get-tuple-element.40.joined_ref, bf16[2048,2816]{1,0:T(8,128)(2,1)S(1)} %bitcast.35), custom_call_target="tpu_custom_call" | custom-call | flops 7381975040 | bytes 18874368 | tf_op jit(solution)/shard_map/pallas_call | solution.py:375
  115.2 0.0 copy-start.1
  115.3 0.0 copy-start.2
  115.3 5.2 %all-to-all-start.3 = ((bf16[32,16,2560]{2,1,0:T(8,128)(2,1)}), bf16[32,16,2560]{2,1,0:T(8,128)(2,1)}, u32[]{:S(2)}, u32[]{:S(2)}) async-start(bf16[32,16,2560]{2,1,0:T(8,128)(2,1)} %bitcast.10), calls=%async_computation.3 | async-start | bytes 5242880 | tf_op jit(solution)/shard_map/all_to_all | solution.py:389
  120.5 0.0 copy-start
  120.5 2.6 %copy-done = bf16[1,1408,2048]{2,1,0:T(8,128)(2,1)S(1)} copy-done((bf16[1,1408,2048]{2,1,0:T(8,128)(2,1)S(1)}, bf16[1,1408,2048]{2,1,0:T(8,128)(2,1)}, u32[]{:S(2)}) %copy-start) | copy-done | bytes 5767192
  123.1 5.1 %shard_map.101 = (f32[1024,512]{1,0:T(8,128)S(1)}, bf16[1024,512]{1,0:T(8,128)(2,1)S(1)}) custom-call(bf16[640,512]{1,0:T(8,128)(2,1)S(1)} %get-tuple-element.41.grads_ref, bf16[128,2048]{1,0:T(8,128)(2,1)S(1)} %copy-done.1, bf16[128,512]{1,0:T(8,128)(2,1)S(1)} %get-tuple-element.37.embed_grad_ref, bf16[640,1408]{1,0:T(8,128)(2,1)S(1)} %copy-done.2, ...), custom_call_target="tpu_custom_call" | custom-call | tf_op jit(solution)/shard_map/pallas_call | solution.py:375
  128.2 0.6 collective-permute-start.2
  128.8 2.3 %collective-permute-done.2 = bf16[1024,512]{1,0:T(8,128)(2,1)S(1)} collective-permute-done((bf16[1024,512]{1,0:T(8,128)(2,1)S(1)}, bf16[1024,512]{1,0:T(8,128)(2,1)S(1)}, u32[]{:S(2)}, u32[]{:S(2)}) %collective-permute-start.2) | collective-permute-done | bytes 1048608 | tf_op jit(solution)/shard_map/ppermute | solution.py:489
  131.1 0.2 shard_map.102
  131.2 2.0 %collective-permute-start.3 = (bf16[2,128,512]{2,1,0:T(8,128)(2,1)S(1)}, bf16[2,128,512]{2,1,0:T(8,128)(2,1)S(1)}, u32[]{:S(2)}, u32[]{:S(2)}) collective-permute-start(bf16[2,128,512]{2,1,0:T(8,128)(2,1)S(1)} %get-tuple-element.46), channel_id=1, source_target_pairs={{0,32},{32,0},{64,96},{96,64},{1,33},{33,1},{65,97},{97,65},{2,34}... | collective-permute-start | bytes 786440 | tf_op jit(solution)/shard_map/ppermute | solution.py:493
  133.2 2.5 %collective-permute-start.4 = (bf16[2,128,512]{2,1,0:T(8,128)(2,1)S(1)}, bf16[2,128,512]{2,1,0:T(8,128)(2,1)S(1)}, u32[]{:S(2)}, u32[]{:S(2)}) collective-permute-start(bf16[2,128,512]{2,1,0:T(8,128)(2,1)S(1)} %get-tuple-element.48), channel_id=1, source_target_pairs={{0,96},{32,64},{64,32},{96,0},{1,97},{33,65},{65,33},{97,1},{2,98}... | collective-permute-start | bytes 786440 | tf_op jit(solution)/shard_map/ppermute | solution.py:493
  135.8 4.3 %collective-permute-done.3.first_in_ref = bf16[2,128,512]{2,1,0:T(8,128)(2,1)S(1)} collective-permute-done((bf16[2,128,512]{2,1,0:T(8,128)(2,1)S(1)}, bf16[2,128,512]{2,1,0:T(8,128)(2,1)S(1)}, u32[]{:S(2)}, u32[]{:S(2)}) %collective-permute-start.3) | collective-permute-done | bytes 262176 | tf_op jit(solution)/shard_map/ppermute | solution.py:493
  140.1 2.7 %collective-permute-done.4.last_in_ref = bf16[2,128,512]{2,1,0:T(8,128)(2,1)S(1)} collective-permute-done((bf16[2,128,512]{2,1,0:T(8,128)(2,1)S(1)}, bf16[2,128,512]{2,1,0:T(8,128)(2,1)S(1)}, u32[]{:S(2)}, u32[]{:S(2)}) %collective-permute-start.4) | collective-permute-done | bytes 262176 | tf_op jit(solution)/shard_map/ppermute | solution.py:493
  142.7 0.1 shard_map.103
  142.8 2.6 %collective-permute-start.5 = (bf16[128,512]{1,0:T(8,128)(2,1)S(1)}, bf16[128,512]{1,0:T(8,128)(2,1)S(1)}, u32[]{:S(2)}, u32[]{:S(2)}) collective-permute-start(bf16[128,512]{1,0:T(8,128)(2,1)S(1)} %get-tuple-element.50), channel_id=1, source_target_pairs={{0,96},{32,64},{64,32},{96,0},{1,97},{33,65},{65,33},{97,1},{2,98}... | collective-permute-start | bytes 393224 | tf_op jit(solution)/shard_map/ppermute | solution.py:493
  145.4 0.0 collective-permute-start.6
  145.4 3.6 %collective-permute-done.5 = bf16[128,512]{1,0:T(8,128)(2,1)S(1)} collective-permute-done((bf16[128,512]{1,0:T(8,128)(2,1)S(1)}, bf16[128,512]{1,0:T(8,128)(2,1)S(1)}, u32[]{:S(2)}, u32[]{:S(2)}) %collective-permute-start.5) | collective-permute-done | bytes 131104 | tf_op jit(solution)/shard_map/ppermute | solution.py:493
  149.1 1.3 collective-permute-done.6
  150.4 0.8 add_convert_fusion
  151.2 3.7 %all-to-all-done.3 = bf16[32,16,2560]{2,1,0:T(8,128)(2,1)} async-done(((bf16[32,16,2560]{2,1,0:T(8,128)(2,1)}), bf16[32,16,2560]{2,1,0:T(8,128)(2,1)}, u32[]{:S(2)}, u32[]{:S(2)}) %all-to-all-start.3) | async-done | bytes 2621472 | tf_op jit(solution)/shard_map/all_to_all | solution.py:389
  154.9 3.5 %all-to-all-start.4 = ((bf16[16,16,512]{2,1,0:T(8,128)(2,1)}), bf16[16,16,512]{2,1,0:T(8,128)(2,1)S(1)}, u32[]{:S(2)}, u32[]{:S(2)}) async-start(bf16[16,16,512]{2,1,0:T(8,128)(2,1)} %bitcast.17), calls=%async_computation.4 | async-start | bytes 524288 | tf_op jit(solution)/shard_map/all_to_all | solution.py:509
  158.4 1.8 %fusion.direct_ref = f32[128,2048]{1,0:T(8,128)} fusion(bf16[128,512]{1,0:T(8,128)(2,1)S(1)} %get-tuple-element.37.embed_grad_ref, bf16[2048,512]{1,0:T(8,128)(2,1)S(1)} %copy-done.10), kind=kOutput, calls=%fused_computation.3 | convolution fusion | flops 268435456 | bytes 3276800 | tf_op jit(solution)/shard_map/dot_general | solution.py:43
  160.2 4.3 %shard_map.104 = bf16[128,2048]{1,0:T(8,128)(2,1)} custom-call(s32[4,128]{1,0:T(4,128)} %bitcast.29, f32[128,2048]{1,0:T(8,128)} %fusion.direct_ref, bf16[512,2560]{1,0:T(8,128)(2,1)} %bitcast.11.back_hbm), custom_call_target="tpu_custom_call" | custom-call | flops 536870912 | bytes 4194304 | tf_op jit(solution)/shard_map/pallas_call | solution.py:375
  164.4 2.4 %all-to-all-done.4 = bf16[16,16,512]{2,1,0:T(8,128)(2,1)S(1)} async-done(((bf16[16,16,512]{2,1,0:T(8,128)(2,1)}), bf16[16,16,512]{2,1,0:T(8,128)(2,1)S(1)}, u32[]{:S(2)}, u32[]{:S(2)}) %all-to-all-start.4) | async-done | bytes 262176 | tf_op jit(solution)/shard_map/all_to_all | solution.py:509
  166.9 0.6 broadcast_multiply_fusion
  (19 shorter events, 0.1 us)
Async XLA Ops:
  3.9 7.4 %copy-start.5 = (s32[1,128]{1,0:T(1,128)S(1)}, s32[1,128]{1,0:T(1,128)}, u32[]{:S(2)}) copy-start(s32[1,128]{1,0:T(1,128)} %matches_ref.1) | copy-start | bytes 1540
  3.9 42.1 %all-to-all-start = ((bf16[32,16,2560]{2,1,0:T(8,128)(2,1)}), bf16[32,16,2560]{2,1,0:T(8,128)(2,1)S(1)}, u32[]{:S(2)}, u32[]{:S(2)}) async-start(bf16[32,16,2560]{2,1,0:T(8,128)(2,1)} %bitcast.38), calls=%async_computation | async-start | bytes 5242880 | tf_op jit(solution)/shard_map/all_to_all | solution.py:389
  11.3 33.2 %collective-permute-start = (bf16[1,128]{1,0:T(2,128)(2,1)S(1)}, bf16[1,128]{1,0:T(2,128)(2,1)S(1)}, u32[]{:S(2)}, u32[]{:S(2)}) collective-permute-start(bf16[1,128]{1,0:T(2,128)(2,1)S(1)} %convert_element_type.12), channel_id=1, source_target_pairs={{0,16},{1,17},{2,18},{3,19},{4,20},{5,21},{6,22},{7,23},{8,24},{9,... | collective-permute-start | bytes 776 | tf_op jit(solution)/shard_map/ppermute | solution.py:411
  46.0 1.5 copy-start.9
  47.5 31.3 %copy-start.3 = (s32[128,4]{0,1:T(4,128)S(1)}, s32[128,4]{0,1:T(4,128)}, u32[]{:S(2)}) copy-start(s32[128,4]{0,1:T(4,128)} %param.8) | copy-start | bytes 6148
  47.5 31.3 %copy-start.4 = (f32[128,4]{0,1:T(4,128)S(1)}, f32[128,4]{0,1:T(4,128)}, u32[]{:S(2)}) copy-start(f32[128,4]{0,1:T(4,128)} %param.9) | copy-start | bytes 6148
  47.5 31.3 %copy-start.6 = (f32[128,512]{1,0:T(8,128)S(1)}, f32[128,512]{1,0:T(8,128)}, u32[]{:S(2)}) copy-start(f32[128,512]{1,0:T(8,128)} %get-tuple-element.34.base_ref) | copy-start | bytes 786436
  62.0 44.3 %slice-start = ((s8[11534336]{0:T(1024)(128)(4,1)}), s8[4194304]{0:T(1024)(128)(4,1)S(1)}, s32[]{:S(2)}) async-start(s8[11534336]{0:T(1024)(128)(4,1)} %bitcast.33), calls=%async_computation.5 | async-start | bytes 8388608
  79.8 7.7 %collective-permute-start.1 = (bf16[128,512]{1,0:T(8,128)(2,1)S(1)}, bf16[128,512]{1,0:T(8,128)(2,1)S(1)}, u32[]{:S(2)}, u32[]{:S(2)}) collective-permute-start(bf16[128,512]{1,0:T(8,128)(2,1)S(1)} %get-tuple-element.36.unit_ref), channel_id=1, source_target_pairs={{0,16},{1,17},{2,18},{3,19},{4,20},{5,21},{6,22},{7,23},{8,24},{9,... | collective-permute-start | bytes 393224 | tf_op jit(solution)/shard_map/ppermute | solution.py:452
  87.5 17.3 %copy-start.7 = (bf16[1408,512]{1,0:T(8,128)(2,1)S(1)}, bf16[1408,512]{1,0:T(8,128)(2,1)}, u32[]{:S(2)}) copy-start(bf16[1408,512]{1,0:T(8,128)(2,1)} %get-tuple-element.32.mixed_hbm.mixed_ref) | copy-start | bytes 4325380
  87.5 17.3 %copy-start.8 = (bf16[640,2816]{1,0:T(8,128)(2,1)S(1)}, bf16[640,2816]{1,0:T(8,128)(2,1)}, u32[]{:S(2)}) copy-start(bf16[640,2816]{1,0:T(8,128)(2,1)} %get-tuple-element.39.slopes_ref) | copy-start | bytes 10813444
  87.5 18.8 %slice-start.1 = ((s8[11534336]{0:T(1024)(128)(4,1)}), s8[4194304]{0:T(1024)(128)(4,1)S(1)}, s32[]{:S(2)}) async-start(s8[11534336]{0:T(1024)(128)(4,1)} %bitcast.33), calls=%async_computation.6 | async-start | bytes 8388608
  87.5 18.8 %slice-start.2 = ((s8[11534336]{0:T(1024)(128)(4,1)}), s8[3145728]{0:T(1024)(128)(4,1)S(1)}, s32[]{:S(2)}) async-start(s8[11534336]{0:T(1024)(128)(4,1)} %bitcast.33), calls=%async_computation.7 | async-start | bytes 6291456
  115.2 5.2 %copy-start.1 = (bf16[128,2048]{1,0:T(8,128)(2,1)S(1)}, bf16[128,2048]{1,0:T(8,128)(2,1)}, u32[]{:S(2)}) copy-start(bf16[128,2048]{1,0:T(8,128)(2,1)} %tokens_ref.1) | copy-start | bytes 1572868
  115.3 5.2 %copy-start.2 = (bf16[640,1408]{1,0:T(8,128)(2,1)S(1)}, bf16[640,1408]{1,0:T(8,128)(2,1)}, u32[]{:S(2)}) copy-start(bf16[640,1408]{1,0:T(8,128)(2,1)} %get-tuple-element.42.hidden_ref) | copy-start | bytes 5406724
  115.3 39.6 %all-to-all-start.3 = ((bf16[32,16,2560]{2,1,0:T(8,128)(2,1)}), bf16[32,16,2560]{2,1,0:T(8,128)(2,1)}, u32[]{:S(2)}, u32[]{:S(2)}) async-start(bf16[32,16,2560]{2,1,0:T(8,128)(2,1)} %bitcast.10), calls=%async_computation.3 | async-start | bytes 5242880 | tf_op jit(solution)/shard_map/all_to_all | solution.py:389
  120.5 2.6 %copy-start = (bf16[1,1408,2048]{2,1,0:T(8,128)(2,1)S(1)}, bf16[1,1408,2048]{2,1,0:T(8,128)(2,1)}, u32[]{:S(2)}) copy-start(bf16[1,1408,2048]{2,1,0:T(8,128)(2,1)} %param.11) | copy-start | bytes 17301508
  128.2 2.8 %collective-permute-start.2 = (bf16[1024,512]{1,0:T(8,128)(2,1)S(1)}, bf16[1024,512]{1,0:T(8,128)(2,1)S(1)}, u32[]{:S(2)}, u32[]{:S(2)}) collective-permute-start(bf16[1024,512]{1,0:T(8,128)(2,1)S(1)} %get-tuple-element.44), channel_id=1, source_target_pairs={{0,1},{1,0},{2,3},{3,2},{4,5},{5,4},{6,7},{7,6},{8,9},{9,8},{10,11... | collective-permute-start | bytes 3145736 | tf_op jit(solution)/shard_map/ppermute | solution.py:489
  131.1 27.3 %copy-start.10 = (bf16[2048,512]{1,0:T(8,128)(2,1)S(1)}, bf16[2048,512]{1,0:T(8,128)(2,1)}, u32[]{:S(2)}) copy-start(bf16[2048,512]{1,0:T(8,128)(2,1)} %head_hbm.1) | copy-start | bytes 6291460
  131.2 8.8 %collective-permute-start.3 = (bf16[2,128,512]{2,1,0:T(8,128)(2,1)S(1)}, bf16[2,128,512]{2,1,0:T(8,128)(2,1)S(1)}, u32[]{:S(2)}, u32[]{:S(2)}) collective-permute-start(bf16[2,128,512]{2,1,0:T(8,128)(2,1)S(1)} %get-tuple-element.46), channel_id=1, source_target_pairs={{0,32},{32,0},{64,96},{96,64},{1,33},{33,1},{65,97},{97,65},{2,34}... | collective-permute-start | bytes 786440 | tf_op jit(solution)/shard_map/ppermute | solution.py:493
  133.2 9.5 %collective-permute-start.4 = (bf16[2,128,512]{2,1,0:T(8,128)(2,1)S(1)}, bf16[2,128,512]{2,1,0:T(8,128)(2,1)S(1)}, u32[]{:S(2)}, u32[]{:S(2)}) collective-permute-start(bf16[2,128,512]{2,1,0:T(8,128)(2,1)S(1)} %get-tuple-element.48), channel_id=1, source_target_pairs={{0,96},{32,64},{64,32},{96,0},{1,97},{33,65},{65,33},{97,1},{2,98}... | collective-permute-start | bytes 786440 | tf_op jit(solution)/shard_map/ppermute | solution.py:493
  142.8 6.3 %collective-permute-start.5 = (bf16[128,512]{1,0:T(8,128)(2,1)S(1)}, bf16[128,512]{1,0:T(8,128)(2,1)S(1)}, u32[]{:S(2)}, u32[]{:S(2)}) collective-permute-start(bf16[128,512]{1,0:T(8,128)(2,1)S(1)} %get-tuple-element.50), channel_id=1, source_target_pairs={{0,96},{32,64},{64,32},{96,0},{1,97},{33,65},{65,33},{97,1},{2,98}... | collective-permute-start | bytes 393224 | tf_op jit(solution)/shard_map/ppermute | solution.py:493
  145.4 5.0 %collective-permute-start.6 = (bf16[128,512]{1,0:T(8,128)(2,1)S(1)}, bf16[128,512]{1,0:T(8,128)(2,1)S(1)}, u32[]{:S(2)}, u32[]{:S(2)}) collective-permute-start(bf16[128,512]{1,0:T(8,128)(2,1)S(1)} %get-tuple-element.51), channel_id=1, source_target_pairs={{0,32},{32,0},{64,96},{96,64},{1,33},{33,1},{65,97},{97,65},{2,34}... | collective-permute-start | bytes 393224 | tf_op jit(solution)/shard_map/ppermute | solution.py:493
  154.9 12.0 %all-to-all-start.4 = ((bf16[16,16,512]{2,1,0:T(8,128)(2,1)}), bf16[16,16,512]{2,1,0:T(8,128)(2,1)S(1)}, u32[]{:S(2)}, u32[]{:S(2)}) async-start(bf16[16,16,512]{2,1,0:T(8,128)(2,1)} %bitcast.17), calls=%async_computation.4 | async-start | bytes 524288 | tf_op jit(solution)/shard_map/all_to_all | solution.py:509

commit v7 on v6

--- a/solution.py
+++ b/solution.py
@@ -152,19 +152,27 @@
     extra_copy = bring(recv_hbm.at[:, pl.ds(WIDTH, quarter)], extra_ref, 7)
     main_copy = bring(recv_hbm.at[:, pl.ds(0, WIDTH)], x_ref.at[pl.ds(0, SLOTS), :], 8)
     groups = ((0, 1), (1, 3), (3, len(CHUNKS)))
-    weight_copies = []
-    for g, (begin, end) in enumerate(groups):
+
+    def bring_group(g):
+        begin, end = groups[g]
         lo, hi = CHUNKS[begin][0], CHUNKS[end - 1][1]
-        for h in range(2):
-            cols = pl.ds(h * HIDDEN + lo, hi - lo)
-            weight_copies.append(bring(w_hbm.at[:, cols], w_ref.at[:, cols], 1 + 2 * g + h))
-    mixed_copy = bring(mixed_hbm, mixed_ref, 0)
+        return [
+            bring(
+                w_hbm.at[:, pl.ds(h * HIDDEN + lo, hi - lo)],
+                w_ref.at[:, pl.ds(h * HIDDEN + lo, hi - lo)],
+                1 + 2 * g + h,
+            )
+            for h in range(2)
+        ]
+
+    weight_copies = bring_group(0)
     turned = unpacker()
     extra_copy.wait()
     spread = dot(turned, extra_ref[...]).astype(BF16)
     for j in range(4):
         x_ref[SLOTS:, j * quarter : (j + 1) * quarter] = spread[j * SPARE : (j + 1) * SPARE]
     main_copy.wait()
+    weight_copies += bring_group(1)
     outgoing = []
 
     def send(source, target, lo, wide):
@@ -176,6 +184,9 @@
     for g, (begin, end) in enumerate(groups):
         weight_copies[2 * g].wait()
         weight_copies[2 * g + 1].wait()
+        if g == 0:
+            weight_copies += bring_group(2)
+            mixed_copy = bring(mixed_hbm, mixed_ref, 0)
         for c in range(begin, end):
             lo, hi = CHUNKS[c]
             slot = c % 2

time: 168 us -> 168 us (level)
  no operation moved by 1% of the time
where the time goes in v7:
time: 168 us
  waiting for transfers between devices  49.7 us (30%)
  Pallas kernels  47.7 us (28%)
  blocking collectives  33 us (20%)
  starting transfers between devices  29 us (17%)
  local copies, waits for them, and re-layouts  4.21 us (3%)
  matrix products  1.79 us (1%)
    pallas_call x11, Pallas kernels, call(): pl.pallas_call(kernel, out_shape=tuple((jax.ShapeDtypeStruct(shape, dtype...  47.7 us
    all_to_all x2, blocking collectives, exchanged(): return lax.all_to_all(blocks, axes, 0, 0, tiled=True).reshape(rows, width)  33 us
    ppermute x1, waiting for transfers between devices, body(): partner_matches = lax.ppermute(matches.astype(BF16), EXPERT, partner)  22.1 us
    all_to_all x2, starting transfers between devices, exchanged(): return lax.all_to_all(blocks, axes, 0, 0, tiled=True).reshape(rows, width)  12.6 us
    ppermute x4, waiting for transfers between devices, around(): return lax.ppermute(value, 'dp', [(i, i ^ distance) for i in range(4)])  11.9 us
    ppermute x4, starting transfers between devices, around(): return lax.ppermute(value, 'dp', [(i, i ^ distance) for i in range(4)])  7.13 us
    ppermute x1, waiting for transfers between devices, body(): keys = lax.ppermute(unit, EXPERT, partner)  5.94 us
    all_to_all x2, waiting for transfers between devices, exchanged(): return lax.all_to_all(blocks, axes, 0, 0, tiled=True).reshape(rows, width)  5.05 us
  transfers between devices with their start and end apart: 10, of which 10 were waited for; matrix products, arithmetic and copies ran while one was open for 2% of the time, Pallas kernels for 10%

profile of v7, /device:TPU:0, one launch (start us, length us, event | category | flops | bytes accessed | tf_op | source)
XLA Modules:
  0.0 167.7 jit_solution(6372073502344031492)
XLA Ops:
  0.6 3.2 %shard_map.94 = bf16[512,2560]{1,0:T(8,128)(2,1)} custom-call(s32[4,128]{1,0:T(4,128)} %bitcast.28, bf16[128,2048]{1,0:T(8,128)(2,1)} %tokens_ref.1), custom_call_target="tpu_custom_call" | custom-call | flops 536870912 | bytes 3145728 | tf_op jit(solution)/shard_map/pallas_call | solution.py:386
  3.9 0.0 copy-start.5
  3.9 7.4 %all-to-all-start = ((bf16[32,16,2560]{2,1,0:T(8,128)(2,1)}), bf16[32,16,2560]{2,1,0:T(8,128)(2,1)S(1)}, u32[]{:S(2)}, u32[]{:S(2)}) async-start(bf16[32,16,2560]{2,1,0:T(8,128)(2,1)} %bitcast.38), calls=%async_computation | async-start | bytes 5242880 | tf_op jit(solution)/shard_map/all_to_all | solution.py:400
  11.3 0.0 copy-done.5
  11.3 3.4 %collective-permute-start = (bf16[1,128]{1,0:T(2,128)(2,1)S(1)}, bf16[1,128]{1,0:T(2,128)(2,1)S(1)}, u32[]{:S(2)}, u32[]{:S(2)}) collective-permute-start(bf16[1,128]{1,0:T(2,128)(2,1)S(1)} %convert_element_type.12), channel_id=1, source_target_pairs={{0,16},{1,17},{2,18},{3,19},{4,20},{5,21},{6,22},{7,23},{8,24},{9,... | collective-permute-start | bytes 776 | tf_op jit(solution)/shard_map/ppermute | solution.py:422
  14.7 7.8 %shard_map.95 = (bf16[1408,512]{1,0:T(8,128)(2,1)}, f32[128,512]{1,0:T(8,128)}) custom-call(bf16[1408,2048]{1,0:T(8,128)(2,1)} %bitcast.21, bf16[2048,512]{1,0:T(8,128)(2,1)} %head_hbm.1, bf16[128,2048]{1,0:T(8,128)(2,1)} %tokens_ref.1), custom_call_target="tpu_custom_call" | custom-call | flops 3221225472 | bytes 8388608 | tf_op jit(solution)/shard_map/pallas_call | solution.py:386
  22.5 22.1 %collective-permute-done.partner_ref = bf16[1,128]{1,0:T(2,128)(2,1)S(1)} collective-permute-done((bf16[1,128]{1,0:T(2,128)(2,1)S(1)}, bf16[1,128]{1,0:T(2,128)(2,1)S(1)}, u32[]{:S(2)}, u32[]{:S(2)}) %collective-permute-start) | collective-permute-done | bytes 288 | tf_op jit(solution)/shard_map/ppermute | solution.py:422
  44.6 1.4 all-to-all-done
  46.0 1.5 copy-done.9
  47.5 14.6 %shard_map.96 = (bf16[512,640]{1,0:T(8,128)(2,1)}, bf16[640,1408]{1,0:T(8,128)(2,1)}, bf16[640,2816]{1,0:T(8,128)(2,1)}) custom-call(bf16[512,2560]{1,0:T(8,128)(2,1)} %bitcast.39, bf16[2048,2816]{1,0:T(8,128)(2,1)} %bitcast.32, bf16[1408,512]{1,0:T(8,128)(2,1)} %get-tuple-element.32.mixed_hbm.mixed_ref), custom_call_target="tpu_custom_call" | custom-call | flops 8304721920 | bytes 23068672 | tf_op jit(solution)/shard_map/pallas_call | solution.py:386
  62.1 0.0 slice-start
  62.1 16.8 %all_to_all.25 = bf16[32,16,640]{2,1,0:T(8,128)(2,1)S(1)} all-to-all(bf16[32,16,640]{2,1,0:T(8,128)(2,1)} %bitcast.40), channel_id=1, replica_groups=mesh['dp'=4,'expert_0'=4,'expert_1'=4,'expert_2'=2] {'expert_0','expert_..., dimensions={0} | all-to-all | bytes 1310720 | tf_op jit(solution)/shard_map/all_to_all | solution.py:400
  79.0 0.0 copy-done.3
  79.0 0.0 copy-done.4
  79.0 0.0 copy-done.6
  79.0 0.9 shard_map.97
  79.9 1.8 %collective-permute-start.1 = (bf16[128,512]{1,0:T(8,128)(2,1)S(1)}, bf16[128,512]{1,0:T(8,128)(2,1)S(1)}, u32[]{:S(2)}, u32[]{:S(2)}) collective-permute-start(bf16[128,512]{1,0:T(8,128)(2,1)S(1)} %get-tuple-element.36.unit_ref), channel_id=1, source_target_pairs={{0,16},{1,17},{2,18},{3,19},{4,20},{5,21},{6,22},{7,23},{8,24},{9,... | collective-permute-start | bytes 393224 | tf_op jit(solution)/shard_map/ppermute | solution.py:463
  81.7 5.9 %collective-permute-done.1.key_ref = bf16[128,512]{1,0:T(8,128)(2,1)S(1)} collective-permute-done((bf16[128,512]{1,0:T(8,128)(2,1)S(1)}, bf16[128,512]{1,0:T(8,128)(2,1)S(1)}, u32[]{:S(2)}, u32[]{:S(2)}) %collective-permute-start.1) | collective-permute-done | bytes 131104 | tf_op jit(solution)/shard_map/ppermute | solution.py:463
  87.6 1.1 shard_map.98
  88.7 16.2 %all_to_all.26 = bf16[32,16,640]{2,1,0:T(8,128)(2,1)S(1)} all-to-all(bf16[32,16,640]{2,1,0:T(8,128)(2,1)S(1)} %bitcast.25), channel_id=1, replica_groups=mesh['dp'=4,'expert_0'=4,'expert_1'=4,'expert_2'=2] {'expert_0','expert_..., dimensions={0} | all-to-all | bytes 1310720 | tf_op jit(solution)/shard_map/all_to_all | solution.py:400
  104.9 0.0 copy-done.7
  104.9 1.4 shard_map.99
  106.4 9.0 %shard_map.100 = bf16[512,2560]{1,0:T(8,128)(2,1)} custom-call(bf16[640,2816]{1,0:T(8,128)(2,1)S(1)} %get-tuple-element.40.joined_ref, bf16[2048,2816]{1,0:T(8,128)(2,1)S(1)} %bitcast.35), custom_call_target="tpu_custom_call" | custom-call | flops 7381975040 | bytes 18874368 | tf_op jit(solution)/shard_map/pallas_call | solution.py:386
  115.4 0.0 copy-start.1
  115.4 0.0 copy-start.2
  115.4 5.2 %all-to-all-start.3 = ((bf16[32,16,2560]{2,1,0:T(8,128)(2,1)}), bf16[32,16,2560]{2,1,0:T(8,128)(2,1)}, u32[]{:S(2)}, u32[]{:S(2)}) async-start(bf16[32,16,2560]{2,1,0:T(8,128)(2,1)} %bitcast.10), calls=%async_computation.3 | async-start | bytes 5242880 | tf_op jit(solution)/shard_map/all_to_all | solution.py:400
  120.6 0.0 copy-start
  120.6 2.6 %copy-done = bf16[1,1408,2048]{2,1,0:T(8,128)(2,1)S(1)} copy-done((bf16[1,1408,2048]{2,1,0:T(8,128)(2,1)S(1)}, bf16[1,1408,2048]{2,1,0:T(8,128)(2,1)}, u32[]{:S(2)}) %copy-start) | copy-done | bytes 5767192
  123.3 5.1 %shard_map.101 = (f32[1024,512]{1,0:T(8,128)S(1)}, bf16[1024,512]{1,0:T(8,128)(2,1)S(1)}) custom-call(bf16[640,512]{1,0:T(8,128)(2,1)S(1)} %get-tuple-element.41.grads_ref, bf16[128,2048]{1,0:T(8,128)(2,1)S(1)} %copy-done.1, bf16[128,512]{1,0:T(8,128)(2,1)S(1)} %get-tuple-element.37.embed_grad_ref, bf16[640,1408]{1,0:T(8,128)(2,1)S(1)} %copy-done.2, ...), custom_call_target="tpu_custom_call" | custom-call | tf_op jit(solution)/shard_map/pallas_call | solution.py:386
  128.4 0.6 collective-permute-start.2
  128.9 2.3 %collective-permute-done.2 = bf16[1024,512]{1,0:T(8,128)(2,1)S(1)} collective-permute-done((bf16[1024,512]{1,0:T(8,128)(2,1)S(1)}, bf16[1024,512]{1,0:T(8,128)(2,1)S(1)}, u32[]{:S(2)}, u32[]{:S(2)}) %collective-permute-start.2) | collective-permute-done | bytes 1048608 | tf_op jit(solution)/shard_map/ppermute | solution.py:500
  131.2 0.2 shard_map.102
  131.4 2.0 %collective-permute-start.3 = (bf16[2,128,512]{2,1,0:T(8,128)(2,1)S(1)}, bf16[2,128,512]{2,1,0:T(8,128)(2,1)S(1)}, u32[]{:S(2)}, u32[]{:S(2)}) collective-permute-start(bf16[2,128,512]{2,1,0:T(8,128)(2,1)S(1)} %get-tuple-element.46), channel_id=1, source_target_pairs={{0,32},{32,0},{64,96},{96,64},{1,33},{33,1},{65,97},{97,65},{2,34}... | collective-permute-start | bytes 786440 | tf_op jit(solution)/shard_map/ppermute | solution.py:504
  133.4 2.5 %collective-permute-start.4 = (bf16[2,128,512]{2,1,0:T(8,128)(2,1)S(1)}, bf16[2,128,512]{2,1,0:T(8,128)(2,1)S(1)}, u32[]{:S(2)}, u32[]{:S(2)}) collective-permute-start(bf16[2,128,512]{2,1,0:T(8,128)(2,1)S(1)} %get-tuple-element.48), channel_id=1, source_target_pairs={{0,96},{32,64},{64,32},{96,0},{1,97},{33,65},{65,33},{97,1},{2,98}... | collective-permute-start | bytes 786440 | tf_op jit(solution)/shard_map/ppermute | solution.py:504
  135.9 4.3 %collective-permute-done.3.first_in_ref = bf16[2,128,512]{2,1,0:T(8,128)(2,1)S(1)} collective-permute-done((bf16[2,128,512]{2,1,0:T(8,128)(2,1)S(1)}, bf16[2,128,512]{2,1,0:T(8,128)(2,1)S(1)}, u32[]{:S(2)}, u32[]{:S(2)}) %collective-permute-start.3) | collective-permute-done | bytes 262176 | tf_op jit(solution)/shard_map/ppermute | solution.py:504
  140.2 2.7 %collective-permute-done.4.last_in_ref = bf16[2,128,512]{2,1,0:T(8,128)(2,1)S(1)} collective-permute-done((bf16[2,128,512]{2,1,0:T(8,128)(2,1)S(1)}, bf16[2,128,512]{2,1,0:T(8,128)(2,1)S(1)}, u32[]{:S(2)}, u32[]{:S(2)}) %collective-permute-start.4) | collective-permute-done | bytes 262176 | tf_op jit(solution)/shard_map/ppermute | solution.py:504
  142.9 0.1 shard_map.103
  143.0 2.6 %collective-permute-start.5 = (bf16[128,512]{1,0:T(8,128)(2,1)S(1)}, bf16[128,512]{1,0:T(8,128)(2,1)S(1)}, u32[]{:S(2)}, u32[]{:S(2)}) collective-permute-start(bf16[128,512]{1,0:T(8,128)(2,1)S(1)} %get-tuple-element.50), channel_id=1, source_target_pairs={{0,96},{32,64},{64,32},{96,0},{1,97},{33,65},{65,33},{97,1},{2,98}... | collective-permute-start | bytes 393224 | tf_op jit(solution)/shard_map/ppermute | solution.py:504
  145.6 0.0 collective-permute-start.6
  145.6 3.7 %collective-permute-done.5 = bf16[128,512]{1,0:T(8,128)(2,1)S(1)} collective-permute-done((bf16[128,512]{1,0:T(8,128)(2,1)S(1)}, bf16[128,512]{1,0:T(8,128)(2,1)S(1)}, u32[]{:S(2)}, u32[]{:S(2)}) %collective-permute-start.5) | collective-permute-done | bytes 131104 | tf_op jit(solution)/shard_map/ppermute | solution.py:504
  149.2 1.3 collective-permute-done.6
  150.6 0.8 add_convert_fusion
  151.3 3.7 %all-to-all-done.3 = bf16[32,16,2560]{2,1,0:T(8,128)(2,1)} async-done(((bf16[32,16,2560]{2,1,0:T(8,128)(2,1)}), bf16[32,16,2560]{2,1,0:T(8,128)(2,1)}, u32[]{:S(2)}, u32[]{:S(2)}) %all-to-all-start.3) | async-done | bytes 2621472 | tf_op jit(solution)/shard_map/all_to_all | solution.py:400
  155.0 3.5 %all-to-all-start.4 = ((bf16[16,16,512]{2,1,0:T(8,128)(2,1)}), bf16[16,16,512]{2,1,0:T(8,128)(2,1)S(1)}, u32[]{:S(2)}, u32[]{:S(2)}) async-start(bf16[16,16,512]{2,1,0:T(8,128)(2,1)} %bitcast.17), calls=%async_computation.4 | async-start | bytes 524288 | tf_op jit(solution)/shard_map/all_to_all | solution.py:520
  158.5 1.8 %fusion.direct_ref = f32[128,2048]{1,0:T(8,128)} fusion(bf16[128,512]{1,0:T(8,128)(2,1)S(1)} %get-tuple-element.37.embed_grad_ref, bf16[2048,512]{1,0:T(8,128)(2,1)S(1)} %copy-done.10), kind=kOutput, calls=%fused_computation.3 | convolution fusion | flops 268435456 | bytes 3276800 | tf_op jit(solution)/shard_map/dot_general | solution.py:43
  160.3 4.3 %shard_map.104 = bf16[128,2048]{1,0:T(8,128)(2,1)} custom-call(s32[4,128]{1,0:T(4,128)} %bitcast.29, f32[128,2048]{1,0:T(8,128)} %fusion.direct_ref, bf16[512,2560]{1,0:T(8,128)(2,1)} %bitcast.11.back_hbm), custom_call_target="tpu_custom_call" | custom-call | flops 536870912 | bytes 4194304 | tf_op jit(solution)/shard_map/pallas_call | solution.py:386
  164.6 2.4 %all-to-all-done.4 = bf16[16,16,512]{2,1,0:T(8,128)(2,1)S(1)} async-done(((bf16[16,16,512]{2,1,0:T(8,128)(2,1)}), bf16[16,16,512]{2,1,0:T(8,128)(2,1)S(1)}, u32[]{:S(2)}, u32[]{:S(2)}) %all-to-all-start.4) | async-done | bytes 262176 | tf_op jit(solution)/shard_map/all_to_all | solution.py:520
  167.0 0.6 broadcast_multiply_fusion
  (19 shorter events, 0.1 us)
Async XLA Ops:
  3.9 7.4 %copy-start.5 = (s32[1,128]{1,0:T(1,128)S(1)}, s32[1,128]{1,0:T(1,128)}, u32[]{:S(2)}) copy-start(s32[1,128]{1,0:T(1,128)} %matches_ref.1) | copy-start | bytes 1540
  3.9 42.1 %all-to-all-start = ((bf16[32,16,2560]{2,1,0:T(8,128)(2,1)}), bf16[32,16,2560]{2,1,0:T(8,128)(2,1)S(1)}, u32[]{:S(2)}, u32[]{:S(2)}) async-start(bf16[32,16,2560]{2,1,0:T(8,128)(2,1)} %bitcast.38), calls=%async_computation | async-start | bytes 5242880 | tf_op jit(solution)/shard_map/all_to_all | solution.py:400
  11.3 33.2 %collective-permute-start = (bf16[1,128]{1,0:T(2,128)(2,1)S(1)}, bf16[1,128]{1,0:T(2,128)(2,1)S(1)}, u32[]{:S(2)}, u32[]{:S(2)}) collective-permute-start(bf16[1,128]{1,0:T(2,128)(2,1)S(1)} %convert_element_type.12), channel_id=1, source_target_pairs={{0,16},{1,17},{2,18},{3,19},{4,20},{5,21},{6,22},{7,23},{8,24},{9,... | collective-permute-start | bytes 776 | tf_op jit(solution)/shard_map/ppermute | solution.py:422
  46.0 1.5 copy-start.9
  47.5 31.5 %copy-start.3 = (s32[128,4]{0,1:T(4,128)S(1)}, s32[128,4]{0,1:T(4,128)}, u32[]{:S(2)}) copy-start(s32[128,4]{0,1:T(4,128)} %param.8) | copy-start | bytes 6148
  47.5 31.5 %copy-start.4 = (f32[128,4]{0,1:T(4,128)S(1)}, f32[128,4]{0,1:T(4,128)}, u32[]{:S(2)}) copy-start(f32[128,4]{0,1:T(4,128)} %param.9) | copy-start | bytes 6148
  47.5 31.5 %copy-start.6 = (f32[128,512]{1,0:T(8,128)S(1)}, f32[128,512]{1,0:T(8,128)}, u32[]{:S(2)}) copy-start(f32[128,512]{1,0:T(8,128)} %get-tuple-element.34.base_ref) | copy-start | bytes 786436
  62.1 44.3 %slice-start = ((s8[11534336]{0:T(1024)(128)(4,1)}), s8[4194304]{0:T(1024)(128)(4,1)S(1)}, s32[]{:S(2)}) async-start(s8[11534336]{0:T(1024)(128)(4,1)} %bitcast.33), calls=%async_computation.5 | async-start | bytes 8388608
  79.9 7.7 %collective-permute-start.1 = (bf16[128,512]{1,0:T(8,128)(2,1)S(1)}, bf16[128,512]{1,0:T(8,128)(2,1)S(1)}, u32[]{:S(2)}, u32[]{:S(2)}) collective-permute-start(bf16[128,512]{1,0:T(8,128)(2,1)S(1)} %get-tuple-element.36.unit_ref), channel_id=1, source_target_pairs={{0,16},{1,17},{2,18},{3,19},{4,20},{5,21},{6,22},{7,23},{8,24},{9,... | collective-permute-start | bytes 393224 | tf_op jit(solution)/shard_map/ppermute | solution.py:463
  87.6 17.3 %copy-start.7 = (bf16[1408,512]{1,0:T(8,128)(2,1)S(1)}, bf16[1408,512]{1,0:T(8,128)(2,1)}, u32[]{:S(2)}) copy-start(bf16[1408,512]{1,0:T(8,128)(2,1)} %get-tuple-element.32.mixed_hbm.mixed_ref) | copy-start | bytes 4325380
  87.6 17.3 %copy-start.8 = (bf16[640,2816]{1,0:T(8,128)(2,1)S(1)}, bf16[640,2816]{1,0:T(8,128)(2,1)}, u32[]{:S(2)}) copy-start(bf16[640,2816]{1,0:T(8,128)(2,1)} %get-tuple-element.39.slopes_ref) | copy-start | bytes 10813444
  87.6 18.8 %slice-start.1 = ((s8[11534336]{0:T(1024)(128)(4,1)}), s8[4194304]{0:T(1024)(128)(4,1)S(1)}, s32[]{:S(2)}) async-start(s8[11534336]{0:T(1024)(128)(4,1)} %bitcast.33), calls=%async_computation.6 | async-start | bytes 8388608
  87.6 18.8 %slice-start.2 = ((s8[11534336]{0:T(1024)(128)(4,1)}), s8[3145728]{0:T(1024)(128)(4,1)S(1)}, s32[]{:S(2)}) async-start(s8[11534336]{0:T(1024)(128)(4,1)} %bitcast.33), calls=%async_computation.7 | async-start | bytes 6291456
  115.4 5.2 %copy-start.1 = (bf16[128,2048]{1,0:T(8,128)(2,1)S(1)}, bf16[128,2048]{1,0:T(8,128)(2,1)}, u32[]{:S(2)}) copy-start(bf16[128,2048]{1,0:T(8,128)(2,1)} %tokens_ref.1) | copy-start | bytes 1572868
  115.4 5.2 %copy-start.2 = (bf16[640,1408]{1,0:T(8,128)(2,1)S(1)}, bf16[640,1408]{1,0:T(8,128)(2,1)}, u32[]{:S(2)}) copy-start(bf16[640,1408]{1,0:T(8,128)(2,1)} %get-tuple-element.42.hidden_ref) | copy-start | bytes 5406724
  115.4 39.6 %all-to-all-start.3 = ((bf16[32,16,2560]{2,1,0:T(8,128)(2,1)}), bf16[32,16,2560]{2,1,0:T(8,128)(2,1)}, u32[]{:S(2)}, u32[]{:S(2)}) async-start(bf16[32,16,2560]{2,1,0:T(8,128)(2,1)} %bitcast.10), calls=%async_computation.3 | async-start | bytes 5242880 | tf_op jit(solution)/shard_map/all_to_all | solution.py:400
  120.6 2.6 %copy-start = (bf16[1,1408,2048]{2,1,0:T(8,128)(2,1)S(1)}, bf16[1,1408,2048]{2,1,0:T(8,128)(2,1)}, u32[]{:S(2)}) copy-start(bf16[1,1408,2048]{2,1,0:T(8,128)(2,1)} %param.11) | copy-start | bytes 17301508
  128.4 2.8 %collective-permute-start.2 = (bf16[1024,512]{1,0:T(8,128)(2,1)S(1)}, bf16[1024,512]{1,0:T(8,128)(2,1)S(1)}, u32[]{:S(2)}, u32[]{:S(2)}) collective-permute-start(bf16[1024,512]{1,0:T(8,128)(2,1)S(1)} %get-tuple-element.44), channel_id=1, source_target_pairs={{0,1},{1,0},{2,3},{3,2},{4,5},{5,4},{6,7},{7,6},{8,9},{9,8},{10,11... | collective-permute-start | bytes 3145736 | tf_op jit(solution)/shard_map/ppermute | solution.py:500
  131.2 27.3 %copy-start.10 = (bf16[2048,512]{1,0:T(8,128)(2,1)S(1)}, bf16[2048,512]{1,0:T(8,128)(2,1)}, u32[]{:S(2)}) copy-start(bf16[2048,512]{1,0:T(8,128)(2,1)} %head_hbm.1) | copy-start | bytes 6291460
  131.4 8.8 %collective-permute-start.3 = (bf16[2,128,512]{2,1,0:T(8,128)(2,1)S(1)}, bf16[2,128,512]{2,1,0:T(8,128)(2,1)S(1)}, u32[]{:S(2)}, u32[]{:S(2)}) collective-permute-start(bf16[2,128,512]{2,1,0:T(8,128)(2,1)S(1)} %get-tuple-element.46), channel_id=1, source_target_pairs={{0,32},{32,0},{64,96},{96,64},{1,33},{33,1},{65,97},{97,65},{2,34}... | collective-permute-start | bytes 786440 | tf_op jit(solution)/shard_map/ppermute | solution.py:504
  133.4 9.5 %collective-permute-start.4 = (bf16[2,128,512]{2,1,0:T(8,128)(2,1)S(1)}, bf16[2,128,512]{2,1,0:T(8,128)(2,1)S(1)}, u32[]{:S(2)}, u32[]{:S(2)}) collective-permute-start(bf16[2,128,512]{2,1,0:T(8,128)(2,1)S(1)} %get-tuple-element.48), channel_id=1, source_target_pairs={{0,96},{32,64},{64,32},{96,0},{1,97},{33,65},{65,33},{97,1},{2,98}... | collective-permute-start | bytes 786440 | tf_op jit(solution)/shard_map/ppermute | solution.py:504
  143.0 6.3 %collective-permute-start.5 = (bf16[128,512]{1,0:T(8,128)(2,1)S(1)}, bf16[128,512]{1,0:T(8,128)(2,1)S(1)}, u32[]{:S(2)}, u32[]{:S(2)}) collective-permute-start(bf16[128,512]{1,0:T(8,128)(2,1)S(1)} %get-tuple-element.50), channel_id=1, source_target_pairs={{0,96},{32,64},{64,32},{96,0},{1,97},{33,65},{65,33},{97,1},{2,98}... | collective-permute-start | bytes 393224 | tf_op jit(solution)/shard_map/ppermute | solution.py:504
  145.6 5.0 %collective-permute-start.6 = (bf16[128,512]{1,0:T(8,128)(2,1)S(1)}, bf16[128,512]{1,0:T(8,128)(2,1)S(1)}, u32[]{:S(2)}, u32[]{:S(2)}) collective-permute-start(bf16[128,512]{1,0:T(8,128)(2,1)S(1)} %get-tuple-element.51), channel_id=1, source_target_pairs={{0,32},{32,0},{64,96},{96,64},{1,33},{33,1},{65,97},{97,65},{2,34}... | collective-permute-start | bytes 393224 | tf_op jit(solution)/shard_map/ppermute | solution.py:504
  155.0 12.0 %all-to-all-start.4 = ((bf16[16,16,512]{2,1,0:T(8,128)(2,1)}), bf16[16,16,512]{2,1,0:T(8,128)(2,1)S(1)}, u32[]{:S(2)}, u32[]{:S(2)}) async-start(bf16[16,16,512]{2,1,0:T(8,128)(2,1)} %bitcast.17), calls=%async_computation.4 | async-start | bytes 524288 | tf_op jit(solution)/shard_map/all_to_all | solution.py:520

commit v8 on v6

--- a/solution.py
+++ b/solution.py
@@ -440,7 +440,7 @@
             dma((9,)),
             dma((10,)),
         ],
-        flops=2 * TOTAL * HIDDEN * (2 * WIDTH + EMBED), moved=22 << 20, limit=56.5,
+        flops=2 * TOTAL * HIDDEN * (2 * WIDTH + EMBED), moved=22 << 20, limit=49,
     )
     answer = exchanged(packed, EXPERT, EXPERTS)
     embedding, unit = call(

time: 168 us -> 166 us (0.988)
    unnamed x28 -> x24, local copies, waits for them, and re-layouts: 4.21 us -> 4.04 us
where the time goes in v8:
time: 166 us
  waiting for transfers between devices  49.8 us (30%)
  Pallas kernels  46.7 us (28%)
  blocking collectives  32.3 us (19%)
  starting transfers between devices  29 us (17%)
  local copies, waits for them, and re-layouts  4.04 us (2%)
  matrix products  1.82 us (1%)
    pallas_call x11, Pallas kernels, call(): pl.pallas_call(kernel, out_shape=tuple((jax.ShapeDtypeStruct(shape, dtype...  46.7 us
    all_to_all x2, blocking collectives, exchanged(): return lax.all_to_all(blocks, axes, 0, 0, tiled=True).reshape(rows, width)  32.3 us
    ppermute x1, waiting for transfers between devices, body(): partner_matches = lax.ppermute(matches.astype(BF16), EXPERT, partner)  22.1 us
    all_to_all x2, starting transfers between devices, exchanged(): return lax.all_to_all(blocks, axes, 0, 0, tiled=True).reshape(rows, width)  12.7 us
    ppermute x4, waiting for transfers between devices, around(): return lax.ppermute(value, 'dp', [(i, i ^ distance) for i in range(4)])  11.9 us
    ppermute x4, starting transfers between devices, around(): return lax.ppermute(value, 'dp', [(i, i ^ distance) for i in range(4)])  7.13 us
    ppermute x1, waiting for transfers between devices, body(): keys = lax.ppermute(unit, EXPERT, partner)  5.94 us
    all_to_all x2, waiting for transfers between devices, exchanged(): return lax.all_to_all(blocks, axes, 0, 0, tiled=True).reshape(rows, width)  5.15 us
  transfers between devices with their start and end apart: 10, of which 10 were waited for; matrix products, arithmetic and copies ran while one was open for 2% of the time, Pallas kernels for 10%

profile of v8, /device:TPU:0, one launch (start us, length us, event | category | flops | bytes accessed | tf_op | source)
XLA Modules:
  0.0 165.9 jit_solution(10763725026274495532)
XLA Ops:
  0.6 3.2 %shard_map.94 = bf16[512,2560]{1,0:T(8,128)(2,1)} custom-call(s32[4,128]{1,0:T(4,128)} %bitcast.29, bf16[128,2048]{1,0:T(8,128)(2,1)} %tokens_ref.1), custom_call_target="tpu_custom_call" | custom-call | flops 536870912 | bytes 3145728 | tf_op jit(solution)/shard_map/pallas_call | solution.py:375
  3.9 0.0 copy-start.4
  3.9 7.5 %all-to-all-start = ((bf16[32,16,2560]{2,1,0:T(8,128)(2,1)}), bf16[32,16,2560]{2,1,0:T(8,128)(2,1)}, u32[]{:S(2)}, u32[]{:S(2)}) async-start(bf16[32,16,2560]{2,1,0:T(8,128)(2,1)} %bitcast.39), calls=%async_computation | async-start | bytes 5242880 | tf_op jit(solution)/shard_map/all_to_all | solution.py:389
  11.4 0.0 copy-done.4
  11.4 3.3 %collective-permute-start = (bf16[1,128]{1,0:T(2,128)(2,1)S(1)}, bf16[1,128]{1,0:T(2,128)(2,1)S(1)}, u32[]{:S(2)}, u32[]{:S(2)}) collective-permute-start(bf16[1,128]{1,0:T(2,128)(2,1)S(1)} %convert_element_type.12), channel_id=1, source_target_pairs={{0,16},{1,17},{2,18},{3,19},{4,20},{5,21},{6,22},{7,23},{8,24},{9,... | collective-permute-start | bytes 776 | tf_op jit(solution)/shard_map/ppermute | solution.py:411
  14.8 7.7 %shard_map.95 = (bf16[1408,512]{1,0:T(8,128)(2,1)}, f32[128,512]{1,0:T(8,128)}) custom-call(bf16[1408,2048]{1,0:T(8,128)(2,1)} %bitcast.21, bf16[2048,512]{1,0:T(8,128)(2,1)} %head_hbm.1, bf16[128,2048]{1,0:T(8,128)(2,1)} %tokens_ref.1), custom_call_target="tpu_custom_call" | custom-call | flops 3221225472 | bytes 8388608 | tf_op jit(solution)/shard_map/pallas_call | solution.py:375
  22.5 22.1 %collective-permute-done.partner_ref = bf16[1,128]{1,0:T(2,128)(2,1)S(1)} collective-permute-done((bf16[1,128]{1,0:T(2,128)(2,1)S(1)}, bf16[1,128]{1,0:T(2,128)(2,1)S(1)}, u32[]{:S(2)}, u32[]{:S(2)}) %collective-permute-start) | collective-permute-done | bytes 288 | tf_op jit(solution)/shard_map/ppermute | solution.py:411
  44.6 1.4 all-to-all-done
  46.0 1.4 copy-done.6
  47.4 13.7 %shard_map.96 = (bf16[512,640]{1,0:T(8,128)(2,1)S(1)}, bf16[640,1408]{1,0:T(8,128)(2,1)S(1)}, bf16[640,2816]{1,0:T(8,128)(2,1)}) custom-call(bf16[512,2560]{1,0:T(8,128)(2,1)} %bitcast.3.recv_hbm, bf16[2048,2816]{1,0:T(8,128)(2,1)} %bitcast.33, bf16[1408,512]{1,0:T(8,128)(2,1)S(1)} %copy-done.6), custom_call_target="tpu_custom_call" | custom-call | flops 8304721920 | bytes 23068672 | tf_op jit(solution)/shard_map/pallas_call | solution.py:375
  61.2 0.0 slice-start
  61.2 16.1 %all_to_all.25 = bf16[32,16,640]{2,1,0:T(8,128)(2,1)S(1)} all-to-all(bf16[32,16,640]{2,1,0:T(8,128)(2,1)S(1)} %bitcast.27), channel_id=1, replica_groups=mesh['dp'=4,'expert_0'=4,'expert_1'=4,'expert_2'=2] {'expert_0','expert_..., dimensions={0} | all-to-all | bytes 1310720 | tf_op jit(solution)/shard_map/all_to_all | solution.py:389
  77.3 0.0 copy-done.2
  77.3 0.0 copy-done.3
  77.3 0.0 copy-done.5
  77.3 0.9 shard_map.97
  78.2 1.7 %collective-permute-start.1 = (bf16[128,512]{1,0:T(8,128)(2,1)S(1)}, bf16[128,512]{1,0:T(8,128)(2,1)S(1)}, u32[]{:S(2)}, u32[]{:S(2)}) collective-permute-start(bf16[128,512]{1,0:T(8,128)(2,1)S(1)} %get-tuple-element.36.unit_ref), channel_id=1, source_target_pairs={{0,16},{1,17},{2,18},{3,19},{4,20},{5,21},{6,22},{7,23},{8,24},{9,... | collective-permute-start | bytes 393224 | tf_op jit(solution)/shard_map/ppermute | solution.py:452
  80.0 5.9 %collective-permute-done.1.key_ref = bf16[128,512]{1,0:T(8,128)(2,1)S(1)} collective-permute-done((bf16[128,512]{1,0:T(8,128)(2,1)S(1)}, bf16[128,512]{1,0:T(8,128)(2,1)S(1)}, u32[]{:S(2)}, u32[]{:S(2)}) %collective-permute-start.1) | collective-permute-done | bytes 131104 | tf_op jit(solution)/shard_map/ppermute | solution.py:452
  85.9 1.1 shard_map.98
  87.0 16.2 %all_to_all.26 = bf16[32,16,640]{2,1,0:T(8,128)(2,1)S(1)} all-to-all(bf16[32,16,640]{2,1,0:T(8,128)(2,1)S(1)} %bitcast.25), channel_id=1, replica_groups=mesh['dp'=4,'expert_0'=4,'expert_1'=4,'expert_2'=2] {'expert_0','expert_..., dimensions={0} | all-to-all | bytes 1310720 | tf_op jit(solution)/shard_map/all_to_all | solution.py:389
  103.2 0.0 copy-done.7
  103.2 1.4 shard_map.99
  104.7 0.0 slice-done
  104.7 9.0 %shard_map.100 = bf16[512,2560]{1,0:T(8,128)(2,1)} custom-call(bf16[640,2816]{1,0:T(8,128)(2,1)S(1)} %get-tuple-element.40.joined_ref, bf16[2048,2816]{1,0:T(8,128)(2,1)S(1)} %bitcast.36), custom_call_target="tpu_custom_call" | custom-call | flops 7381975040 | bytes 18874368 | tf_op jit(solution)/shard_map/pallas_call | solution.py:375
  113.7 0.0 copy-start.1
  113.7 5.2 %all-to-all-start.3 = ((bf16[32,16,2560]{2,1,0:T(8,128)(2,1)}), bf16[32,16,2560]{2,1,0:T(8,128)(2,1)}, u32[]{:S(2)}, u32[]{:S(2)}) async-start(bf16[32,16,2560]{2,1,0:T(8,128)(2,1)} %bitcast.10), calls=%async_computation.3 | async-start | bytes 5242880 | tf_op jit(solution)/shard_map/all_to_all | solution.py:389
  118.9 0.0 copy-start
  118.9 2.6 %copy-done = bf16[1,1408,2048]{2,1,0:T(8,128)(2,1)S(1)} copy-done((bf16[1,1408,2048]{2,1,0:T(8,128)(2,1)S(1)}, bf16[1,1408,2048]{2,1,0:T(8,128)(2,1)}, u32[]{:S(2)}) %copy-start) | copy-done | bytes 5767192
  121.5 5.1 %shard_map.101 = (f32[1024,512]{1,0:T(8,128)S(1)}, bf16[1024,512]{1,0:T(8,128)(2,1)S(1)}) custom-call(bf16[640,512]{1,0:T(8,128)(2,1)S(1)} %get-tuple-element.41.grads_ref, bf16[128,2048]{1,0:T(8,128)(2,1)S(1)} %copy-done.1, bf16[128,512]{1,0:T(8,128)(2,1)S(1)} %get-tuple-element.37.embed_grad_ref, bf16[640,1408]{1,0:T(8,128)(2,1)S(1)} %get-tuple-element.42.hidden_ref, ...), custom_call_target="tpu_custom_call" | custom-call | tf_op jit(solution)/shard_map/pallas_call | solution.py:375
  126.6 0.5 collective-permute-start.2
  127.2 2.3 %collective-permute-done.2 = bf16[1024,512]{1,0:T(8,128)(2,1)S(1)} collective-permute-done((bf16[1024,512]{1,0:T(8,128)(2,1)S(1)}, bf16[1024,512]{1,0:T(8,128)(2,1)S(1)}, u32[]{:S(2)}, u32[]{:S(2)}) %collective-permute-start.2) | collective-permute-done | bytes 1048608 | tf_op jit(solution)/shard_map/ppermute | solution.py:489
  129.5 0.2 shard_map.102
  129.6 2.0 %collective-permute-start.3 = (bf16[2,128,512]{2,1,0:T(8,128)(2,1)S(1)}, bf16[2,128,512]{2,1,0:T(8,128)(2,1)S(1)}, u32[]{:S(2)}, u32[]{:S(2)}) collective-permute-start(bf16[2,128,512]{2,1,0:T(8,128)(2,1)S(1)} %get-tuple-element.46), channel_id=1, source_target_pairs={{0,32},{32,0},{64,96},{96,64},{1,33},{33,1},{65,97},{97,65},{2,34}... | collective-permute-start | bytes 786440 | tf_op jit(solution)/shard_map/ppermute | solution.py:493
  131.6 2.5 %collective-permute-start.4 = (bf16[2,128,512]{2,1,0:T(8,128)(2,1)S(1)}, bf16[2,128,512]{2,1,0:T(8,128)(2,1)S(1)}, u32[]{:S(2)}, u32[]{:S(2)}) collective-permute-start(bf16[2,128,512]{2,1,0:T(8,128)(2,1)S(1)} %get-tuple-element.48), channel_id=1, source_target_pairs={{0,96},{32,64},{64,32},{96,0},{1,97},{33,65},{65,33},{97,1},{2,98}... | collective-permute-start | bytes 786440 | tf_op jit(solution)/shard_map/ppermute | solution.py:493
  134.2 4.3 %collective-permute-done.3.first_in_ref = bf16[2,128,512]{2,1,0:T(8,128)(2,1)S(1)} collective-permute-done((bf16[2,128,512]{2,1,0:T(8,128)(2,1)S(1)}, bf16[2,128,512]{2,1,0:T(8,128)(2,1)S(1)}, u32[]{:S(2)}, u32[]{:S(2)}) %collective-permute-start.3) | collective-permute-done | bytes 262176 | tf_op jit(solution)/shard_map/ppermute | solution.py:493
  138.5 2.7 %collective-permute-done.4.last_in_ref = bf16[2,128,512]{2,1,0:T(8,128)(2,1)S(1)} collective-permute-done((bf16[2,128,512]{2,1,0:T(8,128)(2,1)S(1)}, bf16[2,128,512]{2,1,0:T(8,128)(2,1)S(1)}, u32[]{:S(2)}, u32[]{:S(2)}) %collective-permute-start.4) | collective-permute-done | bytes 262176 | tf_op jit(solution)/shard_map/ppermute | solution.py:493
  141.1 0.1 shard_map.103
  141.2 2.6 %collective-permute-start.5 = (bf16[128,512]{1,0:T(8,128)(2,1)S(1)}, bf16[128,512]{1,0:T(8,128)(2,1)S(1)}, u32[]{:S(2)}, u32[]{:S(2)}) collective-permute-start(bf16[128,512]{1,0:T(8,128)(2,1)S(1)} %get-tuple-element.50), channel_id=1, source_target_pairs={{0,96},{32,64},{64,32},{96,0},{1,97},{33,65},{65,33},{97,1},{2,98}... | collective-permute-start | bytes 393224 | tf_op jit(solution)/shard_map/ppermute | solution.py:493
  143.8 0.0 collective-permute-start.6
  143.8 3.7 %collective-permute-done.5 = bf16[128,512]{1,0:T(8,128)(2,1)S(1)} collective-permute-done((bf16[128,512]{1,0:T(8,128)(2,1)S(1)}, bf16[128,512]{1,0:T(8,128)(2,1)S(1)}, u32[]{:S(2)}, u32[]{:S(2)}) %collective-permute-start.5) | collective-permute-done | bytes 131104 | tf_op jit(solution)/shard_map/ppermute | solution.py:493
  147.5 1.3 collective-permute-done.6
  148.8 0.8 add_convert_fusion
  149.6 3.7 %all-to-all-done.3 = bf16[32,16,2560]{2,1,0:T(8,128)(2,1)} async-done(((bf16[32,16,2560]{2,1,0:T(8,128)(2,1)}), bf16[32,16,2560]{2,1,0:T(8,128)(2,1)}, u32[]{:S(2)}, u32[]{:S(2)}) %all-to-all-start.3) | async-done | bytes 2621472 | tf_op jit(solution)/shard_map/all_to_all | solution.py:389
  153.3 3.5 %all-to-all-start.4 = ((bf16[16,16,512]{2,1,0:T(8,128)(2,1)}), bf16[16,16,512]{2,1,0:T(8,128)(2,1)S(1)}, u32[]{:S(2)}, u32[]{:S(2)}) async-start(bf16[16,16,512]{2,1,0:T(8,128)(2,1)} %bitcast.17), calls=%async_computation.4 | async-start | bytes 524288 | tf_op jit(solution)/shard_map/all_to_all | solution.py:509
  156.8 1.8 %fusion.direct_ref = f32[128,2048]{1,0:T(8,128)} fusion(bf16[128,512]{1,0:T(8,128)(2,1)S(1)} %get-tuple-element.37.embed_grad_ref, bf16[2048,512]{1,0:T(8,128)(2,1)S(1)} %copy-done.8), kind=kOutput, calls=%fused_computation.3 | convolution fusion | flops 268435456 | bytes 3276800 | tf_op jit(solution)/shard_map/dot_general | solution.py:43
  158.6 4.3 %shard_map.104 = bf16[128,2048]{1,0:T(8,128)(2,1)} custom-call(s32[4,128]{1,0:T(4,128)} %bitcast.30, f32[128,2048]{1,0:T(8,128)} %fusion.direct_ref, bf16[512,2560]{1,0:T(8,128)(2,1)} %bitcast.11.back_hbm), custom_call_target="tpu_custom_call" | custom-call | flops 536870912 | bytes 4194304 | tf_op jit(solution)/shard_map/pallas_call | solution.py:375
  162.9 2.4 %all-to-all-done.4 = bf16[16,16,512]{2,1,0:T(8,128)(2,1)S(1)} async-done(((bf16[16,16,512]{2,1,0:T(8,128)(2,1)}), bf16[16,16,512]{2,1,0:T(8,128)(2,1)S(1)}, u32[]{:S(2)}, u32[]{:S(2)}) %all-to-all-start.4) | async-done | bytes 262176 | tf_op jit(solution)/shard_map/all_to_all | solution.py:509
  165.3 0.6 broadcast_multiply_fusion
  (15 shorter events, 0.1 us)
Async XLA Ops:
  3.9 7.6 %copy-start.4 = (s32[1,128]{1,0:T(1,128)S(1)}, s32[1,128]{1,0:T(1,128)}, u32[]{:S(2)}) copy-start(s32[1,128]{1,0:T(1,128)} %matches_ref.1) | copy-start | bytes 1540
  3.9 42.2 %all-to-all-start = ((bf16[32,16,2560]{2,1,0:T(8,128)(2,1)}), bf16[32,16,2560]{2,1,0:T(8,128)(2,1)}, u32[]{:S(2)}, u32[]{:S(2)}) async-start(bf16[32,16,2560]{2,1,0:T(8,128)(2,1)} %bitcast.39), calls=%async_computation | async-start | bytes 5242880 | tf_op jit(solution)/shard_map/all_to_all | solution.py:389
  11.4 33.2 %collective-permute-start = (bf16[1,128]{1,0:T(2,128)(2,1)S(1)}, bf16[1,128]{1,0:T(2,128)(2,1)S(1)}, u32[]{:S(2)}, u32[]{:S(2)}) collective-permute-start(bf16[1,128]{1,0:T(2,128)(2,1)S(1)} %convert_element_type.12), channel_id=1, source_target_pairs={{0,16},{1,17},{2,18},{3,19},{4,20},{5,21},{6,22},{7,23},{8,24},{9,... | collective-permute-start | bytes 776 | tf_op jit(solution)/shard_map/ppermute | solution.py:411
  46.0 1.4 copy-start.6
  47.4 29.9 %copy-start.2 = (s32[128,4]{0,1:T(4,128)S(1)}, s32[128,4]{0,1:T(4,128)}, u32[]{:S(2)}) copy-start(s32[128,4]{0,1:T(4,128)} %param.8) | copy-start | bytes 6148
  47.4 29.9 %copy-start.3 = (f32[128,4]{0,1:T(4,128)S(1)}, f32[128,4]{0,1:T(4,128)}, u32[]{:S(2)}) copy-start(f32[128,4]{0,1:T(4,128)} %param.9) | copy-start | bytes 6148
  47.4 29.9 %copy-start.5 = (f32[128,512]{1,0:T(8,128)S(1)}, f32[128,512]{1,0:T(8,128)}, u32[]{:S(2)}) copy-start(f32[128,512]{1,0:T(8,128)} %get-tuple-element.34.base_ref) | copy-start | bytes 786436
  61.2 43.5 %slice-start = ((s8[11534336]{0:T(1024)(128)(4,1)}), s8[4194304]{0:T(1024)(128)(4,1)S(1)}, s32[]{:S(2)}) async-start(s8[11534336]{0:T(1024)(128)(4,1)} %bitcast.34), calls=%async_computation.5 | async-start | bytes 8388608
  78.2 7.7 %collective-permute-start.1 = (bf16[128,512]{1,0:T(8,128)(2,1)S(1)}, bf16[128,512]{1,0:T(8,128)(2,1)S(1)}, u32[]{:S(2)}, u32[]{:S(2)}) collective-permute-start(bf16[128,512]{1,0:T(8,128)(2,1)S(1)} %get-tuple-element.36.unit_ref), channel_id=1, source_target_pairs={{0,16},{1,17},{2,18},{3,19},{4,20},{5,21},{6,22},{7,23},{8,24},{9,... | collective-permute-start | bytes 393224 | tf_op jit(solution)/shard_map/ppermute | solution.py:452
  85.9 17.4 %copy-start.7 = (bf16[640,2816]{1,0:T(8,128)(2,1)S(1)}, bf16[640,2816]{1,0:T(8,128)(2,1)}, u32[]{:S(2)}) copy-start(bf16[640,2816]{1,0:T(8,128)(2,1)} %get-tuple-element.39.slopes_ref) | copy-start | bytes 10813444
  85.9 18.8 %slice-start.1 = ((s8[11534336]{0:T(1024)(128)(4,1)}), s8[4194304]{0:T(1024)(128)(4,1)S(1)}, s32[]{:S(2)}) async-start(s8[11534336]{0:T(1024)(128)(4,1)} %bitcast.34), calls=%async_computation.6 | async-start | bytes 8388608
  85.9 18.8 %slice-start.2 = ((s8[11534336]{0:T(1024)(128)(4,1)}), s8[3145728]{0:T(1024)(128)(4,1)S(1)}, s32[]{:S(2)}) async-start(s8[11534336]{0:T(1024)(128)(4,1)} %bitcast.34), calls=%async_computation.7 | async-start | bytes 6291456
  113.7 5.2 %copy-start.1 = (bf16[128,2048]{1,0:T(8,128)(2,1)S(1)}, bf16[128,2048]{1,0:T(8,128)(2,1)}, u32[]{:S(2)}) copy-start(bf16[128,2048]{1,0:T(8,128)(2,1)} %tokens_ref.1) | copy-start | bytes 1572868
  113.7 39.6 %all-to-all-start.3 = ((bf16[32,16,2560]{2,1,0:T(8,128)(2,1)}), bf16[32,16,2560]{2,1,0:T(8,128)(2,1)}, u32[]{:S(2)}, u32[]{:S(2)}) async-start(bf16[32,16,2560]{2,1,0:T(8,128)(2,1)} %bitcast.10), calls=%async_computation.3 | async-start | bytes 5242880 | tf_op jit(solution)/shard_map/all_to_all | solution.py:389
  118.9 2.6 %copy-start = (bf16[1,1408,2048]{2,1,0:T(8,128)(2,1)S(1)}, bf16[1,1408,2048]{2,1,0:T(8,128)(2,1)}, u32[]{:S(2)}) copy-start(bf16[1,1408,2048]{2,1,0:T(8,128)(2,1)} %param.11) | copy-start | bytes 17301508
  126.6 2.8 %collective-permute-start.2 = (bf16[1024,512]{1,0:T(8,128)(2,1)S(1)}, bf16[1024,512]{1,0:T(8,128)(2,1)S(1)}, u32[]{:S(2)}, u32[]{:S(2)}) collective-permute-start(bf16[1024,512]{1,0:T(8,128)(2,1)S(1)} %get-tuple-element.44), channel_id=1, source_target_pairs={{0,1},{1,0},{2,3},{3,2},{4,5},{5,4},{6,7},{7,6},{8,9},{9,8},{10,11... | collective-permute-start | bytes 3145736 | tf_op jit(solution)/shard_map/ppermute | solution.py:489
  129.5 27.3 %copy-start.8 = (bf16[2048,512]{1,0:T(8,128)(2,1)S(1)}, bf16[2048,512]{1,0:T(8,128)(2,1)}, u32[]{:S(2)}) copy-start(bf16[2048,512]{1,0:T(8,128)(2,1)} %head_hbm.1) | copy-start | bytes 6291460
  129.6 8.8 %collective-permute-start.3 = (bf16[2,128,512]{2,1,0:T(8,128)(2,1)S(1)}, bf16[2,128,512]{2,1,0:T(8,128)(2,1)S(1)}, u32[]{:S(2)}, u32[]{:S(2)}) collective-permute-start(bf16[2,128,512]{2,1,0:T(8,128)(2,1)S(1)} %get-tuple-element.46), channel_id=1, source_target_pairs={{0,32},{32,0},{64,96},{96,64},{1,33},{33,1},{65,97},{97,65},{2,34}... | collective-permute-start | bytes 786440 | tf_op jit(solution)/shard_map/ppermute | solution.py:493
  131.6 9.5 %collective-permute-start.4 = (bf16[2,128,512]{2,1,0:T(8,128)(2,1)S(1)}, bf16[2,128,512]{2,1,0:T(8,128)(2,1)S(1)}, u32[]{:S(2)}, u32[]{:S(2)}) collective-permute-start(bf16[2,128,512]{2,1,0:T(8,128)(2,1)S(1)} %get-tuple-element.48), channel_id=1, source_target_pairs={{0,96},{32,64},{64,32},{96,0},{1,97},{33,65},{65,33},{97,1},{2,98}... | collective-permute-start | bytes 786440 | tf_op jit(solution)/shard_map/ppermute | solution.py:493
  141.2 6.3 %collective-permute-start.5 = (bf16[128,512]{1,0:T(8,128)(2,1)S(1)}, bf16[128,512]{1,0:T(8,128)(2,1)S(1)}, u32[]{:S(2)}, u32[]{:S(2)}) collective-permute-start(bf16[128,512]{1,0:T(8,128)(2,1)S(1)} %get-tuple-element.50), channel_id=1, source_target_pairs={{0,96},{32,64},{64,32},{96,0},{1,97},{33,65},{65,33},{97,1},{2,98}... | collective-permute-start | bytes 393224 | tf_op jit(solution)/shard_map/ppermute | solution.py:493
  143.8 5.0 %collective-permute-start.6 = (bf16[128,512]{1,0:T(8,128)(2,1)S(1)}, bf16[128,512]{1,0:T(8,128)(2,1)S(1)}, u32[]{:S(2)}, u32[]{:S(2)}) collective-permute-start(bf16[128,512]{1,0:T(8,128)(2,1)S(1)} %get-tuple-element.51), channel_id=1, source_target_pairs={{0,32},{32,0},{64,96},{96,64},{1,33},{33,1},{65,97},{97,65},{2,34}... | collective-permute-start | bytes 393224 | tf_op jit(solution)/shard_map/ppermute | solution.py:493
  153.3 12.0 %all-to-all-start.4 = ((bf16[16,16,512]{2,1,0:T(8,128)(2,1)}), bf16[16,16,512]{2,1,0:T(8,128)(2,1)S(1)}, u32[]{:S(2)}, u32[]{:S(2)}) async-start(bf16[16,16,512]{2,1,0:T(8,128)(2,1)} %bitcast.17), calls=%async_computation.4 | async-start | bytes 524288 | tf_op jit(solution)/shard_map/all_to_all | solution.py:509
